TPU v7x, 32 devices: a whole 2x2x4 slice. The times are simulated.
32 devices in a mesh: dp: 4 (over y, x), tensor: 8 (over z, core).
Axes of the slice: x: 2, y: 2, z: 4, core: 2. Of those that a mesh axis runs over, the one named last changes fastest.
Arguments:
- tokens: bfloat16 [4096, 2048], P(('dp', 'tensor')), may hold values from -6 to 6
- norm_gain: bfloat16 [2048], replicated, may hold values from 0.099609375 to 1.8984375
- routes: int32 [4096, 6], P(('dp', 'tensor')), may hold values from 0 to 31, all different within a row; in each aligned block of 128 rows (0 to 127, 128 to 255, ...) at most 32 rows name the same one
- route_gates: bfloat16 [4096, 6], P(('dp', 'tensor')), may hold values from 0.19921875 to 1
- lengths: int32 [24], replicated, may hold values from 1 to 480, 4096 in all
- request_adapter: int32 [24], replicated, may hold values from 0 to 31
- adapter_slot: int32 [32], replicated, may hold values from 0 to 31, each once
- expert_gate: bfloat16 [32, 2048, 1408], P('tensor'), may hold values from -0.125 to 0.125
- expert_up: bfloat16 [32, 2048, 1408], P('tensor'), may hold values from -0.125 to 0.125
- expert_down: bfloat16 [32, 1408, 2048], P('tensor'), may hold values from -0.15625 to 0.15625
- shared_gate: bfloat16 [2048, 1408], P(None, 'dp'), may hold values from -0.125 to 0.125
- shared_up_weight: bfloat16 [2048, 1408], P(None, 'dp'), may hold values from -0.125 to 0.125
- shared_down: bfloat16 [1408, 2048], P('dp'), may hold values from -0.15625 to 0.15625
- adapter_down: bfloat16 [32, 2048, 16], P('dp'), may hold values from -0.125 to 0.125
- adapter_up: bfloat16 [32, 16, 2048], P('dp'), may hold values from -1.5 to 1.5
- head_weight: bfloat16 [2048, 65536], P(None, ('dp', 'tensor')), may hold values from -0.375 to 0.375
Outputs:
- sublayer_out: bfloat16 [4096, 2048], P(('dp', 'tensor'))
- last_norm: float32 [24], replicated
- block_logit: float32 [24, 8], P(None, 'tensor')
Inputs may be any that keep to these rules, and one draw needn't show every extreme that they name: `routes`: in each aligned block of 128 rows (the rows of one device), no expert is named by more than 32 rows, a bound that some block reaches. The lengths sum to 4096; the largest is exactly 480. Each position of the store appears once: adapter a is stored at position adapter_slot[a] of adapter_down and adapter_up.
All inputs are finite; a program needn't handle non-finite values.
Results may differ from a plain program's by a relative error of at most 0.0066.
Values may be sent and summed in bfloat16 or wider, within the bound.
No kernel may reach another device: no remote copies, remote signals or barrier semaphores. Data moves between devices by JAX's collectives and lax.ppermute only.
A program may use at most 192 MiB of HBM per device.

v0:
```python
import jax
import jax.numpy as jnp
from jax import lax
from jax.sharding import PartitionSpec as P

CAP = 32


def apply_norm(tokens, norm_gain):
    values = tokens.astype(jnp.float32)
    scaled = lax.rsqrt(jnp.mean(values * values, axis=-1, keepdims=True) + 1e-06)
    return (values * scaled * norm_gain.astype(jnp.float32)).astype(jnp.bfloat16)


def feed_forward(inputs, gate_mat, up_mat, down_mat):
    gate_portion = jnp.dot(inputs, gate_mat, preferred_element_type=jnp.float32)
    up_part = jnp.dot(inputs, up_mat, preferred_element_type=jnp.float32)
    hidden = (jax.nn.silu(gate_portion) * up_part).astype(jnp.bfloat16)
    return jnp.dot(hidden, down_mat, preferred_element_type=jnp.float32)


def token_slots(positions, lengths, request_adapter, adapter_slot):
    request_ends = jnp.cumsum(lengths)
    request = jnp.sum((request_ends[None, :] <= positions[:, None]).astype(jnp.int32), axis=1)
    request_pick = (
        request[:, None] == jnp.arange(request_adapter.shape[0], dtype=jnp.int32)[None, :]
    )
    adapter = jnp.sum(jnp.where(request_pick, request_adapter[None, :], 0), axis=1)
    adapter_pick = adapter[:, None] == jnp.arange(adapter_slot.shape[0], dtype=jnp.int32)[None, :]
    return jnp.sum(jnp.where(adapter_pick, adapter_slot[None, :], 0), axis=1)


def adapter_delta(inputs, slot_ids, down_store, up_store):
    held_count = down_store.shape[0]
    model_width = down_store.shape[1]
    rank_size = down_store.shape[2]
    flat_down = jnp.transpose(down_store, (1, 0, 2)).reshape(model_width, held_count * rank_size)
    low_rank = jnp.dot(inputs, flat_down, preferred_element_type=jnp.float32)
    low_rank = low_rank.reshape(inputs.shape[0], held_count, rank_size)
    keep_mask = slot_ids[:, None] == jnp.arange(held_count, dtype=jnp.int32)[None, :]
    low_rank = jnp.where(keep_mask[:, :, None], low_rank, 0.0).astype(jnp.bfloat16)
    low_rank = low_rank.reshape(inputs.shape[0], held_count * rank_size)
    flat_up = up_store.reshape(held_count * rank_size, up_store.shape[2])
    return jnp.dot(low_rank, flat_up, preferred_element_type=jnp.float32)


def local(
    tokens,
    norm_gain,
    routes,
    route_gates,
    lengths,
    request_adapter,
    adapter_slot,
    expert_gate,
    expert_up,
    expert_down,
    shared_gate,
    shared_up_weight,
    shared_down,
    adapter_down,
    adapter_up,
    head_weight,
):
    tok_rows = tokens.shape[0]
    model_width = tokens.shape[1]
    route_count = routes.shape[1]
    tensor_size = lax.axis_size("tensor")
    tensor_pos = lax.axis_index("tensor")
    data_pos = lax.axis_index("dp")
    local_experts = expert_gate.shape[0]
    all_experts = local_experts * tensor_size
    slot_range = jnp.arange(CAP, dtype=jnp.int32)
    normed = apply_norm(tokens, norm_gain)
    numbers = jnp.arange(all_experts, dtype=jnp.int32)
    route_hits = routes[:, :, None] == numbers[None, None, :]
    chosen = jnp.any(route_hits, axis=1)
    weight = jnp.sum(
        jnp.where(route_hits, route_gates[:, :, None], jnp.zeros((), jnp.bfloat16)), axis=1
    )
    slot_place = jnp.cumsum(chosen.astype(jnp.int32), axis=0) - 1
    pooled, pooled_routes = (
        lax.all_gather(normed, "tensor", axis=0, tiled=True),
        lax.all_gather(routes.astype(jnp.bfloat16), "tensor", axis=0, tiled=True),
    )
    pooled = pooled.reshape(tensor_size, tok_rows, model_width)
    source_routes = pooled_routes.astype(jnp.int32).reshape(tensor_size, tok_rows, route_count)
    own_numbers = tensor_pos * local_experts + jnp.arange(local_experts, dtype=jnp.int32)
    source_hits = source_routes[:, :, :, None] == own_numbers[None, None, None, :]
    source_chosen = jnp.any(source_hits, axis=2)
    source_place = jnp.cumsum(source_chosen.astype(jnp.int32), axis=1) - 1
    source_pick = source_chosen[:, :, :, None] & (
        source_place[:, :, :, None] == slot_range[None, None, None, :]
    )
    source_pick = jnp.where(source_pick, 1.0, 0.0).astype(jnp.bfloat16)
    incoming = jnp.einsum(
        "sijc,sid->sjcd", source_pick, pooled, preferred_element_type=jnp.float32
    ).astype(jnp.bfloat16)
    gate_portion = jnp.einsum(
        "secd,edf->secf", incoming, expert_gate, preferred_element_type=jnp.float32
    )
    up_part = jnp.einsum("secd,edf->secf", incoming, expert_up, preferred_element_type=jnp.float32)
    hidden = (jax.nn.silu(gate_portion) * up_part).astype(jnp.bfloat16)
    expert_out = jnp.einsum(
        "secf,efd->secd", hidden, expert_down, preferred_element_type=jnp.float32
    ).astype(jnp.bfloat16)
    returned_rows = lax.all_to_all(expert_out, "tensor", split_axis=0, concat_axis=0, tiled=True)
    returned_rows = returned_rows.reshape(all_experts, CAP, model_width)
    mixing_result = jnp.where(
        slot_place[:, :, None] == slot_range[None, None, :],
        weight[:, :, None],
        jnp.zeros((), jnp.bfloat16),
    )
    routed_output = jnp.einsum(
        "kbt,btw->kw", mixing_result, returned_rows, preferred_element_type=jnp.float32
    )
    own_base = (data_pos * tensor_size + tensor_pos) * tok_rows
    own_positions = own_base + jnp.arange(tok_rows, dtype=jnp.int32)
    peer_rows = lax.all_gather(normed, "dp", axis=0, tiled=True)
    shared_sum = lax.psum_scatter(
        feed_forward(peer_rows, shared_gate, shared_up_weight, shared_down),
        "dp",
        scatter_dimension=0,
        tiled=True,
    )
    own_slots = token_slots(own_positions, lengths, request_adapter, adapter_slot)
    store_down, store_up = (
        lax.all_gather(adapter_down, "dp", axis=0, tiled=True),
        lax.all_gather(adapter_up, "dp", axis=0, tiled=True),
    )
    summed = routed_output + shared_sum + adapter_delta(normed, own_slots, store_down, store_up)
    sublayer_out = summed.astype(jnp.bfloat16)
    request_ends = jnp.cumsum(lengths)
    last_pick = jnp.where(request_ends[:, None] - 1 == own_positions[None, :], 1.0, 0.0).astype(
        jnp.bfloat16
    )
    last_part = jnp.dot(last_pick, sublayer_out, preferred_element_type=jnp.float32)
    last_states = lax.psum(last_part, ("dp", "tensor"))
    last_norm = jnp.sqrt(jnp.sum(last_states * last_states, axis=1))
    logits = jnp.dot(
        last_states.astype(jnp.bfloat16), head_weight, preferred_element_type=jnp.float32
    )
    block_logit = lax.pmax(jnp.max(logits, axis=1), "dp")
    return (sublayer_out, last_norm, block_logit[:, None])


def solution(mesh):
    placed = (
        P(("dp", "tensor"), None),
        P(),
        P(("dp", "tensor"), None),
        P(("dp", "tensor"), None),
        P(),
        P(),
        P(),
        P("tensor", None, None),
        P("tensor", None, None),
        P("tensor", None, None),
        P(None, "dp"),
        P(None, "dp"),
        P("dp", None),
        P("dp", None, None),
        P("dp", None, None),
        P(None, ("dp", "tensor")),
    )
    return jax.shard_map(
        local,
        mesh=mesh,
        in_specs=placed,
        out_specs=(P(("dp", "tensor"), None), P(), P(None, "tensor")),
        check_vma=False,
    )
```

profile of v0, /device:TPU:0, one launch (start us, length us, event | category | flops | bytes accessed | tf_op | source)
XLA Modules:
  0.0 399.5 jit_solution(8841968495264773676)
XLA Ops:
  7.2 0.8 convert_element_type.67
  8.0 1.2 fusion.31
  9.3 2.0 fusion.33
  11.4 0.7 all-gather.5.cloned.1.call-update
  12.1 37.4 %all-gather.7.cloned.1.call-done = bf16[512,2048]{1,0:T(8,128)(2,1)} async-done(((bf16[128,2048]{1,0:T(8,128)(2,1)}), bf16[512,2048]{1,0:T(8,128)(2,1)}) %all-gather.7.cloned.1.call-update) | async-done | bytes 2097168 | tf_op jit(solution)/shard_map/all_gather | solution.py:119
  49.5 3.9 fusion.70
  53.4 5.7 %fusion.22 = f32[512,2048]{1,0:T(8,128)} fusion(bf16[352,2048]{1,0:T(8,128)(2,1)S(1)} %copy-done, bf16[512,2048]{1,0:T(8,128)(2,1)S(1)} %copy-done.9, bf16[2048,352]{0,1:T(8,128)(2,1)} %param.27, f32[512,352]{0,1:T(8,128)} %fusion.70), kind=kOutput, calls=%fused_computation.28 | convolution fusion | flops 1477476352 | bytes 9895936 | tf_op jit(solution)/shard_map/dot_general | solution.py:19
  59.1 0.7 copy-done.6
  59.8 13.5 %all_gather.15 = bf16[1024,6]{0,1:T(8,128)(2,1)S(1)} all-gather(bf16[128,6]{0,1:T(8,128)(2,1)S(1)} %convert_element_type.63), channel_id=1, replica_groups=mesh['dp'=4,'tensor'=8] {'tensor'}, dimensions={0}, use_global_device_ids=true | all-gather | bytes 13824 | tf_op jit(solution)/shard_map/all_gather | solution.py:84
  73.4 0.3 copy.64
  73.7 23.4 %broadcast_add_fusion = s32[8,128,4]{2,0,1:T(8,128)S(1)} fusion(s32[8,128,4]{2,0,1:T(8,128)S(1)} %copy.64), kind=kOutput, calls=%fused_computation.50 | output fusion | flops 524288 | bytes 32768 | tf_op jit(solution)/shard_map/jit(cumsum)/reduce_window_sum | solution.py:91
  97.1 0.2 copy.65
  97.3 1.6 all-gather.5.cloned.1.call-done
  98.9 3.4 convolution_convert_fusion
  102.4 14.3 %fusion.2 = f32[4,8,32,1408]{3,2,1,0:T(8,128)} fusion(bf16[4,2048,1408]{2,1,0:T(8,128)(2,1)} %param.24, bf16[8,4,32,2048]{3,2,1,0:T(8,128)(2,1)S(1)} %convolution_convert_fusion), kind=kOutput, calls=%fused_computation.2 | convolution fusion | flops 5905580032 | bytes 33030144 | tf_op jit(solution)/shard_map/secd,edf->secf/dot_general | solution.py:102
  116.7 17.1 %fusion.6 = bf16[8,4,32,1408]{3,2,0,1:T(8,128)(2,1)S(1)} fusion(f32[4,8,32,1408]{3,2,1,0:T(8,128)} %fusion.2, bf16[4,2048,1408]{2,1,0:T(8,128)(2,1)} %param.23, bf16[8,4,32,2048]{3,2,1,0:T(8,128)(2,1)S(1)} %convolution_convert_fusion), kind=kOutput, calls=%fused_computation.7 | convolution fusion | flops 5914230784 | bytes 35913728 | tf_op jit(solution)/shard_map/secd,edf->secf/dot_general | solution.py:99
  133.7 11.9 %convert_bitcast_fusion = bf16[8,4,32,2048]{3,2,0,1:T(8,128)(2,1)S(1)} fusion(bf16[8,4,32,1408]{3,2,0,1:T(8,128)(2,1)S(1)} %fusion.6, bf16[4,1408,2048]{2,1,0:T(8,128)(2,1)} %param.25), kind=kOutput, calls=%fused_computation.13 | convolution fusion | flops 5907677184 | bytes 30146560 | tf_op jit(solution)/shard_map/secf,efd->secd/dot_general | solution.py:104
  145.6 2.5 copy.68
  148.1 4.7 %all-to-all-start = ((bf16[8,4,32,2048]{3,2,1,0:T(8,128)(2,1)}), bf16[8,4,32,2048]{3,2,1,0:T(8,128)(2,1)}, u32[]{:S(2)}, u32[]{:S(2)}) async-start(bf16[8,4,32,2048]{3,2,1,0:T(8,128)(2,1)} %copy.68), calls=%async_computation | async-start | bytes 8388608 | tf_op jit(solution)/shard_map/all_to_all | solution.py:107
  152.8 0.3 all-gather.11.cloned.1.call-start
  153.1 1.1 copy.71
  154.2 0.5 all-gather.9.cloned.1.call-update
  154.9 0.2 reduce_window_sum.30
  155.8 91.0 %all-to-all-done = bf16[8,4,32,2048]{3,2,1,0:T(8,128)(2,1)} async-done(((bf16[8,4,32,2048]{3,2,1,0:T(8,128)(2,1)}), bf16[8,4,32,2048]{3,2,1,0:T(8,128)(2,1)}, u32[]{:S(2)}, u32[]{:S(2)}) %all-to-all-start) | async-done | bytes 4194336 | tf_op jit(solution)/shard_map/all_to_all | solution.py:107
  246.8 3.2 fusion.17
  250.1 4.3 %fusion.18 = bf16[128,2048]{1,0:T(8,128)(2,1)S(1)} fusion(f32[128,2048]{1,0:T(8,128)S(1)} %fusion.17, bf16[32,16,2048]{2,0,1:T(8,128)(2,1)} %all-gather.11.cloned.1.call-done, bf16[32,16,2048]{2,1,0:T(8,128)(2,1)} %bitcast.87, bf16[128,2048]{1,0:T(8,128)(2,1)S(1)} %copy-done.2, pred[128,32]{0,1:T(8,128)(4,1)S(1)} %iota_compare_fusion.3), kind=kOutput, calls=%fused_computation.21 | convolution fusion | flops 537526272 | bytes 6295552 | tf_op jit(solution)/shard_map/dot_general | solution.py:44
  254.4 0.9 fusion.58
  255.3 122.0 %all-reduce.2.cloned.1.call-done = f32[24,2048]{1,0:T(8,128)} async-done(((f32[24,2048]{1,0:T(8,128)}), f32[24,2048]{1,0:T(8,128)}) %all-reduce.2.cloned.1.call-update) | async-done | bytes 196624 | tf_op jit(solution)/shard_map/psum | solution.py:138
  377.3 4.8 %convolution_reduce_fusion = f32[24]{0:T(128)S(1)} fusion(bf16[2048,2048]{1,0:T(8,128)(2,1)} %param.31, f32[24,2048]{1,0:T(8,128)} %all-reduce.2.cloned.1.call-done), kind=kOutput, calls=%fused_computation.31 | convolution fusion | flops 201424864 | bytes 8585312 | tf_op jit(solution)/shard_map/dot_general | solution.py:140
  382.2 9.8 %pmax.7 = f32[24,1]{0,1:T(1,128)} all-reduce(f32[24,1]{0,1:T(1,128)S(1)} %bitcast.89), channel_id=1, replica_groups=mesh['dp'=4,'tensor'=8] {'dp'}, use_global_device_ids=true, to_apply=%region_14.15 | all-reduce | flops 24 | bytes 192 | tf_op jit(solution)/shard_map/pmax | solution.py:143
  392.0 0.1 multiply_reduce_fusion
  392.1 0.5 sqrt.3
  (58 shorter events, 1.3 us)
Async XLA Ops:
  7.2 46.3 %copy-start = (bf16[352,2048]{1,0:T(8,128)(2,1)S(1)}, bf16[352,2048]{1,0:T(8,128)(2,1)}, u32[]{:S(2)}) copy-start(bf16[352,2048]{1,0:T(8,128)(2,1)} %param.28) | copy-start | bytes 4325380
  7.2 42.3 %all-gather.7.cloned.1.call-start = ((), (), s32[]{:S(2)}) async-start(), calls=%async_computation.3 | async-start | bytes 2621440 | tf_op jit(solution)/shard_map/all_gather | solution.py:119
  11.3 87.6 %all-gather.5.cloned.1.call-start = ((), (), s32[]{:S(2)}) async-start(), calls=%async_computation.2 | async-start | bytes 4718592 | tf_op jit(solution)/shard_map/all_gather | solution.py:83
  12.1 143.7 %reduce-scatter.2.cloned.1.call-start = ((), (), s32[]{:S(2)}) async-start(), calls=%async_computation.4 | async-start | bytes 5242880 | tf_op jit(solution)/shard_map/reduce_scatter | solution.py:120
  49.5 4.0 copy-start.9
  59.1 0.7 copy-start.6
  148.0 5.0 %copy-start.5 = (bf16[8,16,2048]{2,1,0:T(8,128)(2,1)S(1)}, bf16[8,16,2048]{2,1,0:T(8,128)(2,1)}, u32[]{:S(2)}) copy-start(bf16[8,16,2048]{2,1,0:T(8,128)(2,1)} %param.30) | copy-start | bytes 1572868
  148.0 7.1 %copy-start.8 = (s32[24]{0:T(128)S(1)}, s32[24]{0:T(128)}, u32[]{:S(2)}) copy-start(s32[24]{0:T(128)} %param.20) | copy-start | bytes 292
  148.0 7.5 %copy-start.10 = (s32[24]{0:T(128)S(1)}, s32[24]{0:T(128)}, u32[]{:S(2)}) copy-start(s32[24]{0:T(128)} %param.21) | copy-start | bytes 292
  148.0 7.6 %copy-start.11 = (s32[32]{0:T(128)S(1)}, s32[32]{0:T(128)}, u32[]{:S(2)}) copy-start(s32[32]{0:T(128)} %param.22) | copy-start | bytes 388
  148.0 7.7 %copy-start.7 = (bf16[128,6]{0,1:T(8,128)(2,1)S(1)}, bf16[128,6]{0,1:T(8,128)(2,1)}, u32[]{:S(2)}) copy-start(bf16[128,6]{0,1:T(8,128)(2,1)} %param.19) | copy-start | bytes 4612
  148.1 98.7 %all-to-all-start = ((bf16[8,4,32,2048]{3,2,1,0:T(8,128)(2,1)}), bf16[8,4,32,2048]{3,2,1,0:T(8,128)(2,1)}, u32[]{:S(2)}, u32[]{:S(2)}) async-start(bf16[8,4,32,2048]{3,2,1,0:T(8,128)(2,1)} %copy.68), calls=%async_computation | async-start | bytes 8388608 | tf_op jit(solution)/shard_map/all_to_all | solution.py:107
  152.8 97.3 %all-gather.11.cloned.1.call-start = ((), (), s32[]{:S(2)}) async-start(), calls=%async_computation.6 | async-start | bytes 2621440 | tf_op jit(solution)/shard_map/all_gather | solution.py:129
  154.1 95.9 %copy-start.2 = (bf16[128,2048]{1,0:T(8,128)(2,1)S(1)}, bf16[128,2048]{1,0:T(8,128)(2,1)}, u32[]{:S(2)}) copy-start(bf16[128,2048]{1,0:T(8,128)(2,1)} %fusion.33) | copy-start | bytes 1572868
  154.2 95.9 %all-gather.9.cloned.1.call-start = ((), (), s32[]{:S(2)}) async-start(), calls=%async_computation.5 | async-start | bytes 2621440 | tf_op jit(solution)/shard_map/all_gather | solution.py:128
  154.8 222.6 %all-reduce.2.cloned.1.call-start = ((), (), s32[]{:S(2)}) async-start(), calls=%async_computation.7 | async-start | bytes 393216 | tf_op jit(solution)/shard_map/psum | solution.py:138
  254.4 127.8 %copy-start.3 = (bf16[128,2048]{1,0:T(8,128)(2,1)}, bf16[128,2048]{1,0:T(8,128)(2,1)S(1)}, u32[]{:S(2)}) copy-start(bf16[128,2048]{1,0:T(8,128)(2,1)S(1)} %fusion.18) | copy-start | bytes 1572868
  255.3 137.3 %copy-start.1 = (bf16[352,2048]{1,0:T(8,128)(2,1)S(1)}, bf16[352,2048]{1,0:T(8,128)(2,1)}, u32[]{:S(2)}) copy-start(bf16[352,2048]{1,0:T(8,128)(2,1)} %param.28) | copy-start | bytes 4325380
  377.3 14.6 %copy-start.4 = (f32[24,2048]{1,0:T(8,128)S(1)}, f32[24,2048]{1,0:T(8,128)}, u32[]{:S(2)}) copy-start(f32[24,2048]{1,0:T(8,128)} %all-reduce.2.cloned.1.call-done) | copy-start | bytes 589828
Sparse Core Ops, SparseCore 0:
  11.4 38.0 all-gather.6
  51.6 47.2 all-gather.4
  101.9 51.4 reduce-scatter.1
  155.3 36.5 all-gather.10
  193.8 35.2 all-gather.8
  255.4 121.8 all-reduce.1
where the time goes:
time: 400 us; the launch traced here: 399 us
  waiting for transfers between devices  253 us (63%)
  matrix products  69.5 us (17%)
  other arithmetic  28.3 us (7%)
  blocking collectives  23.3 us (6%)
  between operations  14.4 us (4%)
  local copies, waits for them, and re-layouts  5.5 us (1%)
  starting transfers between devices  5.19 us (1%)
    psum x1, waiting for transfers between devices, local(): last_states = lax.psum(last_part, ('dp', 'tensor'))  122 us
    all_to_all x1, waiting for transfers between devices, local(): lax.all_to_all(expert_out, 'tensor', split_axis=0, concat_axis=0, tiled=T...  91 us
    all_gather x1, waiting for transfers between devices, local(): peer_rows = lax.all_gather(normed, 'dp', axis=0, tiled=True)  37.4 us
    another operation x1, other arithmetic, local(): source_place = jnp.cumsum(source_chosen.astype(jnp.int32), axis=1) - 1  23.4 us
    dot_general x1, matrix products, local(): jnp.einsum('secd,edf->secf', incoming, expert_gate, preferred_element_typ...  17.1 us
    dot_general x1, matrix products, local(): jnp.einsum('secd,edf->secf', incoming, expert_up, preferred_element_type=...  14.3 us
    all_gather x1, blocking collectives, local(): lax.all_gather(routes.astype(jnp.bfloat16), 'tensor', axis=0, tiled=True)  13.5 us
    dot_general x1, matrix products, local(): jnp.einsum('secf,efd->secd', hidden, expert_down, preferred_element_type=...  11.9 us
  transfers between devices with their start and end apart: 7, of which 4 were waited for; matrix products, arithmetic and copies ran while one was open for 22% of the time, Pallas kernels for 0%

commit v1 on v0

--- a/solution.py
+++ b/solution.py
@@ -1,6 +1,10 @@
+import functools
+
 import jax
 import jax.numpy as jnp
 from jax import lax
+from jax.experimental import pallas as pl
+from jax.experimental.pallas import tpu as pltpu
 from jax.sharding import PartitionSpec as P
 
 CAP = 32
@@ -144,6 +148,371 @@
     return (sublayer_out, last_norm, block_logit[:, None])
 
 
+def prep_kernel(tok_ref, gain_ref, routes_ref, gates_ref, first_ref, second_ref, whole_ref):
+    rows = tok_ref.shape[0]
+    half = second_ref.shape[1]
+    experts = 32
+    values = tok_ref[...].astype(jnp.float32)
+    scaled = lax.rsqrt(jnp.mean(values * values, axis=-1, keepdims=True) + 1e-06)
+    normed = (values * scaled * gain_ref[...].astype(jnp.float32)).astype(jnp.bfloat16)
+    whole_ref[...] = normed
+    first_ref[:, :half] = normed[:, :half]
+    second_ref[...] = normed[:, half:]
+    numbers = lax.broadcasted_iota(jnp.int32, (rows, experts), 1)
+    chosen = jnp.zeros((rows, experts), jnp.float32)
+    weight = jnp.zeros((rows, experts), jnp.float32)
+    for k in range(routes_ref.shape[1]):
+        hit = routes_ref[:, k : k + 1] == numbers
+        chosen = jnp.where(hit, 1.0, chosen)
+        weight = jnp.where(hit, gates_ref[:, k : k + 1].astype(jnp.float32), weight)
+    row = lax.broadcasted_iota(jnp.int32, (rows, rows), 0)
+    column = lax.broadcasted_iota(jnp.int32, (rows, rows), 1)
+    upto = jnp.where(row <= column, 1.0, 0.0).astype(jnp.bfloat16)
+    same = jnp.where(row == column, 1.0, 0.0).astype(jnp.bfloat16)
+    turn = (((0,), (0,)), ((), ()))
+    chosen = chosen.astype(jnp.bfloat16)
+    count = lax.dot_general(chosen, upto, turn, preferred_element_type=jnp.float32)
+    taken = lax.dot_general(chosen, same, turn, preferred_element_type=jnp.float32)
+    weight = lax.dot_general(
+        weight.astype(jnp.bfloat16), same, turn, preferred_element_type=jnp.float32
+    )
+    place = jnp.where(taken > 0.5, count - 1.0, -1.0)
+    first_ref[:experts, half:] = place.astype(jnp.bfloat16)
+    first_ref[experts : 2 * experts, half:] = weight.astype(jnp.bfloat16)
+    first_ref[2 * experts :, half:] = jnp.zeros((rows - 2 * experts, rows), jnp.bfloat16)
+
+
+def prepare(tokens, norm_gain, routes, route_gates):
+    rows, width = tokens.shape
+    half = width // 2
+    return pl.pallas_call(
+        prep_kernel,
+        out_shape=(
+            jax.ShapeDtypeStruct((rows, half + rows), jnp.bfloat16),
+            jax.ShapeDtypeStruct((rows, half), jnp.bfloat16),
+            jax.ShapeDtypeStruct((rows, width), jnp.bfloat16),
+        ),
+        name="prepare",
+    )(tokens, norm_gain.reshape(1, width), routes, route_gates)
+
+
+def fill_incoming(blocks, places_ref, incoming, width):
+    count = (len(blocks) + 1) // 2
+    experts = places_ref.shape[1]
+    slots = lax.broadcasted_iota(jnp.int32, (CAP, 128), 0)
+    for d in range(count):
+        for c in range(2):
+            picks = [
+                jnp.where(places_ref[2 * d + c, e : e + 1, :] == slots, 1.0, 0.0)
+                for e in range(experts)
+            ]
+            pick = jnp.concatenate(picks, axis=0).astype(jnp.bfloat16)
+            part = pl.ds(c * 128, 128)
+            rows = blocks[d][part, :width]
+            if d > 0:
+                rows = rows + blocks[2 * count - 1 - d][part, :width]
+            chosen = jnp.dot(pick, rows, preferred_element_type=jnp.float32).astype(jnp.bfloat16)
+            for e in range(experts):
+                at = pl.ds((2 * d + c) * CAP, CAP)
+                incoming[e, at, :] = chosen[e * CAP : (e + 1) * CAP]
+
+
+def first_kernel(places_ref, *refs):
+    blocks, (gate_ref, up_ref, gate_out, up_out, incoming) = refs[:-5], refs[-5:]
+    e = pl.program_id(0)
+
+    @pl.when(e == 0)
+    def _():
+        fill_incoming(blocks, places_ref, incoming, incoming.shape[2])
+
+    rows = incoming[e]
+    gate_out[0] = jnp.dot(rows, gate_ref[0], preferred_element_type=jnp.float32)
+    up_out[0] = jnp.dot(rows, up_ref[0], preferred_element_type=jnp.float32)
+
+
+def first_half(places, blocks, gate, up):
+    sources, experts, _ = places.shape
+    half = gate.shape[1] // 2
+    hidden = gate.shape[2]
+    weight_spec = pl.BlockSpec((1, half, hidden), lambda e: (e, 0, 0))
+    out_spec = pl.BlockSpec((1, sources * CAP, hidden), lambda e: (e, 0, 0))
+    out_shape = jax.ShapeDtypeStruct((experts, sources * CAP, hidden), jnp.float32)
+    whole = lambda a: pl.BlockSpec(a.shape, lambda e: (0,) * a.ndim)
+    return pl.pallas_call(
+        first_kernel,
+        grid=(experts,),
+        in_specs=[whole(places)] + [whole(b) for b in blocks] + [weight_spec, weight_spec],
+        out_specs=(out_spec, out_spec),
+        out_shape=(out_shape, out_shape),
+        scratch_shapes=[pltpu.VMEM((experts, sources * CAP, half), jnp.bfloat16)],
+        compiler_params=pltpu.CompilerParams(vmem_limit_bytes=48 << 20),
+        cost_estimate=pl.CostEstimate(
+            flops=4 * experts * sources * CAP * half * hidden,
+            bytes_accessed=4 * experts * half * hidden + 8 * experts * sources * CAP * hidden,
+            transcendentals=0,
+        ),
+        name="first_half",
+    )(places, *blocks, gate, up)
+
+
+def second_kernel(experts, places_ref, weights_ref, *refs):
+    blocks, rest = refs[:-11], refs[-11:]
+    gate_ref, up_ref, gate_acc, up_acc, down_ref, left_ref, right_ref = rest[:7]
+    incoming, hidden, outs, mix = rest[7:]
+    sources = places_ref.shape[0]
+    i = pl.program_id(0)
+
+    @pl.when(i == 0)
+    def _():
+        fill_incoming(blocks, places_ref, incoming, incoming.shape[2])
+        slots = lax.broadcasted_iota(jnp.int32, (CAP, 128), 0)
+        for s in range(sources):
+            for e in range(experts):
+                mix[s, e * CAP : (e + 1) * CAP, :] = jnp.where(
+                    places_ref[s, e : e + 1, :] == slots, weights_ref[s, e : e + 1, :], 0.0
+                ).astype(jnp.bfloat16)
+
+    @pl.when(i < experts)
+    def _():
+        rows = incoming[i]
+        gate = gate_acc[0] + jnp.dot(rows, gate_ref[0], preferred_element_type=jnp.float32)
+        up = up_acc[0] + jnp.dot(rows, up_ref[0], preferred_element_type=jnp.float32)
+        hidden[i] = (gate / (1.0 + jnp.exp(-gate)) * up).astype(jnp.bfloat16)
+
+    @pl.when(i >= experts)
+    def _():
+        step = i - experts
+        e = lax.rem(step, experts)
+        n = lax.div(step, experts)
+        out = jnp.dot(hidden[e], down_ref[0], preferred_element_type=jnp.float32)
+        out = out.astype(jnp.bfloat16)
+        at = pl.ds(pl.multiple_of(e * CAP, CAP), CAP)
+        for s in range(sources):
+            outs[s, at, :] = out[s * CAP : (s + 1) * CAP]
+
+        def combine(to_ref):
+            for s in range(sources):
+                to_ref[s] = lax.dot_general(
+                    mix[s], outs[s], (((0,), (0,)), ((), ())), preferred_element_type=jnp.float32
+                ).astype(jnp.bfloat16)
+
+        pl.when((e == experts - 1) & (n < 2))(lambda: combine(left_ref))
+        pl.when((e == experts - 1) & (n >= 2))(lambda: combine(right_ref))
+
+
+def second_half(places, weights, blocks, gate, up, gate_acc, up_acc, down):
+    sources, experts, rows = places.shape
+    half = gate.shape[1] // 2
+    width = gate.shape[1]
+    hidden = gate.shape[2]
+    tile = half // 2
+    slots = sources * CAP
+    now = lambda i: jnp.minimum(i, experts - 1)
+    later = lambda i: jnp.maximum(i - experts, 0)
+    weight_spec = pl.BlockSpec((1, half, hidden), lambda i: (now(i), 1, 0))
+    acc_spec = pl.BlockSpec((1, slots, hidden), lambda i: (now(i), 0, 0))
+    down_spec = pl.BlockSpec(
+        (1, hidden, tile), lambda i: (lax.rem(later(i), experts), 0, lax.div(later(i), experts))
+    )
+    left_spec = pl.BlockSpec(
+        (sources, rows, tile), lambda i: (0, 0, jnp.minimum(lax.div(later(i), experts), 1))
+    )
+    right_spec = pl.BlockSpec(
+        (sources, rows, tile), lambda i: (0, 0, jnp.maximum(lax.div(later(i), experts) - 2, 0))
+    )
+    out_shape = jax.ShapeDtypeStruct((sources, rows, half), jnp.bfloat16)
+    whole = lambda a: pl.BlockSpec(a.shape, lambda i: (0,) * a.ndim)
+    return pl.pallas_call(
+        functools.partial(second_kernel, experts),
+        grid=(experts + (width // tile) * experts,),
+        in_specs=[whole(places), whole(weights)]
+        + [whole(b) for b in blocks]
+        + [weight_spec, weight_spec, acc_spec, acc_spec, down_spec],
+        out_specs=(left_spec, right_spec),
+        out_shape=(out_shape, out_shape),
+        scratch_shapes=[
+            pltpu.VMEM((experts, slots, half), jnp.bfloat16),
+            pltpu.VMEM((experts, slots, hidden), jnp.bfloat16),
+            pltpu.VMEM((sources, experts * CAP, tile), jnp.bfloat16),
+            pltpu.VMEM((sources, experts * CAP, rows), jnp.bfloat16),
+        ],
+        compiler_params=pltpu.CompilerParams(vmem_limit_bytes=52 << 20),
+        cost_estimate=pl.CostEstimate(
+            flops=8 * experts * slots * half * hidden,
+            bytes_accessed=8 * experts * half * hidden + 8 * experts * slots * hidden,
+            transcendentals=experts * slots * hidden,
+        ),
+        name="second_half",
+    )(places, weights, *blocks, gate, up, gate_acc, up_acc, down)
+
+
+def add(*terms):
+    total = terms[0].astype(jnp.float32)
+    for term in terms[1:]:
+        total = total + term.astype(jnp.float32)
+    return total.astype(jnp.bfloat16)
+
+
+def swap_cores(value, tensor_size):
+    return lax.ppermute(value, "tensor", [(i, i ^ 1) for i in range(tensor_size)])
+
+
+def spread_pairs(chips, k):
+    upward = [(2 * z, 2 * z + 2) for z in range(k - 1, chips - 1)]
+    return upward + [(2 * z + 1, 2 * z - 1) for z in range(1, chips - k + 1)]
+
+
+def collect_pairs(chips, k):
+    upward = [(2 * z, 2 * z + 2) for z in range(0, k)]
+    return upward + [(2 * z + 1, 2 * z - 1) for z in range(chips - k, chips)]
+
+
+def spread(chunks, core, tensor_size):
+    chips = tensor_size // 2
+    last, mine, other = [], [], []
+    for chunk in chunks:
+        twin = swap_cores(chunk, tensor_size)
+        pair = jnp.where(
+            core == 0, jnp.concatenate([chunk, twin]), jnp.concatenate([twin, chunk])
+        )
+        last.append(pair)
+        mine.append([pair])
+        other.append([])
+    for k in range(1, chips):
+        for j in range(len(chunks)):
+            last[j] = lax.ppermute(last[j], "tensor", spread_pairs(chips, k))
+            mine[j].append(last[j])
+            other[j].append(swap_cores(last[j], tensor_size))
+    return [m + o for m, o in zip(mine, other)]
+
+
+def collect(parts, core, tensor_size):
+    chips = tensor_size // 2
+    run = [None] * len(parts)
+    for k in range(1, chips):
+        for j, part in enumerate(parts):
+            got = swap_cores(part[chips - k], tensor_size)
+            terms = (part[k], got) if run[j] is None else (part[k], got, run[j])
+            run[j] = lax.ppermute(add(*terms), "tensor", collect_pairs(chips, k))
+    done = []
+    for j, part in enumerate(parts):
+        total = add(part[0], run[j])
+        rows = total.shape[0] // 2
+        low, high = total[:rows], total[rows:]
+        got = swap_cores(jnp.where(core == 0, high, low), tensor_size)
+        done.append(jnp.where(core == 0, low, high).astype(jnp.float32) + got.astype(jnp.float32))
+    return done
+
+
+def across(value, combine, axis, size):
+    step = 1
+    while step < size:
+        pairs = [(i, i ^ step) for i in range(size)]
+        value = combine(value, lax.ppermute(value, axis, pairs))
+        step *= 2
+    return value
+
+
+def local_line(
+    tokens,
+    norm_gain,
+    routes,
+    route_gates,
+    lengths,
+    request_adapter,
+    adapter_slot,
+    expert_gate,
+    expert_up,
+    expert_down,
+    shared_gate,
+    shared_up_weight,
+    shared_down,
+    adapter_down,
+    adapter_up,
+    head_weight,
+):
+    tok_rows, width = tokens.shape
+    half = width // 2
+    tensor_size = lax.axis_size("tensor")
+    data_size = lax.axis_size("dp")
+    tensor_pos = lax.axis_index("tensor")
+    data_pos = lax.axis_index("dp")
+    chips = tensor_size // 2
+    chip, core = tensor_pos // 2, tensor_pos % 2
+    experts = expert_gate.shape[0]
+    all_experts = experts * tensor_size
+    first, second, normed = prepare(tokens, norm_gain, routes, route_gates)
+    blocks_a, blocks_b = spread([first, second], core, tensor_size)
+    own_first = tensor_pos * experts
+
+    def held(begin):
+        rows = []
+        for d in range(chips):
+            for c in range(2):
+                take = lambda b: lax.dynamic_slice(
+                    b[:, half:], (c * tok_rows + begin + own_first, 0), (experts, tok_rows)
+                )
+                row = take(blocks_a[d])
+                if d > 0:
+                    row = row + take(blocks_a[2 * chips - 1 - d])
+                rows.append(row)
+        return jnp.stack(rows)
+
+    places = held(0).astype(jnp.int32)
+    weights = held(all_experts).astype(jnp.float32)
+    gate_acc, up_acc = first_half(places, blocks_a, expert_gate, expert_up)
+    left, right = second_half(
+        places, weights, blocks_b, expert_gate, expert_up, gate_acc, up_acc, expert_down
+    )
+    peer_rows = lax.all_gather(normed, "dp", axis=0, tiled=True)
+    block_rows = jnp.arange(tok_rows, dtype=jnp.int32)
+    bases = (jnp.arange(data_size, dtype=jnp.int32) * tensor_size + tensor_pos) * tok_rows
+    peer_positions = (bases[:, None] + block_rows[None, :]).reshape(-1)
+    peer_slots = token_slots(peer_positions, lengths, request_adapter, adapter_slot)
+    held_slots = peer_slots - data_pos * adapter_down.shape[0]
+    peer_part = feed_forward(peer_rows, shared_gate, shared_up_weight, shared_down)
+    peer_part = peer_part + adapter_delta(peer_rows, held_slots, adapter_down, adapter_up)
+    peer_part = peer_part.astype(jnp.bfloat16)
+    shared_sum = lax.psum_scatter(peer_part, "dp", scatter_dimension=0, tiled=True)
+    ends = jnp.cumsum(lengths) - 1
+    owner, row = ends // tok_rows, ends % tok_rows
+    owner_dp, owner_tensor = owner // tensor_size, owner % tensor_size
+    away = jnp.where(core == 0, chip - owner_tensor // 2, owner_tensor // 2 - chip) % chips
+    line_row = jnp.where(
+        owner_dp == data_pos, (away * 2 + owner_tensor % 2) * tok_rows + row, -1
+    )
+    peer_row = jnp.where(owner_tensor == tensor_pos, owner_dp * tok_rows + row, -1)
+
+    def pick(at, count):
+        return jnp.where(
+            at[:, None] == jnp.arange(count, dtype=jnp.int32)[None, :], 1.0, 0.0
+        ).astype(jnp.bfloat16)
+
+    line_pick = pick(line_row, 2 * chips * tok_rows)
+    last_part = jnp.concatenate(
+        [
+            jnp.dot(line_pick, p.reshape(-1, half), preferred_element_type=jnp.float32)
+            for p in (left, right)
+        ],
+        axis=1,
+    )
+    last_part = last_part + jnp.dot(
+        pick(peer_row, data_size * tok_rows), peer_part, preferred_element_type=jnp.float32
+    )
+    last = across(last_part, jnp.add, "tensor", tensor_size)
+    last = across(last, jnp.add, "dp", data_size).astype(jnp.bfloat16)
+    last_values = last.astype(jnp.float32)
+    last_norm = jnp.sqrt(jnp.sum(last_values * last_values, axis=1))
+    logits = jnp.dot(last, head_weight, preferred_element_type=jnp.float32)
+    block_logit = across(jnp.max(logits, axis=1, keepdims=True), jnp.maximum, "dp", data_size)
+    parts = [
+        [p.reshape(chips, 2 * tok_rows, half)[d] for d in range(chips)] for p in (left, right)
+    ]
+    routed = collect(parts, core, tensor_size)
+    out = jnp.concatenate(routed, axis=1) + shared_sum.astype(jnp.float32)
+    return (out.astype(jnp.bfloat16), last_norm, block_logit)
+
+
 def solution(mesh):
     placed = (
         P(("dp", "tensor"), None),
@@ -163,8 +532,9 @@
         P("dp", None, None),
         P(None, ("dp", "tensor")),
     )
+    short = mesh.shape["tensor"] == 8 and mesh.shape["dp"] == 4
     return jax.shard_map(
-        local,
+        local_line if short else local,
         mesh=mesh,
         in_specs=placed,
         out_specs=(P(("dp", "tensor"), None), P(), P(None, "tensor")),

time: 400 us -> 233 us (0.58)
  waiting for transfers between devices: 253 us -> 39.2 us
  starting transfers between devices: 5.19 us -> 72.7 us
  Pallas kernels: 0 us -> 54.5 us
  matrix products: 69.5 us -> 20.4 us
  blocking collectives: 23.3 us -> 0 us
  other arithmetic: 28.3 us -> 13.6 us
  local copies, waits for them, and re-layouts: 5.5 us -> 16.2 us
    psum x1 -> x0, waiting for transfers between devices: 122 us -> none  [local(): last_states = lax.psum(last_part, ('dp', 'tensor'))]
    all_to_all x1 -> x0, waiting for transfers between devices: 91 us -> none  [local(): lax.all_to_all(expert_out, 'tensor', split_axis=0, concat_axis=0, tiled=T...]
    ppermute x0 -> x35, starting transfers between devices: none -> 72.6 us  [the longest x6 22.8 us: collect(): run[j] = lax.ppermute(add(*terms), 'tensor', collect_pairs(chips, k))]
    pallas_call x0 -> x3, Pallas kernels: none -> 54.5 us  [the longest x1 36.7 us: second_half(): pl.pallas_call(functools.partial(second_kernel, experts), grid=(experts +...]
    dot_general x7 -> x4, matrix products: 55.6 us -> 4.97 us  [the longest x2 2.14 us: local_line(): jnp.dot(line_pick, p.reshape(-1, half), preferred_element_type=jnp.float32)]
    ppermute x0 -> x35, waiting for transfers between devices: none -> 39.2 us  [the longest x7 21.3 us: across(): value = combine(value, lax.ppermute(value, axis, pairs))]
    all_gather x4 -> x1, waiting for transfers between devices: 39 us -> 0.01 us  [local_line(): peer_rows = lax.all_gather(normed, 'dp', axis=0, tiled=True)]
    another operation x4 -> x3, other arithmetic: 23.7 us -> 0.19 us  [the longest x1 23.4 us: local(): source_place = jnp.cumsum(source_chosen.astype(jnp.int32), axis=1) - 1]
  transfers between devices with their start and end apart: 7 -> 37, of which waited for: 4 -> 10; matrix products, arithmetic and copies ran while one was open for 22% -> 17% of each run, Pallas kernels for 0% -> 23%
where the time goes in v1:
time: 233 us; the launch traced here: 231 us
  starting transfers between devices  72.7 us (31%)
  Pallas kernels  54.5 us (23%)
  waiting for transfers between devices  39.2 us (17%)
  matrix products  20.4 us (9%)
  local copies, waits for them, and re-layouts  16.2 us (7%)
  between operations  14.7 us (6%)
  other arithmetic  13.6 us (6%)
    pallas_call x1, Pallas kernels, second_half(): pl.pallas_call(functools.partial(second_kernel, experts), grid=(experts +...  36.7 us
    ppermute x6, starting transfers between devices, collect(): run[j] = lax.ppermute(add(*terms), 'tensor', collect_pairs(chips, k))  22.8 us
    ppermute x16, starting transfers between devices, swap_cores(): lax.ppermute(value, 'tensor', [(i, i ^ 1) for i in range(tensor_size)])  22.3 us
    ppermute x7, waiting for transfers between devices, across(): value = combine(value, lax.ppermute(value, axis, pairs))  21.3 us
    ppermute x6, starting transfers between devices, spread(): last[j] = lax.ppermute(last[j], 'tensor', spread_pairs(chips, k))  18.8 us
    pallas_call x1, Pallas kernels, first_half(): pl.pallas_call(first_kernel, grid=(experts,), in_specs=[whole(places)] +...  15.5 us
    ppermute x6, waiting for transfers between devices, spread(): last[j] = lax.ppermute(last[j], 'tensor', spread_pairs(chips, k))  11.4 us
    ppermute x7, starting transfers between devices, across(): value = combine(value, lax.ppermute(value, axis, pairs))  8.72 us
  transfers between devices with their start and end apart: 37, of which 10 were waited for; matrix products, arithmetic and copies ran while one was open for 17% of the time, Pallas kernels for 23%

profile of v1, /device:TPU:0, one launch (start us, length us, event | category | flops | bytes accessed | tf_op | source)
XLA Modules:
  0.0 231.3 jit_solution(17502339222966556691)
XLA Ops:
  11.5 2.3 %prepare.1 = (bf16[128,1152]{1,0:T(8,128)(2,1)}, bf16[128,1024]{1,0:T(8,128)(2,1)}, bf16[128,2048]{1,0:T(8,128)(2,1)}) custom-call(bf16[128,2048]{1,0:T(8,128)(2,1)} %tok_ref.1, bf16[1,2048]{1,0:T(2,128)(2,1)} %reshape.221.gain_ref, s32[128,6]{1,0:T(8,128)} %copy.25.routes_ref, bf16[128,6]{1,0:T(8,128)(2,1)} %copy.26.gates_ref), custom_call_target="tpu_custom_call" | custom-call | tf_op jit(solution)/shard_map/prepare/pallas_call | solution.py:188
  16.9 4.9 %collective-permute-start.1 = (bf16[256,1152]{1,0:T(8,128)(2,1)S(1)}, bf16[256,1152]{1,0:T(8,128)(2,1)S(1)}, u32[]{:S(2)}, u32[]{:S(2)}) collective-permute-start(bf16[256,1152]{1,0:T(8,128)(2,1)S(1)} %maximum_select_fusion.refs_0_), channel_id=1, source_target_pairs={{0,2},{2,4},{4,6},{3,1},{5,3},{7,5},{8,10},{10,12},{12,14},{11,9},... | collective-permute-start | bytes 1769480 | tf_op jit(solution)/shard_map/ppermute | solution.py:383
  21.8 7.3 %collective-permute-done.1.refs_1_ = bf16[256,1152]{1,0:T(8,128)(2,1)S(1)} collective-permute-done((bf16[256,1152]{1,0:T(8,128)(2,1)S(1)}, bf16[256,1152]{1,0:T(8,128)(2,1)S(1)}, u32[]{:S(2)}, u32[]{:S(2)}) %collective-permute-start.1) | collective-permute-done | bytes 589856 | tf_op jit(solution)/shard_map/ppermute | solution.py:383
  32.1 8.0 %collective-permute-start.8 = (bf16[256,1024]{1,0:T(8,128)(2,1)S(1)}, bf16[256,1024]{1,0:T(8,128)(2,1)}, u32[]{:S(2)}, u32[]{:S(2)}) collective-permute-start(bf16[256,1024]{1,0:T(8,128)(2,1)S(1)} %maximum_select_fusion.1.refs_0_), channel_id=1, source_target_pairs={{0,2},{2,4},{4,6},{3,1},{5,3},{7,5},{8,10},{10,12},{12,14},{11,9},... | collective-permute-start | bytes 1572872 | tf_op jit(solution)/shard_map/ppermute | solution.py:383
  41.9 4.1 %collective-permute-done.8.refs_1_ = bf16[256,1024]{1,0:T(8,128)(2,1)} collective-permute-done((bf16[256,1024]{1,0:T(8,128)(2,1)S(1)}, bf16[256,1024]{1,0:T(8,128)(2,1)}, u32[]{:S(2)}, u32[]{:S(2)}) %collective-permute-start.8) | collective-permute-done | bytes 524320 | tf_op jit(solution)/shard_map/ppermute | solution.py:383
  49.2 9.6 %collective-permute-start.5 = (bf16[256,1152]{1,0:T(8,128)(2,1)}, bf16[256,1152]{1,0:T(8,128)(2,1)}, u32[]{:S(2)}, u32[]{:S(2)}) collective-permute-start(bf16[256,1152]{1,0:T(8,128)(2,1)} %collective-permute-done.2.refs_2_), channel_id=1, source_target_pairs={{0,1},{1,0},{2,3},{3,2},{4,5},{5,4},{6,7},{7,6},{8,9},{9,8},{10,11... | collective-permute-start | bytes 1769480 | tf_op jit(solution)/shard_map/ppermute | solution.py:357
  61.2 6.7 %collective-permute-start.13 = (bf16[256,1024]{1,0:T(8,128)(2,1)}, bf16[256,1024]{1,0:T(8,128)(2,1)S(1)}, u32[]{:S(2)}, u32[]{:S(2)}) collective-permute-start(bf16[256,1024]{1,0:T(8,128)(2,1)} %collective-permute-done.10.refs_3_), channel_id=1, source_target_pairs={{0,1},{1,0},{2,3},{3,2},{4,5},{5,4},{6,7},{7,6},{8,9},{9,8},{10,11... | collective-permute-start | bytes 1572872 | tf_op jit(solution)/shard_map/ppermute | solution.py:357
  70.7 15.5 %first_half.1 = (f32[4,256,1408]{2,1,0:T(8,128)}, f32[4,256,1408]{2,1,0:T(8,128)}) custom-call(s32[8,4,128]{2,1,0:T(4,128)S(1)} %convert_element_type.138.places_ref, bf16[256,1152]{1,0:T(8,128)(2,1)S(1)} %maximum_select_fusion.refs_0_, bf16[256,1152]{1,0:T(8,128)(2,1)S(1)} %collective-permute-done.1.refs_1_, ...), custom_call_target="tpu_custom_call" | custom-call | flops 5905580032 | bytes 34603008 | tf_op jit(solution)/shard_map/first_half/pallas_call | solution.py:241
  87.4 36.7 %second_half.1 = (bf16[8,128,1024]{2,1,0:T(8,128)(2,1)}, bf16[8,128,1024]{2,1,0:T(8,128)(2,1)}) custom-call(s32[8,4,128]{2,1,0:T(4,128)S(1)} %convert_element_type.138.places_ref, f32[8,4,128]{2,1,0:T(4,128)S(1)} %convert_element_type.139.weights_ref, bf16[256,1024]{1,0:T(8,128)(2,1)S(1)} %maximum_select_fusion.1.refs_0_, ...), custom_call_target="tpu_custom_call" | custom-call | flops 11811160064 | bytes 57671680 | tf_op jit(solution)/shard_map/second_half/pallas_call | solution.py:325
  124.0 4.4 %fusion.71 = (bf16[2,128,1024]{2,1,0:T(8,128)(2,1)}, bf16[2,128,1024]{2,1,0:T(8,128)(2,1)}, bf16[2,128,1024]{2,1,0:T(8,128)(2,1)}, bf16[2,128,1024]{2,1,0:T(8,12...) fusion(bf16[8,128,1024]{2,1,0:T(8,128)(2,1)} %get-tuple-element, ...), kind=kLoop, calls=%fused_computation.164 | loop fusion | bytes 8388608 | tf_op jit(solution)/shard_map/slice | solution.py:509
  131.1 3.4 %fusion.73 = f32[512,352]{0,1:T(8,128)} fusion(bf16[512,2048]{1,0:T(8,128)(2,1)} %all-gather.2.cloned.1.call-done, bf16[2048,352]{0,1:T(8,128)(2,1)S(1)} %copy-done.15), kind=kOutput, calls=%fused_computation.166 | convolution fusion | flops 738197504 | bytes 4259840 | tf_op jit(solution)/shard_map/dot_general | solution.py:20
  134.5 5.4 %fusion.14 = f32[512,2048,1]{1,0,2:T(8,128)} fusion(bf16[8,16,2048]{2,1,0:T(8,128)(2,1)} %param.30, bf16[512,2048]{1,0:T(8,128)(2,1)} %all-gather.2.cloned.1.call-done, bf16[8,2048,16]{1,2,0:T(8,128)(2,1)} %param.29, pred[512,8]{0,1:T(8,128)(4,1)S(1)} %iota_compare_fusion.4), kind=kOutput, calls=%fused_computation.22 | convolution fusion | flops 537001984 | bytes 7344128 | tf_op jit(solution)/shard_map/dot_general | solution.py:48
  140.0 6.6 %fusion = bf16[512,2048]{1,0:T(8,128)(2,1)} fusion(f32[512,2048,1]{1,0,2:T(8,128)} %fusion.14, bf16[352,2048]{1,0:T(8,128)(2,1)S(1)} %copy-done, bf16[512,2048]{1,0:T(8,128)(2,1)} %all-gather.2.cloned.1.call-done, bf16[2048,352]{0,1:T(8,128)(2,1)S(1)} %copy-done.16, f32[512,352]{0,1:T(8,128)} %fusion.73), kind=kOutput, calls=%fused_computation.1 | convolution fusion | flops 1479573504 | bytes 11993088 | tf_op jit(solution)/shard_map/dot_general | solution.py:23
  151.4 1.6 collective-permute-start.17
  154.6 3.9 %collective-permute-start.24 = (bf16[256,1024]{1,0:T(8,128)(2,1)S(1)}, bf16[256,1024]{1,0:T(8,128)(2,1)S(1)}, u32[]{:S(2)}, u32[]{:S(2)}) collective-permute-start(bf16[256,1024]{1,0:T(8,128)(2,1)S(1)} %add_convert_fusion.2), channel_id=1, source_target_pairs={{0,2},{7,5},{8,10},{15,13},{16,18},{23,21},{24,26},{31,29}} | collective-permute-start | bytes 1572872 | tf_op jit(solution)/shard_map/ppermute | solution.py:396
  158.5 5.3 %collective-permute-done.29 = f32[24,2048]{1,0:T(8,128)S(1)} collective-permute-done((f32[24,2048]{1,0:T(8,128)S(1)}, f32[24,2048]{1,0:T(8,128)S(1)}, u32[]{:S(2)}, u32[]{:S(2)}) %collective-permute-start.29) | collective-permute-done | bytes 196640 | tf_op jit(solution)/shard_map/ppermute | solution.py:411
  163.8 2.9 %collective-permute-start.30 = (f32[24,2048]{1,0:T(8,128)S(1)}, f32[24,2048]{1,0:T(8,128)S(1)}, u32[]{:S(2)}, u32[]{:S(2)}) collective-permute-start(f32[24,2048]{1,0:T(8,128)S(1)} %add.354), channel_id=1, source_target_pairs={{0,4},{1,5},{2,6},{3,7},{4,0},{5,1},{6,2},{7,3},{8,12},{9,13},{10,... | collective-permute-start | bytes 589832 | tf_op jit(solution)/shard_map/ppermute | solution.py:411
  166.7 4.9 %collective-permute-done.30 = f32[24,2048]{1,0:T(8,128)S(1)} collective-permute-done((f32[24,2048]{1,0:T(8,128)S(1)}, f32[24,2048]{1,0:T(8,128)S(1)}, u32[]{:S(2)}, u32[]{:S(2)}) %collective-permute-start.30) | collective-permute-done | bytes 196640 | tf_op jit(solution)/shard_map/ppermute | solution.py:411
  171.6 3.9 %collective-permute-start.14 = (bf16[256,1024]{1,0:T(8,128)(2,1)S(1)}, bf16[256,1024]{1,0:T(8,128)(2,1)S(1)}, u32[]{:S(2)}, u32[]{:S(2)}) collective-permute-start(bf16[256,1024]{1,0:T(8,128)(2,1)S(1)} %bitcast.128), channel_id=1, source_target_pairs={{0,1},{1,0},{2,3},{3,2},{4,5},{5,4},{6,7},{7,6},{8,9},{9,8},{10,11... | collective-permute-start | bytes 1572872 | tf_op jit(solution)/shard_map/ppermute | solution.py:357
  175.6 1.6 collective-permute-start.31
  177.2 1.7 add_convert_fusion.4
  178.8 7.6 %collective-permute-done.31 = f32[24,2048]{1,0:T(8,128)S(1)} collective-permute-done((f32[24,2048]{1,0:T(8,128)S(1)}, f32[24,2048]{1,0:T(8,128)S(1)}, u32[]{:S(2)}, u32[]{:S(2)}) %collective-permute-start.31) | collective-permute-done | bytes 196640 | tf_op jit(solution)/shard_map/ppermute | solution.py:411
  186.5 6.6 %collective-permute-start.18 = (bf16[256,1024]{1,0:T(8,128)(2,1)S(1)}, bf16[256,1024]{1,0:T(8,128)(2,1)S(1)}, u32[]{:S(2)}, u32[]{:S(2)}) collective-permute-start(bf16[256,1024]{1,0:T(8,128)(2,1)S(1)} %add_convert_fusion.4), channel_id=1, source_target_pairs={{0,2},{2,4},{5,3},{7,5},{8,10},{10,12},{13,11},{15,13},{16,18},{18... | collective-permute-start | bytes 1572872 | tf_op jit(solution)/shard_map/ppermute | solution.py:396
  193.1 1.5 collective-permute-start.32
  195.0 1.9 collective-permute-start.25
  196.9 2.0 collective-permute-done.32
  201.0 4.4 %collective-permute-start.19 = (bf16[256,1024]{1,0:T(8,128)(2,1)S(1)}, bf16[256,1024]{1,0:T(8,128)(2,1)S(1)}, u32[]{:S(2)}, u32[]{:S(2)}) collective-permute-start(bf16[256,1024]{1,0:T(8,128)(2,1)S(1)} %add_convert_fusion.3), channel_id=1, source_target_pairs={{0,2},{2,4},{4,6},{3,1},{5,3},{7,5},{8,10},{10,12},{12,14},{11,9},... | collective-permute-start | bytes 1572872 | tf_op jit(solution)/shard_map/ppermute | solution.py:396
  206.8 4.3 %collective-permute-start.26 = (bf16[256,1024]{1,0:T(8,128)(2,1)S(1)}, bf16[256,1024]{1,0:T(8,128)(2,1)S(1)}, u32[]{:S(2)}, u32[]{:S(2)}) collective-permute-start(bf16[256,1024]{1,0:T(8,128)(2,1)S(1)} %add_convert_fusion), channel_id=1, source_target_pairs={{0,2},{2,4},{4,6},{3,1},{5,3},{7,5},{8,10},{10,12},{12,14},{11,9},... | collective-permute-start | bytes 1572872 | tf_op jit(solution)/shard_map/ppermute | solution.py:396
  213.4 4.3 %collective-permute-done.26 = bf16[256,1024]{1,0:T(8,128)(2,1)S(1)} collective-permute-done((bf16[256,1024]{1,0:T(8,128)(2,1)S(1)}, bf16[256,1024]{1,0:T(8,128)(2,1)S(1)}, u32[]{:S(2)}, u32[]{:S(2)}) %collective-permute-start.26) | collective-permute-done | bytes 524320 | tf_op jit(solution)/shard_map/ppermute | solution.py:396
  218.1 1.5 collective-permute-start.34
  220.2 1.5 collective-permute-done.34
  222.5 1.9 fusion.10
  (149 shorter events, 38.3 us)
Async XLA Ops:
  7.2 123.9 %all-gather.2.cloned.1.call-start = ((), (), s32[]{:S(2)}) async-start(), calls=%async_computation.1 | async-start | bytes 2621440 | tf_op jit(solution)/shard_map/all_gather | solution.py:467
  16.9 12.2 %collective-permute-start.1 = (bf16[256,1152]{1,0:T(8,128)(2,1)S(1)}, bf16[256,1152]{1,0:T(8,128)(2,1)S(1)}, u32[]{:S(2)}, u32[]{:S(2)}) collective-permute-start(bf16[256,1152]{1,0:T(8,128)(2,1)S(1)} %maximum_select_fusion.refs_0_), channel_id=1, source_target_pairs={{0,2},{2,4},{4,6},{3,1},{5,3},{7,5},{8,10},{10,12},{12,14},{11,9},... | collective-permute-start | bytes 1769480 | tf_op jit(solution)/shard_map/ppermute | solution.py:383
  21.8 9.2 %collective-permute-start.7 = (bf16[128,1024]{1,0:T(8,128)(2,1)}, bf16[128,1024]{1,0:T(8,128)(2,1)S(1)}, u32[]{:S(2)}, u32[]{:S(2)}) collective-permute-start(bf16[128,1024]{1,0:T(8,128)(2,1)} %get-tuple-element.11), channel_id=1, source_target_pairs={{0,1},{1,0},{2,3},{3,2},{4,5},{5,4},{6,7},{7,6},{8,9},{9,8},{10,11... | collective-permute-start | bytes 786440 | tf_op jit(solution)/shard_map/ppermute | solution.py:357
  29.1 11.2 %collective-permute-start.2 = (bf16[256,1152]{1,0:T(8,128)(2,1)S(1)}, bf16[256,1152]{1,0:T(8,128)(2,1)}, u32[]{:S(2)}, u32[]{:S(2)}) collective-permute-start(bf16[256,1152]{1,0:T(8,128)(2,1)S(1)} %collective-permute-done.1.refs_1_), channel_id=1, source_target_pairs={{2,4},{4,6},{3,1},{5,3},{10,12},{12,14},{11,9},{13,11},{18,20},{20... | collective-permute-start | bytes 1769480 | tf_op jit(solution)/shard_map/ppermute | solution.py:383
  30.6 191.9 %reduce-scatter.2.cloned.1.call-start = ((), (), s32[]{:S(2)}) async-start(), calls=%async_computation.2 | async-start | bytes 2621440 | tf_op jit(solution)/shard_map/reduce_scatter | solution.py:476
  32.1 13.9 %collective-permute-start.8 = (bf16[256,1024]{1,0:T(8,128)(2,1)S(1)}, bf16[256,1024]{1,0:T(8,128)(2,1)}, u32[]{:S(2)}, u32[]{:S(2)}) collective-permute-start(bf16[256,1024]{1,0:T(8,128)(2,1)S(1)} %maximum_select_fusion.1.refs_0_), channel_id=1, source_target_pairs={{0,2},{2,4},{4,6},{3,1},{5,3},{7,5},{8,10},{10,12},{12,14},{11,9},... | collective-permute-start | bytes 1572872 | tf_op jit(solution)/shard_map/ppermute | solution.py:383
  40.3 18.4 %collective-permute-start.3 = (bf16[256,1152]{1,0:T(8,128)(2,1)}, bf16[256,1152]{1,0:T(8,128)(2,1)}, u32[]{:S(2)}, u32[]{:S(2)}) collective-permute-start(bf16[256,1152]{1,0:T(8,128)(2,1)} %collective-permute-done.2.refs_2_), channel_id=1, source_target_pairs={{4,6},{3,1},{12,14},{11,9},{20,22},{19,17},{28,30},{27,25}} | collective-permute-start | bytes 1769480 | tf_op jit(solution)/shard_map/ppermute | solution.py:383
  47.6 12.7 %collective-permute-start.6 = (bf16[256,1152]{1,0:T(8,128)(2,1)S(1)}, bf16[256,1152]{1,0:T(8,128)(2,1)}, u32[]{:S(2)}, u32[]{:S(2)}) collective-permute-start(bf16[256,1152]{1,0:T(8,128)(2,1)S(1)} %collective-permute-done.1.refs_1_), channel_id=1, source_target_pairs={{0,1},{1,0},{2,3},{3,2},{4,5},{5,4},{6,7},{7,6},{8,9},{9,8},{10,11... | collective-permute-start | bytes 1769480 | tf_op jit(solution)/shard_map/ppermute | solution.py:357
  47.7 13.5 %collective-permute-start.10 = (bf16[256,1024]{1,0:T(8,128)(2,1)}, bf16[256,1024]{1,0:T(8,128)(2,1)}, u32[]{:S(2)}, u32[]{:S(2)}) collective-permute-start(bf16[256,1024]{1,0:T(8,128)(2,1)} %collective-permute-done.9.refs_2_), channel_id=1, source_target_pairs={{4,6},{3,1},{12,14},{11,9},{20,22},{19,17},{28,30},{27,25}} | collective-permute-start | bytes 1572872 | tf_op jit(solution)/shard_map/ppermute | solution.py:383
  49.2 19.6 %collective-permute-start.5 = (bf16[256,1152]{1,0:T(8,128)(2,1)}, bf16[256,1152]{1,0:T(8,128)(2,1)}, u32[]{:S(2)}, u32[]{:S(2)}) collective-permute-start(bf16[256,1152]{1,0:T(8,128)(2,1)} %collective-permute-done.2.refs_2_), channel_id=1, source_target_pairs={{0,1},{1,0},{2,3},{3,2},{4,5},{5,4},{6,7},{7,6},{8,9},{9,8},{10,11... | collective-permute-start | bytes 1769480 | tf_op jit(solution)/shard_map/ppermute | solution.py:357
  58.8 10.9 %collective-permute-start.4 = (bf16[256,1152]{1,0:T(8,128)(2,1)}, bf16[256,1152]{1,0:T(8,128)(2,1)}, u32[]{:S(2)}, u32[]{:S(2)}) collective-permute-start(bf16[256,1152]{1,0:T(8,128)(2,1)} %collective-permute-done.3.refs_3_), channel_id=1, source_target_pairs={{0,1},{1,0},{2,3},{3,2},{4,5},{5,4},{6,7},{7,6},{8,9},{9,8},{10,11... | collective-permute-start | bytes 1769480 | tf_op jit(solution)/shard_map/ppermute | solution.py:357
  59.0 27.2 %collective-permute-start.11 = (bf16[256,1024]{1,0:T(8,128)(2,1)}, bf16[256,1024]{1,0:T(8,128)(2,1)S(1)}, u32[]{:S(2)}, u32[]{:S(2)}) collective-permute-start(bf16[256,1024]{1,0:T(8,128)(2,1)} %collective-permute-done.8.refs_1_), channel_id=1, source_target_pairs={{0,1},{1,0},{2,3},{3,2},{4,5},{5,4},{6,7},{7,6},{8,9},{9,8},{10,11... | collective-permute-start | bytes 1572872 | tf_op jit(solution)/shard_map/ppermute | solution.py:357
  60.3 25.9 %collective-permute-start.12 = (bf16[256,1024]{1,0:T(8,128)(2,1)}, bf16[256,1024]{1,0:T(8,128)(2,1)S(1)}, u32[]{:S(2)}, u32[]{:S(2)}) collective-permute-start(bf16[256,1024]{1,0:T(8,128)(2,1)} %collective-permute-done.9.refs_2_), channel_id=1, source_target_pairs={{0,1},{1,0},{2,3},{3,2},{4,5},{5,4},{6,7},{7,6},{8,9},{9,8},{10,11... | collective-permute-start | bytes 1572872 | tf_op jit(solution)/shard_map/ppermute | solution.py:357
  61.2 25.0 %collective-permute-start.13 = (bf16[256,1024]{1,0:T(8,128)(2,1)}, bf16[256,1024]{1,0:T(8,128)(2,1)S(1)}, u32[]{:S(2)}, u32[]{:S(2)}) collective-permute-start(bf16[256,1024]{1,0:T(8,128)(2,1)} %collective-permute-done.10.refs_3_), channel_id=1, source_target_pairs={{0,1},{1,0},{2,3},{3,2},{4,5},{5,4},{6,7},{7,6},{8,9},{9,8},{10,11... | collective-permute-start | bytes 1572872 | tf_op jit(solution)/shard_map/ppermute | solution.py:357
  128.4 21.8 %collective-permute-start.16 = (bf16[256,1024]{1,0:T(8,128)(2,1)}, bf16[256,1024]{1,0:T(8,128)(2,1)}, u32[]{:S(2)}, u32[]{:S(2)}) collective-permute-start(bf16[256,1024]{1,0:T(8,128)(2,1)} %bitcast.17), channel_id=1, source_target_pairs={{0,1},{1,0},{2,3},{3,2},{4,5},{5,4},{6,7},{7,6},{8,9},{9,8},{10,11... | collective-permute-start | bytes 1572872 | tf_op jit(solution)/shard_map/ppermute | solution.py:357
  128.4 47.1 %collective-permute-start.15 = (bf16[256,1024]{1,0:T(8,128)(2,1)}, bf16[256,1024]{1,0:T(8,128)(2,1)}, u32[]{:S(2)}, u32[]{:S(2)}) collective-permute-start(bf16[256,1024]{1,0:T(8,128)(2,1)} %bitcast.19), channel_id=1, source_target_pairs={{0,1},{1,0},{2,3},{3,2},{4,5},{5,4},{6,7},{7,6},{8,9},{9,8},{10,11... | collective-permute-start | bytes 1572872 | tf_op jit(solution)/shard_map/ppermute | solution.py:357
  128.9 24.4 %collective-permute-start.23 = (bf16[256,1024]{1,0:T(8,128)(2,1)}, bf16[256,1024]{1,0:T(8,128)(2,1)}, u32[]{:S(2)}, u32[]{:S(2)}) collective-permute-start(bf16[256,1024]{1,0:T(8,128)(2,1)} %bitcast.21), channel_id=1, source_target_pairs={{0,1},{1,0},{2,3},{3,2},{4,5},{5,4},{6,7},{7,6},{8,9},{9,8},{10,11... | collective-permute-start | bytes 1572872 | tf_op jit(solution)/shard_map/ppermute | solution.py:357
  151.4 24.1 %collective-permute-start.17 = (bf16[256,1024]{1,0:T(8,128)(2,1)S(1)}, bf16[256,1024]{1,0:T(8,128)(2,1)S(1)}, u32[]{:S(2)}, u32[]{:S(2)}) collective-permute-start(bf16[256,1024]{1,0:T(8,128)(2,1)S(1)} %add_convert_fusion.5), channel_id=1, source_target_pairs={{0,2},{7,5},{8,10},{15,13},{16,18},{23,21},{24,26},{31,29}} | collective-permute-start | bytes 1572872 | tf_op jit(solution)/shard_map/ppermute | solution.py:396
  153.1 40.0 %collective-permute-start.22 = (bf16[256,1024]{1,0:T(8,128)(2,1)S(1)}, bf16[256,1024]{1,0:T(8,128)(2,1)S(1)}, u32[]{:S(2)}, u32[]{:S(2)}) collective-permute-start(bf16[256,1024]{1,0:T(8,128)(2,1)S(1)} %bitcast.129), channel_id=1, source_target_pairs={{0,1},{1,0},{2,3},{3,2},{4,5},{5,4},{6,7},{7,6},{8,9},{9,8},{10,11... | collective-permute-start | bytes 1572872 | tf_op jit(solution)/shard_map/ppermute | solution.py:357
  153.2 10.6 %collective-permute-start.29 = (f32[24,2048]{1,0:T(8,128)S(1)}, f32[24,2048]{1,0:T(8,128)S(1)}, u32[]{:S(2)}, u32[]{:S(2)}) collective-permute-start(f32[24,2048]{1,0:T(8,128)S(1)} %add.353), channel_id=1, source_target_pairs={{0,2},{1,3},{2,0},{3,1},{4,6},{5,7},{6,4},{7,5},{8,10},{9,11},{10,... | collective-permute-start | bytes 589832 | tf_op jit(solution)/shard_map/ppermute | solution.py:411
  154.6 40.1 %collective-permute-start.24 = (bf16[256,1024]{1,0:T(8,128)(2,1)S(1)}, bf16[256,1024]{1,0:T(8,128)(2,1)S(1)}, u32[]{:S(2)}, u32[]{:S(2)}) collective-permute-start(bf16[256,1024]{1,0:T(8,128)(2,1)S(1)} %add_convert_fusion.2), channel_id=1, source_target_pairs={{0,2},{7,5},{8,10},{15,13},{16,18},{23,21},{24,26},{31,29}} | collective-permute-start | bytes 1572872 | tf_op jit(solution)/shard_map/ppermute | solution.py:396
  163.8 7.7 %collective-permute-start.30 = (f32[24,2048]{1,0:T(8,128)S(1)}, f32[24,2048]{1,0:T(8,128)S(1)}, u32[]{:S(2)}, u32[]{:S(2)}) collective-permute-start(f32[24,2048]{1,0:T(8,128)S(1)} %add.354), channel_id=1, source_target_pairs={{0,4},{1,5},{2,6},{3,7},{4,0},{5,1},{6,2},{7,3},{8,12},{9,13},{10,... | collective-permute-start | bytes 589832 | tf_op jit(solution)/shard_map/ppermute | solution.py:411
  171.6 27.5 %collective-permute-start.14 = (bf16[256,1024]{1,0:T(8,128)(2,1)S(1)}, bf16[256,1024]{1,0:T(8,128)(2,1)S(1)}, u32[]{:S(2)}, u32[]{:S(2)}) collective-permute-start(bf16[256,1024]{1,0:T(8,128)(2,1)S(1)} %bitcast.128), channel_id=1, source_target_pairs={{0,1},{1,0},{2,3},{3,2},{4,5},{5,4},{6,7},{7,6},{8,9},{9,8},{10,11... | collective-permute-start | bytes 1572872 | tf_op jit(solution)/shard_map/ppermute | solution.py:357
  175.5 30.0 %collective-permute-start.21 = (bf16[256,1024]{1,0:T(8,128)(2,1)S(1)}, bf16[256,1024]{1,0:T(8,128)(2,1)S(1)}, u32[]{:S(2)}, u32[]{:S(2)}) collective-permute-start(bf16[256,1024]{1,0:T(8,128)(2,1)S(1)} %bitcast.127), channel_id=1, source_target_pairs={{0,1},{1,0},{2,3},{3,2},{4,5},{5,4},{6,7},{7,6},{8,9},{9,8},{10,11... | collective-permute-start | bytes 1572872 | tf_op jit(solution)/shard_map/ppermute | solution.py:357
  175.6 10.9 %collective-permute-start.31 = (f32[24,2048]{1,0:T(8,128)S(1)}, f32[24,2048]{1,0:T(8,128)S(1)}, u32[]{:S(2)}, u32[]{:S(2)}) collective-permute-start(f32[24,2048]{1,0:T(8,128)S(1)} %add.355), channel_id=1, source_target_pairs={{0,8},{8,0},{16,24},{24,16},{1,9},{9,1},{17,25},{25,17},{2,10},{10... | collective-permute-start | bytes 589832 | tf_op jit(solution)/shard_map/ppermute | solution.py:411
  186.5 13.2 %collective-permute-start.18 = (bf16[256,1024]{1,0:T(8,128)(2,1)S(1)}, bf16[256,1024]{1,0:T(8,128)(2,1)S(1)}, u32[]{:S(2)}, u32[]{:S(2)}) collective-permute-start(bf16[256,1024]{1,0:T(8,128)(2,1)S(1)} %add_convert_fusion.4), channel_id=1, source_target_pairs={{0,2},{2,4},{5,3},{7,5},{8,10},{10,12},{13,11},{15,13},{16,18},{18... | collective-permute-start | bytes 1572872 | tf_op jit(solution)/shard_map/ppermute | solution.py:396
  193.1 5.7 %collective-permute-start.32 = (f32[24,2048]{1,0:T(8,128)S(1)}, f32[24,2048]{1,0:T(8,128)S(1)}, u32[]{:S(2)}, u32[]{:S(2)}) collective-permute-start(f32[24,2048]{1,0:T(8,128)S(1)} %add.356), channel_id=1, source_target_pairs={{0,16},{8,24},{16,0},{24,8},{1,17},{9,25},{17,1},{25,9},{2,18},{10... | collective-permute-start | bytes 589832 | tf_op jit(solution)/shard_map/ppermute | solution.py:411
  195.0 10.5 %collective-permute-start.25 = (bf16[256,1024]{1,0:T(8,128)(2,1)S(1)}, bf16[256,1024]{1,0:T(8,128)(2,1)S(1)}, u32[]{:S(2)}, u32[]{:S(2)}) collective-permute-start(bf16[256,1024]{1,0:T(8,128)(2,1)S(1)} %add_convert_fusion.1), channel_id=1, source_target_pairs={{0,2},{2,4},{5,3},{7,5},{8,10},{10,12},{13,11},{15,13},{16,18},{18... | collective-permute-start | bytes 1572872 | tf_op jit(solution)/shard_map/ppermute | solution.py:396
  201.0 12.0 %collective-permute-start.19 = (bf16[256,1024]{1,0:T(8,128)(2,1)S(1)}, bf16[256,1024]{1,0:T(8,128)(2,1)S(1)}, u32[]{:S(2)}, u32[]{:S(2)}) collective-permute-start(bf16[256,1024]{1,0:T(8,128)(2,1)S(1)} %add_convert_fusion.3), channel_id=1, source_target_pairs={{0,2},{2,4},{4,6},{3,1},{5,3},{7,5},{8,10},{10,12},{12,14},{11,9},... | collective-permute-start | bytes 1572872 | tf_op jit(solution)/shard_map/ppermute | solution.py:396
  206.8 10.9 %collective-permute-start.26 = (bf16[256,1024]{1,0:T(8,128)(2,1)S(1)}, bf16[256,1024]{1,0:T(8,128)(2,1)S(1)}, u32[]{:S(2)}, u32[]{:S(2)}) collective-permute-start(bf16[256,1024]{1,0:T(8,128)(2,1)S(1)} %add_convert_fusion), channel_id=1, source_target_pairs={{0,2},{2,4},{4,6},{3,1},{5,3},{7,5},{8,10},{10,12},{12,14},{11,9},... | collective-permute-start | bytes 1572872 | tf_op jit(solution)/shard_map/ppermute | solution.py:396
  212.5 5.6 %collective-permute-start.33 = (f32[24,1]{0,1:T(1,128)S(1)}, f32[24,1]{0,1:T(1,128)S(1)}, u32[]{:S(2)}, u32[]{:S(2)}) collective-permute-start(f32[24,1]{0,1:T(1,128)S(1)} %bitcast.130), channel_id=1, source_target_pairs={{0,8},{8,0},{16,24},{24,16},{1,9},{9,1},{17,25},{25,17},{2,10},{10... | collective-permute-start | bytes 296 | tf_op jit(solution)/shard_map/ppermute | solution.py:411
  213.4 8.9 %collective-permute-start.20 = (bf16[128,1024]{1,0:T(8,128)(2,1)S(1)}, bf16[128,1024]{1,0:T(8,128)(2,1)S(1)}, u32[]{:S(2)}, u32[]{:S(2)}) collective-permute-start(bf16[128,1024]{1,0:T(8,128)(2,1)S(1)} %broadcast_select_fusion.1), channel_id=1, source_target_pairs={{0,1},{1,0},{2,3},{3,2},{4,5},{5,4},{6,7},{7,6},{8,9},{9,8},{10,11... | collective-permute-start | bytes 786440 | tf_op jit(solution)/shard_map/ppermute | solution.py:357
  (24 other events, 387.4 us)
Sparse Core Ops, SparseCore 0:
  30.7 38.4 all-gather.1
  146.8 42.8 reduce-scatter.1

commit v2 on v0

--- a/solution.py
+++ b/solution.py
@@ -1,6 +1,10 @@
+import functools
+
 import jax
 import jax.numpy as jnp
 from jax import lax
+from jax.experimental import pallas as pl
+from jax.experimental.pallas import tpu as pltpu
 from jax.sharding import PartitionSpec as P
 
 CAP = 32
@@ -144,6 +148,265 @@
     return (sublayer_out, last_norm, block_logit[:, None])
 
 
+AHEAD = 3
+
+
+def prep_kernel(tok_ref, gain_ref, routes_ref, gates_ref, packed_ref):
+    rows, width = tok_ref.shape
+    experts = 32
+    values = tok_ref[...].astype(jnp.float32)
+    scaled = lax.rsqrt(jnp.mean(values * values, axis=-1, keepdims=True) + 1e-06)
+    packed_ref[:, :width] = (values * scaled * gain_ref[...].astype(jnp.float32)[None, :]).astype(
+        jnp.bfloat16
+    )
+    numbers = lax.broadcasted_iota(jnp.int32, (experts, rows), 0)
+    chosen = jnp.zeros((experts, rows), jnp.float32)
+    weight = jnp.zeros((experts, rows), jnp.float32)
+    for k in range(routes_ref.shape[0]):
+        hit = routes_ref[k : k + 1, :] == numbers
+        chosen = jnp.where(hit, 1.0, chosen)
+        weight = jnp.where(hit, gates_ref[k : k + 1, :].astype(jnp.float32), weight)
+    row = lax.broadcasted_iota(jnp.int32, (rows, rows), 0)
+    column = lax.broadcasted_iota(jnp.int32, (rows, rows), 1)
+    upto = jnp.where(row <= column, 1.0, 0.0).astype(jnp.bfloat16)
+    count = jnp.dot(chosen.astype(jnp.bfloat16), upto, preferred_element_type=jnp.float32)
+    place = jnp.where(chosen > 0.5, count - 1.0, -1.0)
+    packed_ref[:experts, width:] = place.astype(jnp.bfloat16)
+    packed_ref[experts : 2 * experts, width:] = weight.astype(jnp.bfloat16)
+    packed_ref[2 * experts :, width:] = jnp.zeros((rows - 2 * experts, rows), jnp.bfloat16)
+
+
+def prepare(tokens, norm_gain, routes, route_gates):
+    rows, width = tokens.shape
+    return pl.pallas_call(
+        prep_kernel,
+        out_shape=jax.ShapeDtypeStruct((rows, width + rows), jnp.bfloat16),
+        name="prepare",
+    )(tokens, norm_gain, routes.T, route_gates.T)
+
+
+def experts_kernel(
+    ahead,
+    first_ref,
+    packed_hbm,
+    gate_hbm,
+    up_hbm,
+    down_hbm,
+    out_hbm,
+    packed,
+    gates,
+    ups,
+    downs,
+    held,
+    mix,
+    incoming,
+    outs,
+    result,
+    packed_sem,
+    gate_sem,
+    up_sem,
+    down_sem,
+    out_sem,
+):
+    experts, width, hidden = gate_hbm.shape
+    sources = packed.shape[0]
+    rows = packed.shape[1]
+    numbered = held.shape[0]
+
+    def load(hbm, buffer, sem, e):
+        return pltpu.make_async_copy(hbm.at[e], buffer.at[e % 2], sem.at[e % 2])
+
+    packed_in = [
+        pltpu.make_async_copy(packed_hbm.at[pl.ds(s * rows, rows)], packed.at[s], packed_sem.at[s])
+        for s in range(sources)
+    ]
+    for copy in packed_in:
+        copy.start()
+    gate_in = [load(gate_hbm, gates, gate_sem, e) for e in range(experts)]
+    up_in = [load(up_hbm, ups, up_sem, e) for e in range(experts)]
+    down_in = [load(down_hbm, downs, down_sem, e) for e in range(experts)]
+    order = [copy for e in range(experts) for copy in (gate_in[e], up_in[e], down_in[e])]
+    for copy in order[:ahead]:
+        copy.start()
+
+    def arrived(i):
+        order[i].wait()
+        if i + ahead < len(order):
+            order[i + ahead].start()
+
+    slots = lax.broadcasted_iota(jnp.int32, (CAP, rows), 0).astype(jnp.float32)
+    for s in range(sources):
+        packed_in[s].wait()
+        held[...] = packed[s, :numbered, width:].astype(jnp.float32)
+        picks = []
+        for e in range(experts):
+            place = held[pl.ds(first_ref[0] + e, 1), :]
+            weight = held[pl.ds(first_ref[0] + numbered // 2 + e, 1), :]
+            hit = place == slots
+            picks.append(jnp.where(hit, 1.0, 0.0))
+            mix[s, e * CAP : (e + 1) * CAP, :] = jnp.where(hit, weight, 0.0).astype(jnp.bfloat16)
+        pick = jnp.concatenate(picks, axis=0).astype(jnp.bfloat16)
+        chosen = jnp.dot(pick, packed[s, :, :width], preferred_element_type=jnp.float32)
+        chosen = chosen.astype(jnp.bfloat16)
+        for e in range(experts):
+            incoming[e, s * CAP : (s + 1) * CAP, :] = chosen[e * CAP : (e + 1) * CAP]
+    for e in range(experts):
+        inputs = incoming[e]
+        arrived(3 * e)
+        gate = jnp.dot(inputs, gates[e % 2], preferred_element_type=jnp.float32)
+        arrived(3 * e + 1)
+        up = jnp.dot(inputs, ups[e % 2], preferred_element_type=jnp.float32)
+        mid = (gate / (1.0 + jnp.exp(-gate)) * up).astype(jnp.bfloat16)
+        arrived(3 * e + 2)
+        out = jnp.dot(mid, downs[e % 2], preferred_element_type=jnp.float32).astype(jnp.bfloat16)
+        for s in range(sources):
+            outs[s, e * CAP : (e + 1) * CAP, :] = out[s * CAP : (s + 1) * CAP]
+    sent = []
+    for s in range(sources):
+        result[s] = lax.dot_general(
+            mix[s], outs[s], (((0,), (0,)), ((), ())), preferred_element_type=jnp.float32
+        ).astype(jnp.bfloat16)
+        copy = pltpu.make_async_copy(
+            result.at[s], out_hbm.at[pl.ds(s * rows, rows)], out_sem.at[s]
+        )
+        copy.start()
+        sent.append(copy)
+    for copy in sent:
+        copy.wait()
+
+
+def run_experts(first, packed, gate, up, down, rows):
+    experts, width, hidden = gate.shape
+    sources = packed.shape[0] // rows
+    anywhere = pl.BlockSpec(memory_space=pl.ANY)
+    slots = sources * CAP
+    return pl.pallas_call(
+        functools.partial(experts_kernel, AHEAD),
+        in_specs=[pl.BlockSpec(memory_space=pltpu.SMEM)] + [anywhere] * 4,
+        out_specs=anywhere,
+        out_shape=jax.ShapeDtypeStruct((sources * rows, width), jnp.bfloat16),
+        scratch_shapes=[
+            pltpu.VMEM((sources, rows, packed.shape[1]), jnp.bfloat16),
+            pltpu.VMEM((2, width, hidden), jnp.bfloat16),
+            pltpu.VMEM((2, width, hidden), jnp.bfloat16),
+            pltpu.VMEM((2, hidden, width), jnp.bfloat16),
+            pltpu.VMEM((64, rows), jnp.float32),
+            pltpu.VMEM((sources, experts * CAP, rows), jnp.bfloat16),
+            pltpu.VMEM((experts, slots, width), jnp.bfloat16),
+            pltpu.VMEM((sources, experts * CAP, width), jnp.bfloat16),
+            pltpu.VMEM((sources, rows, width), jnp.bfloat16),
+            pltpu.SemaphoreType.DMA((sources,)),
+            pltpu.SemaphoreType.DMA((2,)),
+            pltpu.SemaphoreType.DMA((2,)),
+            pltpu.SemaphoreType.DMA((2,)),
+            pltpu.SemaphoreType.DMA((sources,)),
+        ],
+        compiler_params=pltpu.CompilerParams(vmem_limit_bytes=58 << 20),
+        cost_estimate=pl.CostEstimate(
+            flops=6 * experts * slots * width * hidden,
+            bytes_accessed=6 * experts * width * hidden,
+            transcendentals=experts * slots * hidden,
+        ),
+        name="run_experts",
+    )(first, packed, gate, up, down)
+
+
+def across(value, combine, axis, size):
+    step = 1
+    while step < size:
+        pairs = [(i, i ^ step) for i in range(lax.axis_size(axis))]
+        value = combine(value, lax.ppermute(value, axis, pairs))
+        step *= 2
+    return value
+
+
+def total(value, axis, steps, size):
+    sent = value.astype(jnp.bfloat16)
+    got = [lax.ppermute(sent, axis, [(i, i ^ step) for i in range(size)]) for step in steps]
+    for part in got:
+        value = value + part.astype(jnp.float32)
+    return value
+
+
+def from_peer(value, step, size):
+    return lax.ppermute(value, "dp", [(i, i ^ step) for i in range(size)])
+
+
+def local_line(
+    tokens,
+    norm_gain,
+    routes,
+    route_gates,
+    lengths,
+    request_adapter,
+    adapter_slot,
+    expert_gate,
+    expert_up,
+    expert_down,
+    shared_gate,
+    shared_up_weight,
+    shared_down,
+    adapter_down,
+    adapter_up,
+    head_weight,
+):
+    tok_rows, width = tokens.shape
+    tensor_size = lax.axis_size("tensor")
+    data_size = lax.axis_size("dp")
+    tensor_pos = lax.axis_index("tensor")
+    data_pos = lax.axis_index("dp")
+    experts = expert_gate.shape[0]
+    packed = prepare(tokens, norm_gain, routes, route_gates)
+    pooled = lax.all_gather(packed, "tensor", axis=0, tiled=True)
+    normed = packed[:, :width]
+    peers = [normed] + [from_peer(normed, d, data_size) for d in range(1, data_size)]
+    peer_rows = jnp.concatenate(peers)
+    block_rows = jnp.arange(tok_rows, dtype=jnp.int32)
+    peer_dp = jnp.arange(data_size, dtype=jnp.int32) ^ data_pos
+    bases = (peer_dp * tensor_size + tensor_pos) * tok_rows
+    peer_positions = (bases[:, None] + block_rows[None, :]).reshape(-1)
+    peer_slots = token_slots(peer_positions, lengths, request_adapter, adapter_slot)
+    held_slots = peer_slots - data_pos * adapter_down.shape[0]
+    peer_part = feed_forward(peer_rows, shared_gate, shared_up_weight, shared_down)
+    peer_part = peer_part + adapter_delta(peer_rows, held_slots, adapter_down, adapter_up)
+    peer_part = peer_part.astype(jnp.bfloat16)
+    parts = peer_part.reshape(data_size, tok_rows, width)
+    came = [from_peer(parts[d], d, data_size) for d in range(1, data_size)]
+    first = (tensor_pos * experts).astype(jnp.int32).reshape(1)
+    first, peer_part = lax.optimization_barrier((first, peer_part))
+    partial = run_experts(first, pooled, expert_gate, expert_up, expert_down, tok_rows)
+    partial, *came = lax.optimization_barrier((partial, *came))
+    routed = lax.psum_scatter(partial, "tensor", scatter_dimension=0, tiled=True)
+    ends = jnp.cumsum(lengths) - 1
+    owner, row = ends // tok_rows, ends % tok_rows
+    owner_dp, owner_tensor = owner // tensor_size, owner % tensor_size
+    line_row = jnp.where(owner_dp == data_pos, owner_tensor * tok_rows + row, -1)
+    peer_row = jnp.where(owner_tensor == tensor_pos, (owner_dp ^ data_pos) * tok_rows + row, -1)
+
+    def pick(at, count):
+        return jnp.where(
+            at[:, None] == jnp.arange(count, dtype=jnp.int32)[None, :], 1.0, 0.0
+        ).astype(jnp.bfloat16)
+
+    last_part = jnp.dot(
+        pick(line_row, tensor_size * tok_rows), partial, preferred_element_type=jnp.float32
+    )
+    last_part = last_part + jnp.dot(
+        pick(peer_row, data_size * tok_rows), peer_part, preferred_element_type=jnp.float32
+    )
+    last = across(last_part, jnp.add, "tensor", 2)
+    last = across(last, jnp.add, "dp", data_size)
+    last = total(last, "tensor", range(2, tensor_size, 2), tensor_size).astype(jnp.bfloat16)
+    last_values = last.astype(jnp.float32)
+    last_norm = jnp.sqrt(jnp.sum(last_values * last_values, axis=1))
+    logits = jnp.dot(last, head_weight, preferred_element_type=jnp.float32)
+    block_logit = across(jnp.max(logits, axis=1, keepdims=True), jnp.maximum, "dp", data_size)
+    out = routed.astype(jnp.float32) + parts[0].astype(jnp.float32)
+    for part in came:
+        out = out + part.astype(jnp.float32)
+    return (out.astype(jnp.bfloat16), last_norm, block_logit)
+
+
 def solution(mesh):
     placed = (
         P(("dp", "tensor"), None),
@@ -163,8 +426,9 @@
         P("dp", None, None),
         P(None, ("dp", "tensor")),
     )
+    short = mesh.shape["tensor"] == 8 and mesh.shape["dp"] == 4
     return jax.shard_map(
-        local,
+        local_line if short else local,
         mesh=mesh,
         in_specs=placed,
         out_specs=(P(("dp", "tensor"), None), P(), P(None, "tensor")),

time: 400 us -> 155 us (0.39)
  waiting for transfers between devices: 253 us -> 59.6 us
  matrix products: 69.5 us -> 22.9 us
  Pallas kernels: 0 us -> 30.4 us
  blocking collectives: 23.3 us -> 0 us
  other arithmetic: 28.3 us -> 5.36 us
  starting transfers between devices: 5.19 us -> 18.4 us
    psum x1 -> x0, waiting for transfers between devices: 122 us -> none  [local(): last_states = lax.psum(last_part, ('dp', 'tensor'))]
    all_to_all x1 -> x0, waiting for transfers between devices: 91 us -> none  [local(): lax.all_to_all(expert_out, 'tensor', split_axis=0, concat_axis=0, tiled=T...]
    dot_general x8 -> x4, matrix products: 59.6 us -> 12.2 us  [the longest x1 4.88 us: local_line(): logits = jnp.dot(last, head_weight, preferred_element_type=jnp.float32)]
    ppermute x0 -> x14, waiting for transfers between devices: none -> 46.4 us  [the longest x6 20.6 us: from_peer(): return lax.ppermute(value, 'dp', [(i, i ^ step) for i in range(size)])]
    all_gather x4 -> x1, waiting for transfers between devices: 39 us -> 4.45 us  [local_line(): pooled = lax.all_gather(packed, 'tensor', axis=0, tiled=True)]
    pallas_call x0 -> x2, Pallas kernels: none -> 30.4 us  [the longest x1 28.2 us: run_experts(): pl.pallas_call(functools.partial(experts_kernel, AHEAD), in_specs=[pl.Blo...]
    another operation x4 -> x2, other arithmetic: 23.7 us -> 0.16 us  [the longest x1 23.4 us: local(): source_place = jnp.cumsum(source_chosen.astype(jnp.int32), axis=1) - 1]
    ppermute x0 -> x14, starting transfers between devices: none -> 18.3 us  [the longest x6 8.03 us: from_peer(): return lax.ppermute(value, 'dp', [(i, i ^ step) for i in range(size)])]
  transfers between devices with their start and end apart: 7 -> 16, of which waited for: 4 -> 11; matrix products, arithmetic and copies ran while one was open for 22% -> 19% of each run, Pallas kernels for 0% -> 18%
where the time goes in v2:
time: 155 us
  waiting for transfers between devices  59.6 us (38%)
  Pallas kernels  30.4 us (20%)
  matrix products  22.9 us (15%)
  starting transfers between devices  18.4 us (12%)
  between operations  14.2 us (9%)
  other arithmetic  5.36 us (3%)
  local copies, waits for them, and re-layouts  4.27 us (3%)
    pallas_call x1, Pallas kernels, run_experts(): pl.pallas_call(functools.partial(experts_kernel, AHEAD), in_specs=[pl.Blo...  28.2 us
    ppermute x6, waiting for transfers between devices, from_peer(): return lax.ppermute(value, 'dp', [(i, i ^ step) for i in range(size)])  20.6 us
    ppermute x5, waiting for transfers between devices, across(): value = combine(value, lax.ppermute(value, axis, pairs))  14.9 us
    ppermute x3, waiting for transfers between devices, total(): lax.ppermute(sent, axis, [(i, i ^ step) for i in range(size)])  10.9 us
    reduce_scatter x1, waiting for transfers between devices, local_line(): lax.psum_scatter(partial, 'tensor', scatter_dimension=0, tiled=True)  8.74 us
    ppermute x6, starting transfers between devices, from_peer(): return lax.ppermute(value, 'dp', [(i, i ^ step) for i in range(size)])  8.03 us
    ppermute x5, starting transfers between devices, across(): value = combine(value, lax.ppermute(value, axis, pairs))  6.75 us
    dot_general x1, matrix products, feed_forward(): return jnp.dot(hidden, down_mat, preferred_element_type=jnp.float32)  5.83 us
  transfers between devices with their start and end apart: 16, of which 11 were waited for; matrix products, arithmetic and copies ran while one was open for 19% of the time, Pallas kernels for 18%

profile of v2, /device:TPU:0, one launch (start us, length us, event | category | flops | bytes accessed | tf_op | source)
XLA Modules:
  0.0 155.2 jit_solution(8943959987188519350)
XLA Ops:
  7.2 2.2 %prepare.1 = bf16[128,2176]{1,0:T(8,128)(2,1)} custom-call(bf16[128,2048]{1,0:T(8,128)(2,1)} %tok_ref.1, bf16[2048]{0:T(1024)(128)(2,1)} %gain_ref.1, s32[6,128]{1,0:T(8,128)} %bitcast.39, bf16[6,128]{1,0:T(8,128)(2,1)} %bitcast.40), custom_call_target="tpu_custom_call" | custom-call | tf_op jit(solution)/shard_map/prepare/pallas_call | solution.py:181
  9.5 1.1 slice.24
  10.6 3.0 %collective-permute-start = (bf16[128,2048]{1,0:T(8,128)(2,1)S(1)}, bf16[128,2048]{1,0:T(8,128)(2,1)}, u32[]{:S(2)}, u32[]{:S(2)}) collective-permute-start(bf16[128,2048]{1,0:T(8,128)(2,1)S(1)} %slice.24), channel_id=1, source_target_pairs={{0,8},{8,0},{16,24},{24,16},{1,9},{9,1},{17,25},{25,17},{2,10},{10... | collective-permute-start | bytes 1572872 | tf_op jit(solution)/shard_map/ppermute | solution.py:332
  13.6 1.5 collective-permute-start.1
  17.7 8.7 %collective-permute-done = bf16[128,2048]{1,0:T(8,128)(2,1)} collective-permute-done((bf16[128,2048]{1,0:T(8,128)(2,1)S(1)}, bf16[128,2048]{1,0:T(8,128)(2,1)}, u32[]{:S(2)}, u32[]{:S(2)}) %collective-permute-start) | collective-permute-done | bytes 524320 | tf_op jit(solution)/shard_map/ppermute | solution.py:332
  26.5 11.9 %collective-permute-done.1 = bf16[128,2048]{1,0:T(8,128)(2,1)} collective-permute-done((bf16[128,2048]{1,0:T(8,128)(2,1)S(1)}, bf16[128,2048]{1,0:T(8,128)(2,1)}, u32[]{:S(2)}, u32[]{:S(2)}) %collective-permute-start.1) | collective-permute-done | bytes 524320 | tf_op jit(solution)/shard_map/ppermute | solution.py:332
  38.3 3.7 %fusion.30 = f32[512,352]{0,1:T(8,128)} fusion(bf16[2048,352]{0,1:T(8,128)(2,1)} %param.27, bf16[128,2048]{1,0:T(8,128)(2,1)} %collective-permute-done.2, bf16[128,2048]{1,0:T(8,128)(2,1)} %collective-permute-done.1, bf16[128,2048]{1,0:T(8,128)(2,1)} %collective-permute-done, bf16[128,2048]{1,0:T(8,128)(2,1)S(1)} %slice.24), kind=kOutput, calls=%fused_computation.57 | convolution fusion | flops 746586112 | bytes 4259840 | tf_op jit(solution)/shard_map/dot_general | solution.py:21
  42.1 4.9 %fusion.10 = f32[512,2048,1]{1,0,2:T(8,128)} fusion(bf16[8,16,2048]{2,1,0:T(8,128)(2,1)S(1)} %copy-done.5, bf16[8,2048,16]{1,2,0:T(8,128)(2,1)S(1)} %copy-done.6, pred[512,8]{0,1:T(8,128)(4,1)S(1)} %iota_compare_fusion.4, bf16[128,2048]{1,0:T(8,128)(2,1)} %collective-permute-done.2, bf16[128,2048]{1,0:T(8,128)(2,1)} %collective-permute-done.1, ...), kind=kOutput, calls=%fused_computation.10 | convolution fusion | flops 545390592 | bytes 7344128 | tf_op jit(solution)/shard_map/dot_general | solution.py:48
  47.0 5.8 %fusion = bf16[512,2048]{1,0:T(8,128)(2,1)S(1)} fusion(f32[512,2048,1]{1,0,2:T(8,128)} %fusion.10, bf16[352,2048]{1,0:T(8,128)(2,1)S(1)} %copy-done, f32[512,352]{0,1:T(8,128)} %fusion.30, bf16[2048,352]{0,1:T(8,128)(2,1)} %param.26, bf16[128,2048]{1,0:T(8,128)(2,1)} %collective-permute-done.2, bf16[128,2048]{1,0:T(8,128)(2,1)} %collective-permute-done.1, ...), kind=kOutput, calls=%fused_computation.1 | convolution fusion | flops 1487962112 | bytes 11993088 | tf_op jit(solution)/shard_map/dot_general | solution.py:23
  52.8 1.2 fusion.33
  54.0 1.2 collective-permute-start.3
  56.2 1.4 collective-permute-start.5
  57.5 4.4 %all-gather.2.cloned.1.call-done.packed_hbm = bf16[1024,2176]{1,0:T(8,128)(2,1)} async-done(((bf16[128,2176]{1,0:T(8,128)(2,1)}), bf16[1024,2176]{1,0:T(8,128)(2,1)}) %all-gather.2.cloned.1.call-update) | async-done | bytes 4456464 | tf_op jit(solution)/shard_map/all_gather | solution.py:360
  62.0 28.2 %run_experts.1 = bf16[1024,2048]{1,0:T(8,128)(2,1)} custom-call(s32[1]{0:T(128)} %bitcast.first_ref, bf16[1024,2176]{1,0:T(8,128)(2,1)} %all-gather.2.cloned.1.call-done.packed_hbm, bf16[4,2048,1408]{2,1,0:T(8,128)(2,1)} %gate_hbm.1, bf16[4,2048,1408]{2,1,0:T(8,128)(2,1)} %up_hbm.1, bf16[4,1408,2048]{2,1,0:T(8,128)(2,1)} %down_hbm.1), custom_call_target="tpu_custom_call" | custom-call | flops 17716740096 | bytes 69206016 | tf_op jit(solution)/shard_map/run_experts/pallas_call | solution.py:283
  91.4 3.1 %convolution_add_fusion = f32[24,2048]{1,0:T(8,128)S(1)} fusion(f32[24,2048]{1,0:T(8,128)S(1)} %fusion.20, bf16[1024,2048]{1,0:T(8,128)(2,1)} %run_experts.1, s32[24]{0:T(128)S(1)} %get-tuple-element.19), kind=kOutput, calls=%fused_computation.2 | convolution fusion | flops 100786176 | bytes 4587616 | tf_op jit(solution)/shard_map/dot_general | solution.py:391
  94.9 1.2 collective-permute-done.6
  96.1 1.7 %collective-permute-start.7 = (f32[24,2048]{1,0:T(8,128)S(1)}, f32[24,2048]{1,0:T(8,128)S(1)}, u32[]{:S(2)}, u32[]{:S(2)}) collective-permute-start(f32[24,2048]{1,0:T(8,128)S(1)} %add.151), channel_id=1, source_target_pairs={{0,8},{8,0},{16,24},{24,16},{1,9},{9,1},{17,25},{25,17},{2,10},{10... | collective-permute-start | bytes 589832 | tf_op jit(solution)/shard_map/ppermute | solution.py:318
  97.8 5.4 %collective-permute-done.7 = f32[24,2048]{1,0:T(8,128)S(1)} collective-permute-done((f32[24,2048]{1,0:T(8,128)S(1)}, f32[24,2048]{1,0:T(8,128)S(1)}, u32[]{:S(2)}, u32[]{:S(2)}) %collective-permute-start.7) | collective-permute-done | bytes 196640 | tf_op jit(solution)/shard_map/ppermute | solution.py:318
  103.2 1.8 %collective-permute-start.8 = (f32[24,2048]{1,0:T(8,128)S(1)}, f32[24,2048]{1,0:T(8,128)S(1)}, u32[]{:S(2)}, u32[]{:S(2)}) collective-permute-start(f32[24,2048]{1,0:T(8,128)S(1)} %add.152), channel_id=1, source_target_pairs={{0,16},{8,24},{16,0},{24,8},{1,17},{9,25},{17,1},{25,9},{2,18},{10... | collective-permute-start | bytes 589832 | tf_op jit(solution)/shard_map/ppermute | solution.py:318
  105.0 4.7 %collective-permute-done.8 = f32[24,2048]{1,0:T(8,128)S(1)} collective-permute-done((f32[24,2048]{1,0:T(8,128)S(1)}, f32[24,2048]{1,0:T(8,128)S(1)}, u32[]{:S(2)}, u32[]{:S(2)}) %collective-permute-start.8) | collective-permute-done | bytes 196640 | tf_op jit(solution)/shard_map/ppermute | solution.py:318
  109.7 1.3 collective-permute-start.10
  111.0 1.2 collective-permute-start.11
  112.2 1.1 collective-permute-start.9
  113.2 9.6 %collective-permute-done.10 = bf16[24,2048]{1,0:T(8,128)(2,1)S(1)} collective-permute-done((bf16[24,2048]{1,0:T(8,128)(2,1)S(1)}, bf16[24,2048]{1,0:T(8,128)(2,1)S(1)}, u32[]{:S(2)}, u32[]{:S(2)}) %collective-permute-start.10) | collective-permute-done | bytes 98336 | tf_op jit(solution)/shard_map/ppermute | solution.py:325
  122.8 1.3 collective-permute-done.9
  124.3 4.9 %convolution_reduce_fusion = f32[24]{0:T(128)S(1)} fusion(bf16[24,2048]{1,0:T(8,128)(2,1)S(1)} %get-tuple-element.16, bf16[2048,2048]{1,0:T(8,128)(2,1)} %param.31), kind=kOutput, calls=%fused_computation.8 | convolution fusion | flops 201375712 | bytes 8487008 | tf_op jit(solution)/shard_map/dot_general | solution.py:402
  129.2 1.5 collective-permute-start.12
  130.7 2.1 %collective-permute-done.12 = f32[24,1]{0,1:T(1,128)S(1)} collective-permute-done((f32[24,1]{0,1:T(1,128)S(1)}, f32[24,1]{0,1:T(1,128)S(1)}, u32[]{:S(2)}, u32[]{:S(2)}) %collective-permute-start.12) | collective-permute-done | bytes 128 | tf_op jit(solution)/shard_map/ppermute | solution.py:318
  132.8 1.5 collective-permute-start.13
  134.8 1.5 collective-permute-done.13
  136.8 8.7 %reduce-scatter.2.cloned.1.call-done = bf16[128,2048]{1,0:T(8,128)(2,1)} async-done(((bf16[1024,2048]{1,0:T(8,128)(2,1)}), bf16[128,2048]{1,0:T(8,128)(2,1)}) %reduce-scatter.2.cloned.1.call-update) | async-done | bytes 524304 | tf_op jit(solution)/shard_map/reduce_scatter | solution.py:379
  145.6 2.7 %add_convert_fusion = bf16[128,2048]{1,0:T(8,128)(2,1)} fusion(bf16[128,2048]{1,0:T(8,128)(2,1)} %collective-permute-done.5, bf16[128,2048]{1,0:T(8,128)(2,1)} %copy-done.4, bf16[128,2048]{1,0:T(8,128)(2,1)} %copy-done.3, bf16[128,2048]{1,0:T(8,128)(2,1)} %reduce-scatter.2.cloned.1.call-done, bf16[512,2048]{1,0:T(8,128)(2,1)S(1)} %fusion), kind=kLoop, calls=%fused_computation.9 | loop fusion | flops 2621440 | bytes 3145728 | tf_op jit(solution)/shard_map/convert_element_type | solution.py:407
  (46 shorter events, 6.4 us)
Async XLA Ops:
  7.2 39.8 %copy-start = (bf16[352,2048]{1,0:T(8,128)(2,1)S(1)}, bf16[352,2048]{1,0:T(8,128)(2,1)}, u32[]{:S(2)}) copy-start(bf16[352,2048]{1,0:T(8,128)(2,1)} %param.28) | copy-start | bytes 4325380
  7.2 54.8 %all-gather.2.cloned.1.call-start = ((), (), s32[]{:S(2)}) async-start(), calls=%async_computation.1 | async-start | bytes 5013504 | tf_op jit(solution)/shard_map/all_gather | solution.py:360
  9.4 136.1 %reduce-scatter.2.cloned.1.call-start = ((), (), s32[]{:S(2)}) async-start(), calls=%async_computation.2 | async-start | bytes 4718592 | tf_op jit(solution)/shard_map/reduce_scatter | solution.py:379
  10.6 31.5 %copy-start.2 = (bf16[128,2048]{1,0:T(8,128)(2,1)}, bf16[128,2048]{1,0:T(8,128)(2,1)S(1)}, u32[]{:S(2)}) copy-start(bf16[128,2048]{1,0:T(8,128)(2,1)S(1)} %slice.24) | copy-start | bytes 1572868
  10.6 15.9 %collective-permute-start = (bf16[128,2048]{1,0:T(8,128)(2,1)S(1)}, bf16[128,2048]{1,0:T(8,128)(2,1)}, u32[]{:S(2)}, u32[]{:S(2)}) collective-permute-start(bf16[128,2048]{1,0:T(8,128)(2,1)S(1)} %slice.24), channel_id=1, source_target_pairs={{0,8},{8,0},{16,24},{24,16},{1,9},{9,1},{17,25},{25,17},{2,10},{10... | collective-permute-start | bytes 1572872 | tf_op jit(solution)/shard_map/ppermute | solution.py:332
  13.6 24.7 %collective-permute-start.1 = (bf16[128,2048]{1,0:T(8,128)(2,1)S(1)}, bf16[128,2048]{1,0:T(8,128)(2,1)}, u32[]{:S(2)}, u32[]{:S(2)}) collective-permute-start(bf16[128,2048]{1,0:T(8,128)(2,1)S(1)} %slice.24), channel_id=1, source_target_pairs={{0,16},{8,24},{16,0},{24,8},{1,17},{9,25},{17,1},{25,9},{2,18},{10... | collective-permute-start | bytes 1572872 | tf_op jit(solution)/shard_map/ppermute | solution.py:332
  15.1 23.2 %collective-permute-start.2 = (bf16[128,2048]{1,0:T(8,128)(2,1)S(1)}, bf16[128,2048]{1,0:T(8,128)(2,1)}, u32[]{:S(2)}, u32[]{:S(2)}) collective-permute-start(bf16[128,2048]{1,0:T(8,128)(2,1)S(1)} %slice.24), channel_id=1, source_target_pairs={{0,24},{8,16},{16,8},{24,0},{1,25},{9,17},{17,9},{25,1},{2,26},{10... | collective-permute-start | bytes 1572872 | tf_op jit(solution)/shard_map/ppermute | solution.py:332
  17.7 24.3 %copy-start.5 = (bf16[8,16,2048]{2,1,0:T(8,128)(2,1)S(1)}, bf16[8,16,2048]{2,1,0:T(8,128)(2,1)}, u32[]{:S(2)}) copy-start(bf16[8,16,2048]{2,1,0:T(8,128)(2,1)} %param.30) | copy-start | bytes 1572868
  17.7 24.3 %copy-start.6 = (bf16[8,2048,16]{1,2,0:T(8,128)(2,1)S(1)}, bf16[8,2048,16]{1,2,0:T(8,128)(2,1)}, u32[]{:S(2)}) copy-start(bf16[8,2048,16]{1,2,0:T(8,128)(2,1)} %param.29) | copy-start | bytes 1572868
  54.0 36.1 %collective-permute-start.3 = (bf16[128,2048]{1,0:T(8,128)(2,1)}, bf16[128,2048]{1,0:T(8,128)(2,1)S(1)}, u32[]{:S(2)}, u32[]{:S(2)}) collective-permute-start(bf16[128,2048]{1,0:T(8,128)(2,1)} %get-tuple-element.24), channel_id=1, source_target_pairs={{0,8},{8,0},{16,24},{24,16},{1,9},{9,1},{17,25},{25,17},{2,10},{10... | collective-permute-start | bytes 1572872 | tf_op jit(solution)/shard_map/ppermute | solution.py:332
  55.3 34.9 %collective-permute-start.4 = (bf16[128,2048]{1,0:T(8,128)(2,1)}, bf16[128,2048]{1,0:T(8,128)(2,1)S(1)}, u32[]{:S(2)}, u32[]{:S(2)}) collective-permute-start(bf16[128,2048]{1,0:T(8,128)(2,1)} %get-tuple-element.23), channel_id=1, source_target_pairs={{0,16},{8,24},{16,0},{24,8},{1,17},{9,25},{17,1},{25,9},{2,18},{10... | collective-permute-start | bytes 1572872 | tf_op jit(solution)/shard_map/ppermute | solution.py:332
  56.2 34.1 %collective-permute-start.5 = (bf16[128,2048]{1,0:T(8,128)(2,1)}, bf16[128,2048]{1,0:T(8,128)(2,1)}, u32[]{:S(2)}, u32[]{:S(2)}) collective-permute-start(bf16[128,2048]{1,0:T(8,128)(2,1)} %get-tuple-element.22), channel_id=1, source_target_pairs={{0,24},{8,16},{16,8},{24,0},{1,25},{9,17},{17,9},{25,1},{2,26},{10... | collective-permute-start | bytes 1572872 | tf_op jit(solution)/shard_map/ppermute | solution.py:332
  90.2 0.8 copy-start.3
  90.2 4.3 %copy-start.4 = (bf16[128,2048]{1,0:T(8,128)(2,1)}, bf16[128,2048]{1,0:T(8,128)(2,1)S(1)}, u32[]{:S(2)}) copy-start(bf16[128,2048]{1,0:T(8,128)(2,1)S(1)} %collective-permute-done.4) | copy-start | bytes 1572868
  94.6 1.5 collective-permute-start.6
  96.1 7.1 %collective-permute-start.7 = (f32[24,2048]{1,0:T(8,128)S(1)}, f32[24,2048]{1,0:T(8,128)S(1)}, u32[]{:S(2)}, u32[]{:S(2)}) collective-permute-start(f32[24,2048]{1,0:T(8,128)S(1)} %add.151), channel_id=1, source_target_pairs={{0,8},{8,0},{16,24},{24,16},{1,9},{9,1},{17,25},{25,17},{2,10},{10... | collective-permute-start | bytes 589832 | tf_op jit(solution)/shard_map/ppermute | solution.py:318
  103.2 6.4 %collective-permute-start.8 = (f32[24,2048]{1,0:T(8,128)S(1)}, f32[24,2048]{1,0:T(8,128)S(1)}, u32[]{:S(2)}, u32[]{:S(2)}) collective-permute-start(f32[24,2048]{1,0:T(8,128)S(1)} %add.152), channel_id=1, source_target_pairs={{0,16},{8,24},{16,0},{24,8},{1,17},{9,25},{17,1},{25,9},{2,18},{10... | collective-permute-start | bytes 589832 | tf_op jit(solution)/shard_map/ppermute | solution.py:318
  109.7 13.2 %collective-permute-start.10 = (bf16[24,2048]{1,0:T(8,128)(2,1)S(1)}, bf16[24,2048]{1,0:T(8,128)(2,1)S(1)}, u32[]{:S(2)}, u32[]{:S(2)}) collective-permute-start(bf16[24,2048]{1,0:T(8,128)(2,1)S(1)} %get-tuple-element.17), channel_id=1, source_target_pairs={{0,4},{1,5},{2,6},{3,7},{4,0},{5,1},{6,2},{7,3},{8,12},{9,13},{10,... | collective-permute-start | bytes 294920 | tf_op jit(solution)/shard_map/ppermute | solution.py:325
  111.0 11.9 %collective-permute-start.11 = (bf16[24,2048]{1,0:T(8,128)(2,1)S(1)}, bf16[24,2048]{1,0:T(8,128)(2,1)S(1)}, u32[]{:S(2)}, u32[]{:S(2)}) collective-permute-start(bf16[24,2048]{1,0:T(8,128)(2,1)S(1)} %get-tuple-element.17), channel_id=1, source_target_pairs={{0,6},{1,7},{2,4},{3,5},{4,2},{5,3},{6,0},{7,1},{8,14},{9,15},{10,... | collective-permute-start | bytes 294920 | tf_op jit(solution)/shard_map/ppermute | solution.py:325
  112.2 11.9 %collective-permute-start.9 = (bf16[24,2048]{1,0:T(8,128)(2,1)S(1)}, bf16[24,2048]{1,0:T(8,128)(2,1)S(1)}, u32[]{:S(2)}, u32[]{:S(2)}) collective-permute-start(bf16[24,2048]{1,0:T(8,128)(2,1)S(1)} %get-tuple-element.17), channel_id=1, source_target_pairs={{0,2},{1,3},{2,0},{3,1},{4,6},{5,7},{6,4},{7,5},{8,10},{9,11},{10,... | collective-permute-start | bytes 294920 | tf_op jit(solution)/shard_map/ppermute | solution.py:325
  124.3 24.0 %copy-start.1 = (bf16[352,2048]{1,0:T(8,128)(2,1)S(1)}, bf16[352,2048]{1,0:T(8,128)(2,1)}, u32[]{:S(2)}) copy-start(bf16[352,2048]{1,0:T(8,128)(2,1)} %param.28) | copy-start | bytes 4325380
  129.2 3.6 %collective-permute-start.12 = (f32[24,1]{0,1:T(1,128)S(1)}, f32[24,1]{0,1:T(1,128)S(1)}, u32[]{:S(2)}, u32[]{:S(2)}) collective-permute-start(f32[24,1]{0,1:T(1,128)S(1)} %bitcast.41), channel_id=1, source_target_pairs={{0,8},{8,0},{16,24},{24,16},{1,9},{9,1},{17,25},{25,17},{2,10},{10... | collective-permute-start | bytes 296 | tf_op jit(solution)/shard_map/ppermute | solution.py:318
  132.8 3.5 %collective-permute-start.13 = (f32[24,1]{0,1:T(1,128)S(1)}, f32[24,1]{0,1:T(1,128)S(1)}, u32[]{:S(2)}, u32[]{:S(2)}) collective-permute-start(f32[24,1]{0,1:T(1,128)S(1)} %bitcast_maximum_fusion), channel_id=1, source_target_pairs={{0,16},{8,24},{16,0},{24,8},{1,17},{9,25},{17,1},{25,9},{2,18},{10... | collective-permute-start | bytes 296 | tf_op jit(solution)/shard_map/ppermute | solution.py:318
Sparse Core Ops, SparseCore 0:
  9.7 52.2 all-gather.1
  90.4 55.1 reduce-scatter.1

commit v3 on v0

--- a/solution.py
+++ b/solution.py
@@ -1,6 +1,10 @@
+import functools
+
 import jax
 import jax.numpy as jnp
 from jax import lax
+from jax.experimental import pallas as pl
+from jax.experimental.pallas import tpu as pltpu
 from jax.sharding import PartitionSpec as P
 
 CAP = 32
@@ -144,6 +148,497 @@
     return (sublayer_out, last_norm, block_logit[:, None])
 
 
+AHEAD = 3
+RANK = 16
+
+
+def scaled_rows(tokens, gain):
+    values = tokens.astype(jnp.float32)
+    scaled = lax.rsqrt(jnp.mean(values * values, axis=-1, keepdims=True) + 1e-06)
+    return (values * scaled * gain).astype(jnp.bfloat16)
+
+
+def prep_kernel(
+    tok_ref, twin_ref, gain_ref, routes_ref, twin_routes_ref, gates_ref, twin_gates_ref, *outs
+):
+    first_ref, second_ref, whole_ref = outs
+    rows, width = tok_ref.shape
+    half = width // 2
+    experts = 32
+    row = lax.broadcasted_iota(jnp.int32, (rows, rows), 0)
+    column = lax.broadcasted_iota(jnp.int32, (rows, rows), 1)
+    upto = jnp.where(row <= column, 1.0, 0.0).astype(jnp.bfloat16)
+    numbers = lax.broadcasted_iota(jnp.int32, (experts, rows), 0)
+    gain = gain_ref[...].astype(jnp.float32)[None, :]
+    own = (tok_ref, routes_ref, gates_ref)
+    twin = (twin_ref, twin_routes_ref, twin_gates_ref)
+    for c, (tokens, routes, gates) in enumerate((own, twin)):
+        at = c * rows
+        normed = scaled_rows(tokens[...], gain)
+        if c == 0:
+            whole_ref[...] = normed
+        first_ref[at : at + rows, :half] = normed[:, :half]
+        second_ref[at : at + rows, :] = normed[:, half:]
+        chosen = jnp.zeros((experts, rows), jnp.float32)
+        weight = jnp.zeros((experts, rows), jnp.float32)
+        for k in range(routes.shape[0]):
+            hit = routes[k : k + 1, :] == numbers
+            chosen = jnp.where(hit, 1.0, chosen)
+            weight = jnp.where(hit, gates[k : k + 1, :].astype(jnp.float32), weight)
+        count = jnp.dot(chosen.astype(jnp.bfloat16), upto, preferred_element_type=jnp.float32)
+        place = jnp.where(chosen > 0.5, count - 1.0, -1.0)
+        first_ref[at : at + experts, half:] = place.astype(jnp.bfloat16)
+        first_ref[at + experts : at + 2 * experts, half:] = weight.astype(jnp.bfloat16)
+        first_ref[at + 2 * experts : at + rows, half:] = jnp.zeros(
+            (rows - 2 * experts, rows), jnp.bfloat16
+        )
+
+
+def prepare(tokens, twin, norm_gain, routes, twin_routes, gates, twin_gates):
+    rows, width = tokens.shape
+    half = width // 2
+    return pl.pallas_call(
+        prep_kernel,
+        out_shape=(
+            jax.ShapeDtypeStruct((2 * rows, half + rows), jnp.bfloat16),
+            jax.ShapeDtypeStruct((2 * rows, half), jnp.bfloat16),
+            jax.ShapeDtypeStruct((rows, width), jnp.bfloat16),
+        ),
+        name="prepare",
+    )(tokens, twin, norm_gain, routes, twin_routes, gates, twin_gates)
+
+
+def across_columns(left, right):
+    return lax.dot_general(left, right, (((1,), (1,)), ((), ())), preferred_element_type=jnp.float32)
+
+
+def experts_kernel(ahead, chips, count, position_ref, last_ref, slots_ref, peer_last_ref, *refs):
+    arrivals = 2 * chips - 1
+    shared_hbm, peers_hbm, refs = refs[:5], refs[5 : 6 + count], refs[6 + count :]
+    left_hbm, right_hbm, refs = refs[:arrivals], refs[arrivals : 2 * arrivals], refs[2 * arrivals :]
+    gate_hbm, up_hbm, down_hbm, refs = *refs[:3], refs[3:]
+    left_out, right_out, last_out = refs[:chips], refs[chips : 2 * chips], refs[2 * chips]
+    parts_hbm, refs = refs[2 * chips + 1 : 2 * chips + 2 + count], refs[2 * chips + 2 + count :]
+    left, right, gates, ups, downs, held, mix, incoming, outs, result = refs[:10]
+    left_sem, right_sem, gate_sem, up_sem, down_sem, left_out_sem, right_out_sem = refs[10:17]
+    shared_sem, peer_sem, part_sem = refs[17:]
+    experts, width, hidden = gate_hbm.shape
+    rows = left.shape[1] // 2
+    half = width // 2
+    numbered = held.shape[0]
+    first = position_ref[0] * experts
+
+    def load(hbm, buffer, sem, e):
+        return pltpu.make_async_copy(hbm.at[e], buffer.at[e % 2], sem.at[e % 2])
+
+    sides = ((left_hbm, left, left_sem), (right_hbm, right, right_sem))
+
+    def fetch(side, d):
+        hbm, buffer, sem = side
+        return pltpu.make_async_copy(hbm[d], buffer.at[d], sem.at[d])
+
+    def fetch_swapped(side, d):
+        hbm, buffer, sem = side
+        for c in range(2):
+            pltpu.make_async_copy(
+                hbm[arrivals - d].at[pl.ds((1 - c) * rows, rows)],
+                buffer.at[d, pl.ds(c * rows, rows)],
+                sem.at[d],
+            ).start()
+
+    chip, core = lax.div(position_ref[0], 2), lax.rem(position_ref[0], 2)
+    for d in range(chips):
+        near = (core == 0) & (chip >= d) | (core == 1) & (chip + d < chips)
+        for side in sides:
+            if d == 0:
+                fetch(side, d).start()
+            else:
+                pl.when(near)(lambda: fetch(side, d).start())
+                pl.when(jnp.logical_not(near))(lambda: fetch_swapped(side, d))
+    gate_in = [load(gate_hbm, gates, gate_sem, e) for e in range(experts)]
+    up_in = [load(up_hbm, ups, up_sem, e) for e in range(experts)]
+    down_in = [load(down_hbm, downs, down_sem, e) for e in range(experts)]
+    order = [copy for e in range(experts) for copy in (gate_in[e], up_in[e], down_in[e])]
+    for copy in order[:ahead]:
+        copy.start()
+
+    def arrived(i):
+        order[i].wait()
+        if i + ahead < len(order):
+            order[i + ahead].start()
+
+    per = incoming.shape[1] // rows
+    peer_in = []
+    for p in range(count + 1):
+        q = min(p, count - 1)
+        to = incoming.at[q // per, pl.ds(q % per * rows, rows)]
+        if p >= count - 1:
+            to = to.at[:, pl.ds((p - count + 1) * half, half)]
+        peer_in.append(pltpu.make_async_copy(peers_hbm[p], to, peer_sem.at[p]))
+    begins = [0]
+    for hbm in shared_hbm:
+        begins.append(begins[-1] + hbm.shape[0])
+    shared_in = [
+        pltpu.make_async_copy(
+            hbm, downs.at[0, pl.ds(begin, hbm.shape[0])], shared_sem.at[i]
+        )
+        for i, (hbm, begin) in enumerate(zip(shared_hbm, begins))
+    ]
+    slots = lax.broadcasted_iota(jnp.int32, (CAP, rows), 0).astype(jnp.float32)
+    for d in range(chips):
+        for side in sides:
+            fetch(side, d).wait()
+        for c in range(2):
+            s = 2 * d + c
+            own = pl.ds(c * rows, rows)
+            held[...] = left[d, pl.ds(c * rows, numbered), half:].astype(jnp.float32)
+            picks = []
+            for e in range(experts):
+                place = held[pl.ds(first + e, 1), :]
+                weight = held[pl.ds(first + numbered // 2 + e, 1), :]
+                hit = place == slots
+                picks.append(jnp.where(hit, 1.0, 0.0))
+                mix[s, e * CAP : (e + 1) * CAP, :] = jnp.where(hit, weight, 0.0).astype(
+                    jnp.bfloat16
+                )
+            pick = jnp.concatenate(picks, axis=0).astype(jnp.bfloat16)
+            for ref, to in ((left, 0), (right, half)):
+                chosen = jnp.dot(pick, ref[d, own, :half], preferred_element_type=jnp.float32)
+                chosen = chosen.astype(jnp.bfloat16)
+                for e in range(experts):
+                    incoming[e, s * CAP : (s + 1) * CAP, to : to + half] = chosen[
+                        e * CAP : (e + 1) * CAP
+                    ]
+    for e in range(experts):
+        inputs = incoming[e]
+        arrived(3 * e)
+        gate = jnp.dot(inputs, gates[e % 2], preferred_element_type=jnp.float32)
+        arrived(3 * e + 1)
+        up = jnp.dot(inputs, ups[e % 2], preferred_element_type=jnp.float32)
+        mid = (gate / (1.0 + jnp.exp(-gate)) * up).astype(jnp.bfloat16)
+        arrived(3 * e + 2)
+        out = jnp.dot(mid, downs[e % 2], preferred_element_type=jnp.float32).astype(jnp.bfloat16)
+        for s in range(2 * chips):
+            outs[s, e * CAP : (e + 1) * CAP, :] = out[s * CAP : (s + 1) * CAP]
+        if e == experts - 2:
+            for copy in peer_in + shared_in:
+                copy.start()
+    sent = []
+    for d in range(chips):
+        for c in range(2):
+            result[d, c * rows : (c + 1) * rows, :] = lax.dot_general(
+                mix[2 * d + c],
+                outs[2 * d + c],
+                (((0,), (0,)), ((), ())),
+                preferred_element_type=jnp.float32,
+            ).astype(jnp.bfloat16)
+        sent.append(
+            pltpu.make_async_copy(result.at[d, :, :half], left_out[d], left_out_sem.at[d])
+        )
+        sent.append(
+            pltpu.make_async_copy(result.at[d, :, half:], right_out[d], right_out_sem.at[d])
+        )
+        sent[-2].start()
+        sent[-1].start()
+    for copy in peer_in + shared_in:
+        copy.wait()
+    gate_ref, up_ref, down_ref, lower_ref, upper_ref = [
+        downs.at[0, pl.ds(begin, hbm.shape[0])] for hbm, begin in zip(shared_hbm, begins)
+    ]
+    batch = incoming.shape[1]
+    at = lax.broadcasted_iota(jnp.int32, (last_ref.shape[0], batch), 1)
+    last = None
+    for b in range(count // per):
+        inputs = incoming[b]
+        gate = across_columns(inputs, gate_ref[...])
+        up = across_columns(inputs, up_ref[...])
+        mid = (gate / (1.0 + jnp.exp(-gate)) * up).astype(jnp.bfloat16)
+        low = across_columns(inputs, lower_ref[...])
+        slot = slots_ref[b * batch : (b + 1) * batch, :]
+        place = lax.broadcasted_iota(jnp.int32, low.shape, 1) - slot * RANK
+        low = jnp.where((place >= 0) & (place < RANK), low, 0.0).astype(jnp.bfloat16)
+        part = jnp.dot(mid, down_ref[...], preferred_element_type=jnp.float32)
+        part = part + jnp.dot(low, upper_ref[...], preferred_element_type=jnp.float32)
+        part = part.astype(jnp.bfloat16)
+        store = experts - count // per + b
+        incoming[store] = part
+        for c in range(per):
+            p = per * b + c
+            value = incoming.at[store, pl.ds(c * rows, rows)]
+            values = [value]
+            if p == count - 1:
+                values = [value.at[:, pl.ds(0, half)], value.at[:, pl.ds(half, half)]]
+            for i, value in enumerate(values):
+                sent.append(pltpu.make_async_copy(value, parts_hbm[p + i], part_sem.at[p + i]))
+                sent[-1].start()
+        pick = jnp.where(peer_last_ref[...] - b * batch == at, 1.0, 0.0).astype(jnp.bfloat16)
+        term = jnp.dot(pick, part, preferred_element_type=jnp.float32)
+        last = term if last is None else last + term
+    at = lax.broadcasted_iota(jnp.int32, (last_ref.shape[0], 2 * rows), 1)
+    for d in range(chips):
+        pick = jnp.where(last_ref[...] - d * 2 * rows == at, 1.0, 0.0).astype(jnp.bfloat16)
+        last = last + jnp.dot(pick, result[d], preferred_element_type=jnp.float32)
+    last_out[...] = last[: last_out.shape[0]]
+    for copy in sent:
+        copy.wait()
+
+
+def run_experts(
+    position, last_at, slots_at, peer_last, shared, peers, left, right, gate, up, down, requests
+):
+    experts, width, hidden = gate.shape
+    arrivals = len(left)
+    count = len(peers) - 1
+    chips = (arrivals + 1) // 2
+    both = left[0].shape[0]
+    rows = both // 2
+    half = width // 2
+    slots = 2 * chips * CAP
+    anywhere = pl.BlockSpec(memory_space=pltpu.MemorySpace.HBM)
+    inside = pl.BlockSpec(memory_space=pltpu.VMEM)
+    passed = jax.ShapeDtypeStruct((both, half), jnp.bfloat16)
+    return pl.pallas_call(
+        functools.partial(experts_kernel, AHEAD, chips, count),
+        in_specs=[pl.BlockSpec(memory_space=pltpu.SMEM)]
+        + [inside] * 3
+        + [anywhere] * (6 + count + 2 * arrivals + 3),
+        out_specs=[anywhere] * (2 * chips) + [inside] + [anywhere] * (count + 1),
+        out_shape=[passed] * (2 * chips)
+        + [jax.ShapeDtypeStruct((requests, width), jnp.float32)]
+        + [jax.ShapeDtypeStruct((rows, width), jnp.bfloat16)] * (count - 1)
+        + [jax.ShapeDtypeStruct((rows, half), jnp.bfloat16)] * 2,
+        scratch_shapes=[
+            pltpu.VMEM((chips, both, half + rows), jnp.bfloat16),
+            pltpu.VMEM((chips, both, half), jnp.bfloat16),
+            pltpu.VMEM((2, width, hidden), jnp.bfloat16),
+            pltpu.VMEM((2, width, hidden), jnp.bfloat16),
+            pltpu.VMEM((2, hidden, width), jnp.bfloat16),
+            pltpu.VMEM((64, rows), jnp.float32),
+            pltpu.VMEM((2 * chips, experts * CAP, rows), jnp.bfloat16),
+            pltpu.VMEM((experts, slots, width), jnp.bfloat16),
+            pltpu.VMEM((2 * chips, experts * CAP, width), jnp.bfloat16),
+            pltpu.VMEM((chips, both, width), jnp.bfloat16),
+            pltpu.SemaphoreType.DMA((chips,)),
+            pltpu.SemaphoreType.DMA((chips,)),
+            pltpu.SemaphoreType.DMA((2,)),
+            pltpu.SemaphoreType.DMA((2,)),
+            pltpu.SemaphoreType.DMA((2,)),
+            pltpu.SemaphoreType.DMA((chips,)),
+            pltpu.SemaphoreType.DMA((chips,)),
+            pltpu.SemaphoreType.DMA((5,)),
+            pltpu.SemaphoreType.DMA((count + 1,)),
+            pltpu.SemaphoreType.DMA((count + 1,)),
+        ],
+        compiler_params=pltpu.CompilerParams(vmem_limit_bytes=60 << 20),
+        cost_estimate=pl.CostEstimate(
+            flops=6 * experts * slots * width * hidden,
+            bytes_accessed=6 * experts * width * hidden,
+            transcendentals=experts * slots * hidden,
+        ),
+        name="run_experts",
+    )(position, last_at, slots_at, peer_last, *shared, *peers, *left, *right, gate, up, down)
+
+
+def add(*terms):
+    total = terms[0].astype(jnp.float32)
+    for term in terms[1:]:
+        total = total + term.astype(jnp.float32)
+    return total.astype(jnp.bfloat16)
+
+
+def swapped(value):
+    rows = value.shape[0] // 2
+    return jnp.concatenate([value[rows:], value[:rows]])
+
+
+def twin_of(value, tensor_size):
+    return lax.ppermute(value, "tensor", [(i, i ^ 1) for i in range(tensor_size)])
+
+
+def along(value, chips, distance, begin=0, end=None):
+    end = chips - distance if end is None else end
+    upward = [(2 * z, 2 * (z + distance)) for z in range(begin, end)]
+    downward = [
+        (2 * (chips - 1 - z) + 1, 2 * (chips - 1 - z - distance) + 1) for z in range(begin, end)
+    ]
+    return lax.ppermute(value, "tensor", upward + downward)
+
+
+def spread(chunks, chips):
+    groups = [[chunk] for chunk in chunks]
+    for k in range(1, chips):
+        for group in groups:
+            group.append(along(group[-1], chips, 1, k - 1))
+    return groups
+
+
+def collect(parts, chips, begin):
+    run = [None] * len(parts)
+    rows = parts[0][0].shape[0]
+    for k in range(1, chips):
+        for j, part in enumerate(parts):
+            got = swapped(twin_of(part[chips - k], 2 * chips))
+            terms = (part[k], got) if run[j] is None else (part[k], got, run[j][:rows])
+            sent = add(*terms)
+            if k == 1 and j == 0:
+                carried, came = begin(sent)
+                carry = carried
+            if k == chips - 1 and j == len(parts) - 1:
+                sent, *came = lax.optimization_barrier((sent, *came))
+            if j == len(parts) - 1:
+                if k > 1:
+                    carry = add(carried, run[j][rows:])
+                sent = jnp.concatenate([sent, carry])
+            run[j] = along(sent, chips, 1, 0, k)
+    done = []
+    for j, part in enumerate(parts):
+        total = add(part[0], run[j][:rows])
+        own, other = total[: rows // 2], total[rows // 2 :]
+        if j == len(parts) - 1:
+            other = jnp.concatenate([other, run[j][rows:]])
+        got = twin_of(other, 2 * chips)
+        done.append((own, got[: rows // 2]))
+    return done, came, [carried, run[-1][rows:], got[rows // 2 :]]
+
+
+def across(value, combine, axis, size):
+    step = 1
+    while step < size:
+        pairs = [(i, i ^ step) for i in range(lax.axis_size(axis))]
+        value = combine(value, lax.ppermute(value, axis, pairs))
+        step *= 2
+    return value
+
+
+def sent_along(value, axis, steps, size):
+    return [lax.ppermute(value, axis, [(i, i ^ step) for i in range(size)]) for step in steps]
+
+
+def after(values, other):
+    *values, _ = lax.optimization_barrier((*values, other))
+    return values
+
+
+def summed(values):
+    result = values[0].astype(jnp.float32)
+    for value in values[1:]:
+        result = result + value.astype(jnp.float32)
+    return result
+
+
+def from_peer(value, step, size):
+    return lax.ppermute(value, "dp", [(i, i ^ step) for i in range(size)])
+
+
+def local_line(
+    tokens,
+    norm_gain,
+    routes,
+    route_gates,
+    lengths,
+    request_adapter,
+    adapter_slot,
+    expert_gate,
+    expert_up,
+    expert_down,
+    shared_gate,
+    shared_up_weight,
+    shared_down,
+    adapter_down,
+    adapter_up,
+    head_weight,
+):
+    tok_rows, width = tokens.shape
+    tensor_size = lax.axis_size("tensor")
+    data_size = lax.axis_size("dp")
+    tensor_pos = lax.axis_index("tensor")
+    data_pos = lax.axis_index("dp")
+    chips = tensor_size // 2
+    small = (routes.T, route_gates.T)
+    own = (tokens, *small)
+    twin = [twin_of(value, tensor_size) for value in own]
+    first, second, normed = prepare(
+        tokens, twin[0], norm_gain, small[0], twin[1], small[1], twin[2]
+    )
+    left, right = spread([first, second], chips)
+    near = [from_peer(normed, d, data_size) for d in (1, 2)]
+    peers = [
+        normed,
+        *near,
+        from_peer(near[1][:, : width // 2], 1, data_size),
+        from_peer(near[0][:, width // 2 :], 2, data_size),
+    ]
+    block_rows = jnp.arange(tok_rows, dtype=jnp.int32)
+    peer_dp = jnp.arange(data_size, dtype=jnp.int32) ^ data_pos
+    bases = (peer_dp * tensor_size + tensor_pos) * tok_rows
+    peer_positions = (bases[:, None] + block_rows[None, :]).reshape(-1)
+    peer_slots = token_slots(peer_positions, lengths, request_adapter, adapter_slot)
+    held_count, _, rank = adapter_down.shape
+    held_slots = (peer_slots - data_pos * held_count)[:, None]
+    lower = jnp.transpose(adapter_down, (0, 2, 1)).reshape(held_count * rank, width)
+    upper = adapter_up.reshape(held_count * rank, width)
+    ends = jnp.cumsum(lengths) - 1
+    owner, row = ends // tok_rows, ends % tok_rows
+    owner_dp, owner_tensor = owner // tensor_size, owner % tensor_size
+    requests = ends.shape[0]
+    chip, core = tensor_pos // 2, tensor_pos % 2
+    steps = jnp.where(core == 0, chip - owner_tensor // 2, owner_tensor // 2 - chip) % chips
+    away = (2 * steps + (owner_tensor % 2 != core)) * tok_rows + row
+    line_at = jnp.where(owner_dp == data_pos, away, -1)
+    across_at = (owner_dp ^ data_pos) * tok_rows + row
+    peer_at = jnp.where(owner_tensor == tensor_pos, across_at, -1)
+    padding = ((0, -requests % 16), (0, 0))
+    line_at = jnp.pad(line_at[:, None], padding, constant_values=-1)
+    peer_at = jnp.pad(peer_at[:, None], padding, constant_values=-1)
+    early = after(left[1:-1] + right[1:-1], right[-2])
+    early = [early[: chips - 2], early[chips - 2 :]]
+    left = left + [twin_of(part, tensor_size) for part in early[0] + left[-1:]]
+    right = right + [twin_of(part, tensor_size) for part in early[1] + right[-1:]]
+    results = run_experts(
+        tensor_pos.astype(jnp.int32).reshape(1),
+        line_at,
+        held_slots,
+        peer_at,
+        [shared_gate.T, shared_up_weight.T, shared_down, lower, upper],
+        peers,
+        left,
+        right,
+        expert_gate,
+        expert_up,
+        expert_down,
+        requests,
+    )
+    passed, last, parts = results[: 2 * chips], results[2 * chips], results[2 * chips + 1 :]
+    half = width // 2
+
+    def begin(ready):
+        value, *tied = after([last, *parts], ready)
+        value = across(value, jnp.add, "tensor", 2)
+        sent = value.astype(jnp.bfloat16)
+        value = summed([value] + sent_along(sent, "dp", range(1, data_size), data_size))
+        far = [from_peer(tied[3], 1, data_size), from_peer(tied[4], 2, data_size)]
+        joined = [
+            jnp.concatenate([tied[1][:, :half], add(tied[1][:, half:], far[1])], axis=1),
+            jnp.concatenate([add(tied[2][:, :half], far[0]), tied[2][:, half:]], axis=1),
+        ]
+        came = [from_peer(joined[0], 1, data_size), from_peer(joined[1], 2, data_size)]
+        value = value.astype(jnp.bfloat16)
+        return jnp.concatenate([value[:, :half], value[:, half:]]), came
+
+    routed, came, carried = collect([passed[:chips], passed[chips:]], chips, begin)
+    last = summed(carried)
+    last = jnp.concatenate([last[:requests], last[requests:]], axis=1).astype(jnp.bfloat16)
+    last_values = last.astype(jnp.float32)
+    last_norm = jnp.sqrt(jnp.sum(last_values * last_values, axis=1))
+    logits = jnp.dot(last, head_weight, preferred_element_type=jnp.float32)
+    top = jnp.max(logits, axis=1, keepdims=True)
+    tops = [top] + sent_along(top, "dp", range(1, data_size), data_size)
+    block_logit = functools.reduce(jnp.maximum, tops)
+    out = jnp.concatenate([a.astype(jnp.float32) + b.astype(jnp.float32) for a, b in routed], axis=1)
+    out = out + summed([parts[0], *came])
+    return (out.astype(jnp.bfloat16), last_norm, block_logit)
+
+
 def solution(mesh):
     placed = (
         P(("dp", "tensor"), None),
@@ -163,8 +658,9 @@
         P("dp", None, None),
         P(None, ("dp", "tensor")),
     )
+    short = mesh.shape["tensor"] == 8 and mesh.shape["dp"] == 4
     return jax.shard_map(
-        local,
+        local_line if short else local,
         mesh=mesh,
         in_specs=placed,
         out_specs=(P(("dp", "tensor"), None), P(), P(None, "tensor")),

time: 400 us -> 152 us (0.38)
  waiting for transfers between devices: 253 us -> 44.6 us
  matrix products: 69.5 us -> 1.31 us
  starting transfers between devices: 5.19 us -> 55.1 us
  Pallas kernels: 0 us -> 39.5 us
  other arithmetic: 28.3 us -> 4.71 us
  blocking collectives: 23.3 us -> 0 us
  between operations: 14.4 us -> 1.36 us
    psum x1 -> x0, waiting for transfers between devices: 122 us -> none  [local(): last_states = lax.psum(last_part, ('dp', 'tensor'))]
    all_to_all x1 -> x0, waiting for transfers between devices: 91 us -> none  [local(): lax.all_to_all(expert_out, 'tensor', split_axis=0, concat_axis=0, tiled=T...]
    dot_general x10 -> x1, matrix products: 69.5 us -> 1.31 us  [local_line(): logits = jnp.dot(last, head_weight, preferred_element_type=jnp.float32)]
    ppermute x0 -> x44, starting transfers between devices: none -> 55.1 us  [the longest x12 29.9 us: along(): return lax.ppermute(value, 'tensor', upward + downward)]
    ppermute x0 -> x44, waiting for transfers between devices: none -> 44.6 us  [the longest x12 18.6 us: along(): return lax.ppermute(value, 'tensor', upward + downward)]
    pallas_call x0 -> x2, Pallas kernels: none -> 39.5 us  [the longest x1 36.7 us: run_experts(): pl.pallas_call(functools.partial(experts_kernel, AHEAD, chips, count), in...]
    all_gather x4 -> x0, waiting for transfers between devices: 39 us -> none  [the longest x1 37.4 us: local(): peer_rows = lax.all_gather(normed, 'dp', axis=0, tiled=True)]
    another operation x4 -> x2, other arithmetic: 23.7 us -> 0.09 us  [the longest x1 23.4 us: local(): source_place = jnp.cumsum(source_chosen.astype(jnp.int32), axis=1) - 1]
  transfers between devices with their start and end apart: 7 -> 44, of which waited for: 4 -> 21; matrix products, arithmetic and copies ran while one was open for 22% -> 5% of each run, Pallas kernels for 0% -> 0%
where the time goes in v3:
time: 152 us
  starting transfers between devices  55.1 us (36%)
  waiting for transfers between devices  44.6 us (29%)
  Pallas kernels  39.5 us (26%)
  local copies, waits for them, and re-layouts  5.33 us (4%)
  other arithmetic  4.71 us (3%)
    pallas_call x1, Pallas kernels, run_experts(): pl.pallas_call(functools.partial(experts_kernel, AHEAD, chips, count), in...  36.7 us
    ppermute x12, starting transfers between devices, along(): return lax.ppermute(value, 'tensor', upward + downward)  29.9 us
    ppermute x12, waiting for transfers between devices, along(): return lax.ppermute(value, 'tensor', upward + downward)  18.6 us
    ppermute x8, waiting for transfers between devices, from_peer(): return lax.ppermute(value, 'dp', [(i, i ^ step) for i in range(size)])  14.1 us
    ppermute x8, starting transfers between devices, from_peer(): return lax.ppermute(value, 'dp', [(i, i ^ step) for i in range(size)])  12.3 us
    ppermute x6, starting transfers between devices, sent_along(): lax.ppermute(value, axis, [(i, i ^ step) for i in range(size)])  7.11 us
    ppermute x6, waiting for transfers between devices, sent_along(): lax.ppermute(value, axis, [(i, i ^ step) for i in range(size)])  6.79 us
    ppermute x17, starting transfers between devices, twin_of(): lax.ppermute(value, 'tensor', [(i, i ^ 1) for i in range(tensor_size)])  5.6 us
  transfers between devices with their start and end apart: 44, of which 21 were waited for; matrix products, arithmetic and copies ran while one was open for 5% of the time, Pallas kernels for 0%

profile of v3, /device:TPU:0, one launch (start us, length us, event | category | flops | bytes accessed | tf_op | source)
XLA Modules:
  0.0 152.0 jit_solution(18261295819258881210)
XLA Ops:
  4.3 2.9 %prepare.1 = (bf16[256,1152]{1,0:T(8,128)(2,1)}, bf16[256,1024]{1,0:T(8,128)(2,1)}, bf16[128,2048]{1,0:T(8,128)(2,1)}) custom-call(bf16[128,2048]{1,0:T(8,128)(2,1)} %tok_ref.1, bf16[128,2048]{1,0:T(8,128)(2,1)} %copy-done.12, bf16[2048]{0:T(1024)(128)(2,1)} %gain_ref.1, s32[6,128]{1,0:T(8,128)} %bitcast.24, s32[6,128]{1,0:T(8,128)} %copy-done.19, ...), custom_call_target="tpu_custom_call" | custom-call | tf_op jit(solution)/shard_map/prepare/pallas_call | solution.py:200
  7.2 4.9 %collective-permute-start.7 = (bf16[256,1152]{1,0:T(8,128)(2,1)}, bf16[256,1152]{1,0:T(8,128)(2,1)S(1)}, u32[]{:S(2)}, u32[]{:S(2)}) collective-permute-start(bf16[256,1152]{1,0:T(8,128)(2,1)} %get-tuple-element.33.refs_10_), channel_id=1, source_target_pairs={{0,2},{2,4},{4,6},{7,5},{5,3},{3,1},{8,10},{10,12},{12,14},{15,13}... | collective-permute-start | bytes 1769480 | tf_op jit(solution)/shard_map/ppermute | solution.py:464
  12.1 4.3 %collective-permute-start.10 = (bf16[256,1024]{1,0:T(8,128)(2,1)}, bf16[256,1024]{1,0:T(8,128)(2,1)}, u32[]{:S(2)}, u32[]{:S(2)}) collective-permute-start(bf16[256,1024]{1,0:T(8,128)(2,1)} %get-tuple-element.34.refs_17_), channel_id=1, source_target_pairs={{0,2},{2,4},{4,6},{7,5},{5,3},{3,1},{8,10},{10,12},{12,14},{15,13}... | collective-permute-start | bytes 1572872 | tf_op jit(solution)/shard_map/ppermute | solution.py:464
  16.4 3.4 %collective-permute-done.7.refs_11_ = bf16[256,1152]{1,0:T(8,128)(2,1)S(1)} collective-permute-done((bf16[256,1152]{1,0:T(8,128)(2,1)}, bf16[256,1152]{1,0:T(8,128)(2,1)S(1)}, u32[]{:S(2)}, u32[]{:S(2)}) %collective-permute-start.7) | collective-permute-done | bytes 589856 | tf_op jit(solution)/shard_map/ppermute | solution.py:464
  20.5 1.6 %collective-permute-start.4 = (bf16[128,2048]{1,0:T(8,128)(2,1)}, bf16[128,2048]{1,0:T(8,128)(2,1)S(1)}, u32[]{:S(2)}, u32[]{:S(2)}) collective-permute-start(bf16[128,2048]{1,0:T(8,128)(2,1)} %get-tuple-element.32.refs_5_), channel_id=1, source_target_pairs={{0,16},{8,24},{16,0},{24,8},{1,17},{9,25},{17,1},{25,9},{2,18},{10... | collective-permute-start | bytes 1572872 | tf_op jit(solution)/shard_map/ppermute | solution.py:530
  22.1 1.5 collective-permute-start.3
  23.6 1.8 %collective-permute-done.10.refs_18_ = bf16[256,1024]{1,0:T(8,128)(2,1)} collective-permute-done((bf16[256,1024]{1,0:T(8,128)(2,1)}, bf16[256,1024]{1,0:T(8,128)(2,1)}, u32[]{:S(2)}, u32[]{:S(2)}) %collective-permute-start.10) | collective-permute-done | bytes 524320 | tf_op jit(solution)/shard_map/ppermute | solution.py:464
  27.5 7.2 %collective-permute-done.4.refs_7_ = bf16[128,2048]{1,0:T(8,128)(2,1)S(1)} collective-permute-done((bf16[128,2048]{1,0:T(8,128)(2,1)}, bf16[128,2048]{1,0:T(8,128)(2,1)S(1)}, u32[]{:S(2)}, u32[]{:S(2)}) %collective-permute-start.4) | collective-permute-done | bytes 524320 | tf_op jit(solution)/shard_map/ppermute | solution.py:530
  34.8 1.7 %collective-permute-start.5 = (bf16[128,1024]{1,0:T(8,128)(2,1)S(1)}, bf16[128,1024]{1,0:T(8,128)(2,1)}, u32[]{:S(2)}, u32[]{:S(2)}) collective-permute-start(bf16[128,1024]{1,0:T(8,128)(2,1)S(1)} %slice.139), channel_id=1, source_target_pairs={{0,8},{8,0},{16,24},{24,16},{1,9},{9,1},{17,25},{25,17},{2,10},{10... | collective-permute-start | bytes 786440 | tf_op jit(solution)/shard_map/ppermute | solution.py:530
  37.3 1.5 collective-permute-start.6
  38.8 1.5 collective-permute-start.15
  40.6 2.1 %collective-permute-done.5.refs_8_ = bf16[128,1024]{1,0:T(8,128)(2,1)} collective-permute-done((bf16[128,1024]{1,0:T(8,128)(2,1)S(1)}, bf16[128,1024]{1,0:T(8,128)(2,1)}, u32[]{:S(2)}, u32[]{:S(2)}) %collective-permute-start.5) | collective-permute-done | bytes 262176 | tf_op jit(solution)/shard_map/ppermute | solution.py:530
  42.7 2.5 %collective-permute-done.6.refs_9_ = bf16[128,1024]{1,0:T(8,128)(2,1)} collective-permute-done((bf16[128,1024]{1,0:T(8,128)(2,1)}, bf16[128,1024]{1,0:T(8,128)(2,1)}, u32[]{:S(2)}, u32[]{:S(2)}) %collective-permute-start.6) | collective-permute-done | bytes 262176 | tf_op jit(solution)/shard_map/ppermute | solution.py:530
  46.9 2.1 %collective-permute-start.17 = (bf16[256,1024]{1,0:T(8,128)(2,1)}, bf16[256,1024]{1,0:T(8,128)(2,1)}, u32[]{:S(2)}, u32[]{:S(2)}) collective-permute-start(bf16[256,1024]{1,0:T(8,128)(2,1)} %collective-permute-done.11.refs_19_), channel_id=1, source_target_pairs={{0,1},{1,0},{2,3},{3,2},{4,5},{5,4},{6,7},{7,6},{8,9},{9,8},{10,11... | collective-permute-start | bytes 1572872 | tf_op jit(solution)/shard_map/ppermute | solution.py:455
  51.7 36.7 %run_experts.1 = (bf16[256,1024]{1,0:T(8,128)(2,1)}, bf16[256,1024]{1,0:T(8,128)(2,1)}, bf16[256,1024]{1,0:T(8,128)(2,1)}, bf16[256,1024]{1,0:T(8,128)(2,1)}, bf...) custom-call(s32[1]{0:T(128)} %bitcast.position_ref, ...), custom_call_target="tpu_custom_call" | custom-call | flops 17716740096 | bytes 69206016 | tf_op jit(solution)/shard_map/run_experts/pallas_call | solution.py:400
  91.3 1.9 %collective-permute-start.22 = (bf16[256,1024]{1,0:T(8,128)(2,1)S(1)}, bf16[256,1024]{1,0:T(8,128)(2,1)S(1)}, u32[]{:S(2)}, u32[]{:S(2)}) collective-permute-start(bf16[256,1024]{1,0:T(8,128)(2,1)S(1)} %add_convert_fusion.7), channel_id=1, source_target_pairs={{0,2},{7,5},{8,10},{15,13},{16,18},{23,21},{24,26},{31,29}} | collective-permute-start | bytes 1572872 | tf_op jit(solution)/shard_map/ppermute | solution.py:464
  93.4 1.6 %collective-permute-start.35 = (bf16[128,1024]{1,0:T(8,128)(2,1)S(1)}, bf16[128,1024]{1,0:T(8,128)(2,1)S(1)}, u32[]{:S(2)}, u32[]{:S(2)}) collective-permute-start(bf16[128,1024]{1,0:T(8,128)(2,1)S(1)} %copy-done.24), channel_id=1, source_target_pairs={{0,16},{8,24},{16,0},{24,8},{1,17},{9,25},{17,1},{25,9},{2,18},{10... | collective-permute-start | bytes 786440 | tf_op jit(solution)/shard_map/ppermute | solution.py:530
  95.4 1.9 %collective-permute-start.32 = (bf16[24,2048]{1,0:T(8,128)(2,1)S(1)}, bf16[24,2048]{1,0:T(8,128)(2,1)S(1)}, u32[]{:S(2)}, u32[]{:S(2)}) collective-permute-start(bf16[24,2048]{1,0:T(8,128)(2,1)S(1)} %get-tuple-element.61), channel_id=1, source_target_pairs={{0,24},{8,16},{16,8},{24,0},{1,25},{9,17},{17,9},{25,1},{2,26},{10... | collective-permute-start | bytes 294920 | tf_op jit(solution)/shard_map/ppermute | solution.py:514
  99.1 2.6 %collective-permute-done.32 = bf16[24,2048]{1,0:T(8,128)(2,1)S(1)} collective-permute-done((bf16[24,2048]{1,0:T(8,128)(2,1)S(1)}, bf16[24,2048]{1,0:T(8,128)(2,1)S(1)}, u32[]{:S(2)}, u32[]{:S(2)}) %collective-permute-start.32) | collective-permute-done | bytes 98336 | tf_op jit(solution)/shard_map/ppermute | solution.py:514
  101.7 1.9 %collective-permute-start.37 = (bf16[128,1024]{1,0:T(8,128)(2,1)S(1)}, bf16[128,1024]{1,0:T(8,128)(2,1)S(1)}, u32[]{:S(2)}, u32[]{:S(2)}) collective-permute-start(bf16[128,1024]{1,0:T(8,128)(2,1)S(1)} %copy-done.25), channel_id=1, source_target_pairs={{0,8},{8,0},{16,24},{24,16},{1,9},{9,1},{17,25},{25,17},{2,10},{10... | collective-permute-start | bytes 786440 | tf_op jit(solution)/shard_map/ppermute | solution.py:530
  103.6 2.8 %collective-permute-done.31 = bf16[24,2048]{1,0:T(8,128)(2,1)S(1)} collective-permute-done((bf16[24,2048]{1,0:T(8,128)(2,1)S(1)}, bf16[24,2048]{1,0:T(8,128)(2,1)S(1)}, u32[]{:S(2)}, u32[]{:S(2)}) %collective-permute-start.31) | collective-permute-done | bytes 98336 | tf_op jit(solution)/shard_map/ppermute | solution.py:514
  106.5 1.5 collective-permute-start.33
  110.2 2.0 %collective-permute-start.23 = (bf16[256,1024]{1,0:T(8,128)(2,1)S(1)}, bf16[256,1024]{1,0:T(8,128)(2,1)S(1)}, u32[]{:S(2)}, u32[]{:S(2)}) collective-permute-start(bf16[256,1024]{1,0:T(8,128)(2,1)S(1)} %add_convert_fusion.6), channel_id=1, source_target_pairs={{0,2},{2,4},{7,5},{5,3},{8,10},{10,12},{15,13},{13,11},{16,18},{18... | collective-permute-start | bytes 1572872 | tf_op jit(solution)/shard_map/ppermute | solution.py:464
  112.2 3.5 %collective-permute-done.33 = bf16[304,1024]{1,0:T(8,128)(2,1)S(1)} collective-permute-done((bf16[304,1024]{1,0:T(8,128)(2,1)S(1)}, bf16[304,1024]{1,0:T(8,128)(2,1)S(1)}, u32[]{:S(2)}, u32[]{:S(2)}) %collective-permute-start.33) | collective-permute-done | bytes 622624 | tf_op jit(solution)/shard_map/ppermute | solution.py:464
  116.1 4.7 %collective-permute-start.34 = (bf16[304,1024]{1,0:T(8,128)(2,1)S(1)}, bf16[304,1024]{1,0:T(8,128)(2,1)S(1)}, u32[]{:S(2)}, u32[]{:S(2)}) collective-permute-start(bf16[304,1024]{1,0:T(8,128)(2,1)S(1)} %pad_maximum_fusion.1), channel_id=1, source_target_pairs={{0,2},{2,4},{7,5},{5,3},{8,10},{10,12},{15,13},{13,11},{16,18},{18... | collective-permute-start | bytes 1867784 | tf_op jit(solution)/shard_map/ppermute | solution.py:464
  120.9 1.6 %collective-permute-start.36 = (bf16[128,2048]{1,0:T(8,128)(2,1)S(1)}, bf16[128,2048]{1,0:T(8,128)(2,1)S(1)}, u32[]{:S(2)}, u32[]{:S(2)}) collective-permute-start(bf16[128,2048]{1,0:T(8,128)(2,1)S(1)} %pad_maximum_fusion.3), channel_id=1, source_target_pairs={{0,8},{8,0},{16,24},{24,16},{1,9},{9,1},{17,25},{25,17},{2,10},{10... | collective-permute-start | bytes 1572872 | tf_op jit(solution)/shard_map/ppermute | solution.py:530
  122.8 3.2 %collective-permute-start.24 = (bf16[256,1024]{1,0:T(8,128)(2,1)S(1)}, bf16[256,1024]{1,0:T(8,128)(2,1)S(1)}, u32[]{:S(2)}, u32[]{:S(2)}) collective-permute-start(bf16[256,1024]{1,0:T(8,128)(2,1)S(1)} %add_convert_fusion.5), channel_id=1, source_target_pairs={{0,2},{2,4},{4,6},{7,5},{5,3},{3,1},{8,10},{10,12},{12,14},{15,13}... | collective-permute-start | bytes 1572872 | tf_op jit(solution)/shard_map/ppermute | solution.py:464
  126.0 2.5 %collective-permute-done.34 = bf16[304,1024]{1,0:T(8,128)(2,1)S(1)} collective-permute-done((bf16[304,1024]{1,0:T(8,128)(2,1)S(1)}, bf16[304,1024]{1,0:T(8,128)(2,1)S(1)}, u32[]{:S(2)}, u32[]{:S(2)}) %collective-permute-start.34) | collective-permute-done | bytes 622624 | tf_op jit(solution)/shard_map/ppermute | solution.py:464
  130.2 3.4 %collective-permute-start.39 = (bf16[304,1024]{1,0:T(8,128)(2,1)S(1)}, bf16[304,1024]{1,0:T(8,128)(2,1)S(1)}, u32[]{:S(2)}, u32[]{:S(2)}) collective-permute-start(bf16[304,1024]{1,0:T(8,128)(2,1)S(1)} %pad_maximum_fusion.2), channel_id=1, source_target_pairs={{0,2},{2,4},{4,6},{7,5},{5,3},{3,1},{8,10},{10,12},{12,14},{15,13}... | collective-permute-start | bytes 1867784 | tf_op jit(solution)/shard_map/ppermute | solution.py:464
  134.4 6.9 %collective-permute-done.39 = bf16[304,1024]{1,0:T(8,128)(2,1)S(1)} collective-permute-done((bf16[304,1024]{1,0:T(8,128)(2,1)S(1)}, bf16[304,1024]{1,0:T(8,128)(2,1)S(1)}, u32[]{:S(2)}, u32[]{:S(2)}) %collective-permute-start.39) | collective-permute-done | bytes 622624 | tf_op jit(solution)/shard_map/ppermute | solution.py:464
  141.7 1.6 %collective-permute-done.40 = bf16[176,1024]{1,0:T(8,128)(2,1)S(1)} collective-permute-done((bf16[176,1024]{1,0:T(8,128)(2,1)S(1)}, bf16[176,1024]{1,0:T(8,128)(2,1)S(1)}, u32[]{:S(2)}, u32[]{:S(2)}) %collective-permute-start.40) | collective-permute-done | bytes 360480 | tf_op jit(solution)/shard_map/ppermute | solution.py:455
  144.8 1.6 %collective-permute-start.42 = (f32[24,1]{0,1:T(1,128)S(1)}, f32[24,1]{0,1:T(1,128)S(1)}, u32[]{:S(2)}, u32[]{:S(2)}) collective-permute-start(f32[24,1]{0,1:T(1,128)S(1)} %bitcast.27), channel_id=1, source_target_pairs={{0,16},{8,24},{16,0},{24,8},{1,17},{9,25},{17,1},{25,9},{2,18},{10... | collective-permute-start | bytes 296 | tf_op jit(solution)/shard_map/ppermute | solution.py:514
  (170 shorter events, 30.0 us)
Async XLA Ops:
  7.2 12.5 %collective-permute-start.7 = (bf16[256,1152]{1,0:T(8,128)(2,1)}, bf16[256,1152]{1,0:T(8,128)(2,1)S(1)}, u32[]{:S(2)}, u32[]{:S(2)}) collective-permute-start(bf16[256,1152]{1,0:T(8,128)(2,1)} %get-tuple-element.33.refs_10_), channel_id=1, source_target_pairs={{0,2},{2,4},{4,6},{7,5},{5,3},{3,1},{8,10},{10,12},{12,14},{15,13}... | collective-permute-start | bytes 1769480 | tf_op jit(solution)/shard_map/ppermute | solution.py:464
  12.1 13.3 %collective-permute-start.10 = (bf16[256,1024]{1,0:T(8,128)(2,1)}, bf16[256,1024]{1,0:T(8,128)(2,1)}, u32[]{:S(2)}, u32[]{:S(2)}) collective-permute-start(bf16[256,1024]{1,0:T(8,128)(2,1)} %get-tuple-element.34.refs_17_), channel_id=1, source_target_pairs={{0,2},{2,4},{4,6},{7,5},{5,3},{3,1},{8,10},{10,12},{12,14},{15,13}... | collective-permute-start | bytes 1572872 | tf_op jit(solution)/shard_map/ppermute | solution.py:464
  19.8 7.1 %collective-permute-start.8 = (bf16[256,1152]{1,0:T(8,128)(2,1)S(1)}, bf16[256,1152]{1,0:T(8,128)(2,1)S(1)}, u32[]{:S(2)}, u32[]{:S(2)}) collective-permute-start(bf16[256,1152]{1,0:T(8,128)(2,1)S(1)} %collective-permute-done.7.refs_11_), channel_id=1, source_target_pairs={{2,4},{4,6},{5,3},{3,1},{10,12},{12,14},{13,11},{11,9},{18,20},{20... | collective-permute-start | bytes 1769480 | tf_op jit(solution)/shard_map/ppermute | solution.py:464
  20.5 14.3 %collective-permute-start.4 = (bf16[128,2048]{1,0:T(8,128)(2,1)}, bf16[128,2048]{1,0:T(8,128)(2,1)S(1)}, u32[]{:S(2)}, u32[]{:S(2)}) collective-permute-start(bf16[128,2048]{1,0:T(8,128)(2,1)} %get-tuple-element.32.refs_5_), channel_id=1, source_target_pairs={{0,16},{8,24},{16,0},{24,8},{1,17},{9,25},{17,1},{25,9},{2,18},{10... | collective-permute-start | bytes 1572872 | tf_op jit(solution)/shard_map/ppermute | solution.py:530
  22.1 14.5 %collective-permute-start.3 = (bf16[128,2048]{1,0:T(8,128)(2,1)}, bf16[128,2048]{1,0:T(8,128)(2,1)S(1)}, u32[]{:S(2)}, u32[]{:S(2)}) collective-permute-start(bf16[128,2048]{1,0:T(8,128)(2,1)} %get-tuple-element.32.refs_5_), channel_id=1, source_target_pairs={{0,8},{8,0},{16,24},{24,16},{1,9},{9,1},{17,25},{25,17},{2,10},{10... | collective-permute-start | bytes 1572872 | tf_op jit(solution)/shard_map/ppermute | solution.py:530
  25.4 13.5 %collective-permute-start.11 = (bf16[256,1024]{1,0:T(8,128)(2,1)}, bf16[256,1024]{1,0:T(8,128)(2,1)}, u32[]{:S(2)}, u32[]{:S(2)}) collective-permute-start(bf16[256,1024]{1,0:T(8,128)(2,1)} %collective-permute-done.10.refs_18_), channel_id=1, source_target_pairs={{2,4},{4,6},{5,3},{3,1},{10,12},{12,14},{13,11},{11,9},{18,20},{20... | collective-permute-start | bytes 1572872 | tf_op jit(solution)/shard_map/ppermute | solution.py:464
  26.8 18.3 %collective-permute-start.9 = (bf16[256,1152]{1,0:T(8,128)(2,1)S(1)}, bf16[256,1152]{1,0:T(8,128)(2,1)S(1)}, u32[]{:S(2)}, u32[]{:S(2)}) collective-permute-start(bf16[256,1152]{1,0:T(8,128)(2,1)S(1)} %collective-permute-done.8.refs_12_), channel_id=1, source_target_pairs={{4,6},{3,1},{12,14},{11,9},{20,22},{19,17},{28,30},{27,25}} | collective-permute-start | bytes 1769480 | tf_op jit(solution)/shard_map/ppermute | solution.py:464
  34.8 7.9 %collective-permute-start.5 = (bf16[128,1024]{1,0:T(8,128)(2,1)S(1)}, bf16[128,1024]{1,0:T(8,128)(2,1)}, u32[]{:S(2)}, u32[]{:S(2)}) collective-permute-start(bf16[128,1024]{1,0:T(8,128)(2,1)S(1)} %slice.139), channel_id=1, source_target_pairs={{0,8},{8,0},{16,24},{24,16},{1,9},{9,1},{17,25},{25,17},{2,10},{10... | collective-permute-start | bytes 786440 | tf_op jit(solution)/shard_map/ppermute | solution.py:530
  37.3 7.8 %collective-permute-start.6 = (bf16[128,1024]{1,0:T(8,128)(2,1)}, bf16[128,1024]{1,0:T(8,128)(2,1)}, u32[]{:S(2)}, u32[]{:S(2)}) collective-permute-start(bf16[128,1024]{1,0:T(8,128)(2,1)} %slice.140), channel_id=1, source_target_pairs={{0,16},{8,24},{16,0},{24,8},{1,17},{9,25},{17,1},{25,9},{2,18},{10... | collective-permute-start | bytes 786440 | tf_op jit(solution)/shard_map/ppermute | solution.py:530
  38.8 8.1 %collective-permute-start.15 = (bf16[256,1024]{1,0:T(8,128)(2,1)}, bf16[256,1024]{1,0:T(8,128)(2,1)}, u32[]{:S(2)}, u32[]{:S(2)}) collective-permute-start(bf16[256,1024]{1,0:T(8,128)(2,1)} %collective-permute-done.11.refs_19_), channel_id=1, source_target_pairs={{4,6},{3,1},{12,14},{11,9},{20,22},{19,17},{28,30},{27,25}} | collective-permute-start | bytes 1572872 | tf_op jit(solution)/shard_map/ppermute | solution.py:464
  40.3 8.7 %collective-permute-start.16 = (bf16[256,1024]{1,0:T(8,128)(2,1)}, bf16[256,1024]{1,0:T(8,128)(2,1)}, u32[]{:S(2)}, u32[]{:S(2)}) collective-permute-start(bf16[256,1024]{1,0:T(8,128)(2,1)} %collective-permute-done.10.refs_18_), channel_id=1, source_target_pairs={{0,1},{1,0},{2,3},{3,2},{4,5},{5,4},{6,7},{7,6},{8,9},{9,8},{10,11... | collective-permute-start | bytes 1572872 | tf_op jit(solution)/shard_map/ppermute | solution.py:455
  42.7 8.2 %collective-permute-start.12 = (bf16[256,1152]{1,0:T(8,128)(2,1)S(1)}, bf16[256,1152]{1,0:T(8,128)(2,1)S(1)}, u32[]{:S(2)}, u32[]{:S(2)}) collective-permute-start(bf16[256,1152]{1,0:T(8,128)(2,1)S(1)} %collective-permute-done.7.refs_11_), channel_id=1, source_target_pairs={{0,1},{1,0},{2,3},{3,2},{4,5},{5,4},{6,7},{7,6},{8,9},{9,8},{10,11... | collective-permute-start | bytes 1769480 | tf_op jit(solution)/shard_map/ppermute | solution.py:455
  45.1 5.8 %collective-permute-start.13 = (bf16[256,1152]{1,0:T(8,128)(2,1)S(1)}, bf16[256,1152]{1,0:T(8,128)(2,1)}, u32[]{:S(2)}, u32[]{:S(2)}) collective-permute-start(bf16[256,1152]{1,0:T(8,128)(2,1)S(1)} %collective-permute-done.8.refs_12_), channel_id=1, source_target_pairs={{0,1},{1,0},{2,3},{3,2},{4,5},{5,4},{6,7},{7,6},{8,9},{9,8},{10,11... | collective-permute-start | bytes 1769480 | tf_op jit(solution)/shard_map/ppermute | solution.py:455
  45.1 6.5 %collective-permute-start.14 = (bf16[256,1152]{1,0:T(8,128)(2,1)S(1)}, bf16[256,1152]{1,0:T(8,128)(2,1)}, u32[]{:S(2)}, u32[]{:S(2)}) collective-permute-start(bf16[256,1152]{1,0:T(8,128)(2,1)S(1)} %collective-permute-done.9.refs_13_), channel_id=1, source_target_pairs={{0,1},{1,0},{2,3},{3,2},{4,5},{5,4},{6,7},{7,6},{8,9},{9,8},{10,11... | collective-permute-start | bytes 1769480 | tf_op jit(solution)/shard_map/ppermute | solution.py:455
  89.4 5.9 %collective-permute-start.26 = (bf16[256,1024]{1,0:T(8,128)(2,1)}, bf16[256,1024]{1,0:T(8,128)(2,1)S(1)}, u32[]{:S(2)}, u32[]{:S(2)}) collective-permute-start(bf16[256,1024]{1,0:T(8,128)(2,1)} %get-tuple-element.45), channel_id=1, source_target_pairs={{0,1},{1,0},{2,3},{3,2},{4,5},{5,4},{6,7},{7,6},{8,9},{9,8},{10,11... | collective-permute-start | bytes 1572872 | tf_op jit(solution)/shard_map/ppermute | solution.py:455
  90.6 7.9 %collective-permute-start.27 = (bf16[256,1024]{1,0:T(8,128)(2,1)}, bf16[256,1024]{1,0:T(8,128)(2,1)S(1)}, u32[]{:S(2)}, u32[]{:S(2)}) collective-permute-start(bf16[256,1024]{1,0:T(8,128)(2,1)} %get-tuple-element.46), channel_id=1, source_target_pairs={{0,1},{1,0},{2,3},{3,2},{4,5},{5,4},{6,7},{7,6},{8,9},{9,8},{10,11... | collective-permute-start | bytes 1572872 | tf_op jit(solution)/shard_map/ppermute | solution.py:455
  91.3 18.6 %collective-permute-start.22 = (bf16[256,1024]{1,0:T(8,128)(2,1)S(1)}, bf16[256,1024]{1,0:T(8,128)(2,1)S(1)}, u32[]{:S(2)}, u32[]{:S(2)}) collective-permute-start(bf16[256,1024]{1,0:T(8,128)(2,1)S(1)} %add_convert_fusion.7), channel_id=1, source_target_pairs={{0,2},{7,5},{8,10},{15,13},{16,18},{23,21},{24,26},{31,29}} | collective-permute-start | bytes 1572872 | tf_op jit(solution)/shard_map/ppermute | solution.py:464
  93.4 27.4 %collective-permute-start.35 = (bf16[128,1024]{1,0:T(8,128)(2,1)S(1)}, bf16[128,1024]{1,0:T(8,128)(2,1)S(1)}, u32[]{:S(2)}, u32[]{:S(2)}) collective-permute-start(bf16[128,1024]{1,0:T(8,128)(2,1)S(1)} %copy-done.24), channel_id=1, source_target_pairs={{0,16},{8,24},{16,0},{24,8},{1,17},{9,25},{17,1},{25,9},{2,18},{10... | collective-permute-start | bytes 786440 | tf_op jit(solution)/shard_map/ppermute | solution.py:530
  95.4 6.3 %collective-permute-start.32 = (bf16[24,2048]{1,0:T(8,128)(2,1)S(1)}, bf16[24,2048]{1,0:T(8,128)(2,1)S(1)}, u32[]{:S(2)}, u32[]{:S(2)}) collective-permute-start(bf16[24,2048]{1,0:T(8,128)(2,1)S(1)} %get-tuple-element.61), channel_id=1, source_target_pairs={{0,24},{8,16},{16,8},{24,0},{1,25},{9,17},{17,9},{25,1},{2,26},{10... | collective-permute-start | bytes 294920 | tf_op jit(solution)/shard_map/ppermute | solution.py:514
  97.4 9.0 %collective-permute-start.31 = (bf16[24,2048]{1,0:T(8,128)(2,1)S(1)}, bf16[24,2048]{1,0:T(8,128)(2,1)S(1)}, u32[]{:S(2)}, u32[]{:S(2)}) collective-permute-start(bf16[24,2048]{1,0:T(8,128)(2,1)S(1)} %get-tuple-element.61), channel_id=1, source_target_pairs={{0,16},{8,24},{16,0},{24,8},{1,17},{9,25},{17,1},{25,9},{2,18},{10... | collective-permute-start | bytes 294920 | tf_op jit(solution)/shard_map/ppermute | solution.py:514
  98.4 7.9 %collective-permute-start.30 = (bf16[24,2048]{1,0:T(8,128)(2,1)S(1)}, bf16[24,2048]{1,0:T(8,128)(2,1)S(1)}, u32[]{:S(2)}, u32[]{:S(2)}) collective-permute-start(bf16[24,2048]{1,0:T(8,128)(2,1)S(1)} %get-tuple-element.61), channel_id=1, source_target_pairs={{0,8},{8,0},{16,24},{24,16},{1,9},{9,1},{17,25},{25,17},{2,10},{10... | collective-permute-start | bytes 294920 | tf_op jit(solution)/shard_map/ppermute | solution.py:514
  101.7 7.3 %collective-permute-start.37 = (bf16[128,1024]{1,0:T(8,128)(2,1)S(1)}, bf16[128,1024]{1,0:T(8,128)(2,1)S(1)}, u32[]{:S(2)}, u32[]{:S(2)}) collective-permute-start(bf16[128,1024]{1,0:T(8,128)(2,1)S(1)} %copy-done.25), channel_id=1, source_target_pairs={{0,8},{8,0},{16,24},{24,16},{1,9},{9,1},{17,25},{25,17},{2,10},{10... | collective-permute-start | bytes 786440 | tf_op jit(solution)/shard_map/ppermute | solution.py:530
  106.5 9.2 %collective-permute-start.33 = (bf16[304,1024]{1,0:T(8,128)(2,1)S(1)}, bf16[304,1024]{1,0:T(8,128)(2,1)S(1)}, u32[]{:S(2)}, u32[]{:S(2)}) collective-permute-start(bf16[304,1024]{1,0:T(8,128)(2,1)S(1)} %pad_maximum_fusion), channel_id=1, source_target_pairs={{0,2},{7,5},{8,10},{15,13},{16,18},{23,21},{24,26},{31,29}} | collective-permute-start | bytes 1867784 | tf_op jit(solution)/shard_map/ppermute | solution.py:464
  109.1 19.7 %collective-permute-start.38 = (bf16[128,2048]{1,0:T(8,128)(2,1)S(1)}, bf16[128,2048]{1,0:T(8,128)(2,1)S(1)}, u32[]{:S(2)}, u32[]{:S(2)}) collective-permute-start(bf16[128,2048]{1,0:T(8,128)(2,1)S(1)} %pad_maximum_fusion.4), channel_id=1, source_target_pairs={{0,16},{8,24},{16,0},{24,8},{1,17},{9,25},{17,1},{25,9},{2,18},{10... | collective-permute-start | bytes 1572872 | tf_op jit(solution)/shard_map/ppermute | solution.py:530
  110.2 12.3 %collective-permute-start.23 = (bf16[256,1024]{1,0:T(8,128)(2,1)S(1)}, bf16[256,1024]{1,0:T(8,128)(2,1)S(1)}, u32[]{:S(2)}, u32[]{:S(2)}) collective-permute-start(bf16[256,1024]{1,0:T(8,128)(2,1)S(1)} %add_convert_fusion.6), channel_id=1, source_target_pairs={{0,2},{2,4},{7,5},{5,3},{8,10},{10,12},{15,13},{13,11},{16,18},{18... | collective-permute-start | bytes 1572872 | tf_op jit(solution)/shard_map/ppermute | solution.py:464
  116.1 12.4 %collective-permute-start.34 = (bf16[304,1024]{1,0:T(8,128)(2,1)S(1)}, bf16[304,1024]{1,0:T(8,128)(2,1)S(1)}, u32[]{:S(2)}, u32[]{:S(2)}) collective-permute-start(bf16[304,1024]{1,0:T(8,128)(2,1)S(1)} %pad_maximum_fusion.1), channel_id=1, source_target_pairs={{0,2},{2,4},{7,5},{5,3},{8,10},{10,12},{15,13},{13,11},{16,18},{18... | collective-permute-start | bytes 1867784 | tf_op jit(solution)/shard_map/ppermute | solution.py:464
  120.9 9.2 %collective-permute-start.36 = (bf16[128,2048]{1,0:T(8,128)(2,1)S(1)}, bf16[128,2048]{1,0:T(8,128)(2,1)S(1)}, u32[]{:S(2)}, u32[]{:S(2)}) collective-permute-start(bf16[128,2048]{1,0:T(8,128)(2,1)S(1)} %pad_maximum_fusion.3), channel_id=1, source_target_pairs={{0,8},{8,0},{16,24},{24,16},{1,9},{9,1},{17,25},{25,17},{2,10},{10... | collective-permute-start | bytes 1572872 | tf_op jit(solution)/shard_map/ppermute | solution.py:530
  122.8 11.3 %collective-permute-start.24 = (bf16[256,1024]{1,0:T(8,128)(2,1)S(1)}, bf16[256,1024]{1,0:T(8,128)(2,1)S(1)}, u32[]{:S(2)}, u32[]{:S(2)}) collective-permute-start(bf16[256,1024]{1,0:T(8,128)(2,1)S(1)} %add_convert_fusion.5), channel_id=1, source_target_pairs={{0,2},{2,4},{4,6},{7,5},{5,3},{3,1},{8,10},{10,12},{12,14},{15,13}... | collective-permute-start | bytes 1572872 | tf_op jit(solution)/shard_map/ppermute | solution.py:464
  130.2 11.1 %collective-permute-start.39 = (bf16[304,1024]{1,0:T(8,128)(2,1)S(1)}, bf16[304,1024]{1,0:T(8,128)(2,1)S(1)}, u32[]{:S(2)}, u32[]{:S(2)}) collective-permute-start(bf16[304,1024]{1,0:T(8,128)(2,1)S(1)} %pad_maximum_fusion.2), channel_id=1, source_target_pairs={{0,2},{2,4},{4,6},{7,5},{5,3},{3,1},{8,10},{10,12},{12,14},{15,13}... | collective-permute-start | bytes 1867784 | tf_op jit(solution)/shard_map/ppermute | solution.py:464
  134.3 7.3 %collective-permute-start.25 = (bf16[128,1024]{1,0:T(8,128)(2,1)S(1)}, bf16[128,1024]{1,0:T(8,128)(2,1)S(1)}, u32[]{:S(2)}, u32[]{:S(2)}) collective-permute-start(bf16[128,1024]{1,0:T(8,128)(2,1)S(1)} %slice.148), channel_id=1, source_target_pairs={{0,1},{1,0},{2,3},{3,2},{4,5},{5,4},{6,7},{7,6},{8,9},{9,8},{10,11... | collective-permute-start | bytes 786440 | tf_op jit(solution)/shard_map/ppermute | solution.py:455
  144.8 5.2 %collective-permute-start.42 = (f32[24,1]{0,1:T(1,128)S(1)}, f32[24,1]{0,1:T(1,128)S(1)}, u32[]{:S(2)}, u32[]{:S(2)}) collective-permute-start(f32[24,1]{0,1:T(1,128)S(1)} %bitcast.27), channel_id=1, source_target_pairs={{0,16},{8,24},{16,0},{24,8},{1,17},{9,25},{17,1},{25,9},{2,18},{10... | collective-permute-start | bytes 296 | tf_op jit(solution)/shard_map/ppermute | solution.py:514
  146.5 4.4 %collective-permute-start.43 = (f32[24,1]{0,1:T(1,128)S(1)}, f32[24,1]{0,1:T(1,128)S(1)}, u32[]{:S(2)}, u32[]{:S(2)}) collective-permute-start(f32[24,1]{0,1:T(1,128)S(1)} %bitcast.28), channel_id=1, source_target_pairs={{0,24},{8,16},{16,8},{24,0},{1,25},{9,17},{17,9},{25,1},{2,26},{10... | collective-permute-start | bytes 296 | tf_op jit(solution)/shard_map/ppermute | solution.py:514
  (40 other events, 378.1 us)

commit v4 on v3

--- a/solution.py
+++ b/solution.py
@@ -348,15 +348,16 @@
     batch = incoming.shape[1]
     at = lax.broadcasted_iota(jnp.int32, (last_ref.shape[0], batch), 1)
     last = None
+    inputs = incoming[: count // per].reshape(count * rows, width)
+    gate = across_columns(inputs, gate_ref[...])
+    up = across_columns(inputs, up_ref[...])
+    mids = (gate / (1.0 + jnp.exp(-gate)) * up).astype(jnp.bfloat16)
+    lows = across_columns(inputs, lower_ref[...])
+    place = lax.broadcasted_iota(jnp.int32, lows.shape, 1) - slots_ref[...] * RANK
+    lows = jnp.where((place >= 0) & (place < RANK), lows, 0.0).astype(jnp.bfloat16)
     for b in range(count // per):
-        inputs = incoming[b]
-        gate = across_columns(inputs, gate_ref[...])
-        up = across_columns(inputs, up_ref[...])
-        mid = (gate / (1.0 + jnp.exp(-gate)) * up).astype(jnp.bfloat16)
-        low = across_columns(inputs, lower_ref[...])
-        slot = slots_ref[b * batch : (b + 1) * batch, :]
-        place = lax.broadcasted_iota(jnp.int32, low.shape, 1) - slot * RANK
-        low = jnp.where((place >= 0) & (place < RANK), low, 0.0).astype(jnp.bfloat16)
+        mid = mids[b * batch : (b + 1) * batch]
+        low = lows[b * batch : (b + 1) * batch]
         part = jnp.dot(mid, down_ref[...], preferred_element_type=jnp.float32)
         part = part + jnp.dot(low, upper_ref[...], preferred_element_type=jnp.float32)
         part = part.astype(jnp.bfloat16)

time: 152 us -> 152 us (level)
  no operation moved by 1% of the time
where the time goes in v4:
time: 152 us
  starting transfers between devices  55.1 us (36%)
  waiting for transfers between devices  44.6 us (29%)
  Pallas kernels  39.2 us (26%)
  local copies, waits for them, and re-layouts  5.33 us (4%)
  other arithmetic  4.71 us (3%)
    pallas_call x1, Pallas kernels, run_experts(): pl.pallas_call(functools.partial(experts_kernel, AHEAD, chips, count), in...  36.3 us
    ppermute x12, starting transfers between devices, along(): return lax.ppermute(value, 'tensor', upward + downward)  30 us
    ppermute x12, waiting for transfers between devices, along(): return lax.ppermute(value, 'tensor', upward + downward)  18.6 us
    ppermute x8, waiting for transfers between devices, from_peer(): return lax.ppermute(value, 'dp', [(i, i ^ step) for i in range(size)])  14.1 us
    ppermute x8, starting transfers between devices, from_peer(): return lax.ppermute(value, 'dp', [(i, i ^ step) for i in range(size)])  12.3 us
    ppermute x6, starting transfers between devices, sent_along(): lax.ppermute(value, axis, [(i, i ^ step) for i in range(size)])  7.11 us
    ppermute x6, waiting for transfers between devices, sent_along(): lax.ppermute(value, axis, [(i, i ^ step) for i in range(size)])  6.79 us
    ppermute x17, starting transfers between devices, twin_of(): lax.ppermute(value, 'tensor', [(i, i ^ 1) for i in range(tensor_size)])  5.59 us
  transfers between devices with their start and end apart: 44, of which 21 were waited for; matrix products, arithmetic and copies ran while one was open for 5% of the time, Pallas kernels for 0%

profile of v4, /device:TPU:0, one launch (start us, length us, event | category | flops | bytes accessed | tf_op | source)
XLA Modules:
  0.0 151.6 jit_solution(13373028485622434255)
XLA Ops:
  4.3 2.9 %prepare.1 = (bf16[256,1152]{1,0:T(8,128)(2,1)}, bf16[256,1024]{1,0:T(8,128)(2,1)}, bf16[128,2048]{1,0:T(8,128)(2,1)}) custom-call(bf16[128,2048]{1,0:T(8,128)(2,1)} %tok_ref.1, bf16[128,2048]{1,0:T(8,128)(2,1)} %copy-done.12, bf16[2048]{0:T(1024)(128)(2,1)} %gain_ref.1, s32[6,128]{1,0:T(8,128)} %bitcast.24, s32[6,128]{1,0:T(8,128)} %copy-done.19, ...), custom_call_target="tpu_custom_call" | custom-call | tf_op jit(solution)/shard_map/prepare/pallas_call | solution.py:200
  7.2 4.9 %collective-permute-start.7 = (bf16[256,1152]{1,0:T(8,128)(2,1)}, bf16[256,1152]{1,0:T(8,128)(2,1)S(1)}, u32[]{:S(2)}, u32[]{:S(2)}) collective-permute-start(bf16[256,1152]{1,0:T(8,128)(2,1)} %get-tuple-element.33.refs_10_), channel_id=1, source_target_pairs={{0,2},{2,4},{4,6},{7,5},{5,3},{3,1},{8,10},{10,12},{12,14},{15,13}... | collective-permute-start | bytes 1769480 | tf_op jit(solution)/shard_map/ppermute | solution.py:465
  12.1 4.3 %collective-permute-start.10 = (bf16[256,1024]{1,0:T(8,128)(2,1)}, bf16[256,1024]{1,0:T(8,128)(2,1)}, u32[]{:S(2)}, u32[]{:S(2)}) collective-permute-start(bf16[256,1024]{1,0:T(8,128)(2,1)} %get-tuple-element.34.refs_17_), channel_id=1, source_target_pairs={{0,2},{2,4},{4,6},{7,5},{5,3},{3,1},{8,10},{10,12},{12,14},{15,13}... | collective-permute-start | bytes 1572872 | tf_op jit(solution)/shard_map/ppermute | solution.py:465
  16.4 3.4 %collective-permute-done.7.refs_11_ = bf16[256,1152]{1,0:T(8,128)(2,1)S(1)} collective-permute-done((bf16[256,1152]{1,0:T(8,128)(2,1)}, bf16[256,1152]{1,0:T(8,128)(2,1)S(1)}, u32[]{:S(2)}, u32[]{:S(2)}) %collective-permute-start.7) | collective-permute-done | bytes 589856 | tf_op jit(solution)/shard_map/ppermute | solution.py:465
  20.5 1.6 %collective-permute-start.4 = (bf16[128,2048]{1,0:T(8,128)(2,1)}, bf16[128,2048]{1,0:T(8,128)(2,1)S(1)}, u32[]{:S(2)}, u32[]{:S(2)}) collective-permute-start(bf16[128,2048]{1,0:T(8,128)(2,1)} %get-tuple-element.32.refs_5_), channel_id=1, source_target_pairs={{0,16},{8,24},{16,0},{24,8},{1,17},{9,25},{17,1},{25,9},{2,18},{10... | collective-permute-start | bytes 1572872 | tf_op jit(solution)/shard_map/ppermute | solution.py:531
  22.1 1.5 collective-permute-start.3
  23.6 1.8 %collective-permute-done.10.refs_18_ = bf16[256,1024]{1,0:T(8,128)(2,1)} collective-permute-done((bf16[256,1024]{1,0:T(8,128)(2,1)}, bf16[256,1024]{1,0:T(8,128)(2,1)}, u32[]{:S(2)}, u32[]{:S(2)}) %collective-permute-start.10) | collective-permute-done | bytes 524320 | tf_op jit(solution)/shard_map/ppermute | solution.py:465
  27.5 7.2 %collective-permute-done.4.refs_7_ = bf16[128,2048]{1,0:T(8,128)(2,1)S(1)} collective-permute-done((bf16[128,2048]{1,0:T(8,128)(2,1)}, bf16[128,2048]{1,0:T(8,128)(2,1)S(1)}, u32[]{:S(2)}, u32[]{:S(2)}) %collective-permute-start.4) | collective-permute-done | bytes 524320 | tf_op jit(solution)/shard_map/ppermute | solution.py:531
  34.8 1.7 %collective-permute-start.5 = (bf16[128,1024]{1,0:T(8,128)(2,1)S(1)}, bf16[128,1024]{1,0:T(8,128)(2,1)}, u32[]{:S(2)}, u32[]{:S(2)}) collective-permute-start(bf16[128,1024]{1,0:T(8,128)(2,1)S(1)} %slice.139), channel_id=1, source_target_pairs={{0,8},{8,0},{16,24},{24,16},{1,9},{9,1},{17,25},{25,17},{2,10},{10... | collective-permute-start | bytes 786440 | tf_op jit(solution)/shard_map/ppermute | solution.py:531
  37.3 1.5 %collective-permute-start.6 = (bf16[128,1024]{1,0:T(8,128)(2,1)}, bf16[128,1024]{1,0:T(8,128)(2,1)}, u32[]{:S(2)}, u32[]{:S(2)}) collective-permute-start(bf16[128,1024]{1,0:T(8,128)(2,1)} %slice.140), channel_id=1, source_target_pairs={{0,16},{8,24},{16,0},{24,8},{1,17},{9,25},{17,1},{25,9},{2,18},{10... | collective-permute-start | bytes 786440 | tf_op jit(solution)/shard_map/ppermute | solution.py:531
  38.8 1.5 collective-permute-start.15
  40.6 2.1 %collective-permute-done.5.refs_8_ = bf16[128,1024]{1,0:T(8,128)(2,1)} collective-permute-done((bf16[128,1024]{1,0:T(8,128)(2,1)S(1)}, bf16[128,1024]{1,0:T(8,128)(2,1)}, u32[]{:S(2)}, u32[]{:S(2)}) %collective-permute-start.5) | collective-permute-done | bytes 262176 | tf_op jit(solution)/shard_map/ppermute | solution.py:531
  42.7 2.5 %collective-permute-done.6.refs_9_ = bf16[128,1024]{1,0:T(8,128)(2,1)} collective-permute-done((bf16[128,1024]{1,0:T(8,128)(2,1)}, bf16[128,1024]{1,0:T(8,128)(2,1)}, u32[]{:S(2)}, u32[]{:S(2)}) %collective-permute-start.6) | collective-permute-done | bytes 262176 | tf_op jit(solution)/shard_map/ppermute | solution.py:531
  46.9 2.1 %collective-permute-start.17 = (bf16[256,1024]{1,0:T(8,128)(2,1)}, bf16[256,1024]{1,0:T(8,128)(2,1)}, u32[]{:S(2)}, u32[]{:S(2)}) collective-permute-start(bf16[256,1024]{1,0:T(8,128)(2,1)} %collective-permute-done.11.refs_19_), channel_id=1, source_target_pairs={{0,1},{1,0},{2,3},{3,2},{4,5},{5,4},{6,7},{7,6},{8,9},{9,8},{10,11... | collective-permute-start | bytes 1572872 | tf_op jit(solution)/shard_map/ppermute | solution.py:456
  51.7 36.3 %run_experts.1 = (bf16[256,1024]{1,0:T(8,128)(2,1)}, bf16[256,1024]{1,0:T(8,128)(2,1)}, bf16[256,1024]{1,0:T(8,128)(2,1)}, bf16[256,1024]{1,0:T(8,128)(2,1)}, bf...) custom-call(s32[1]{0:T(128)} %bitcast.position_ref, ...), custom_call_target="tpu_custom_call" | custom-call | flops 17716740096 | bytes 69206016 | tf_op jit(solution)/shard_map/run_experts/pallas_call | solution.py:401
  91.0 1.9 %collective-permute-start.22 = (bf16[256,1024]{1,0:T(8,128)(2,1)S(1)}, bf16[256,1024]{1,0:T(8,128)(2,1)S(1)}, u32[]{:S(2)}, u32[]{:S(2)}) collective-permute-start(bf16[256,1024]{1,0:T(8,128)(2,1)S(1)} %add_convert_fusion.7), channel_id=1, source_target_pairs={{0,2},{7,5},{8,10},{15,13},{16,18},{23,21},{24,26},{31,29}} | collective-permute-start | bytes 1572872 | tf_op jit(solution)/shard_map/ppermute | solution.py:465
  93.1 1.6 %collective-permute-start.35 = (bf16[128,1024]{1,0:T(8,128)(2,1)S(1)}, bf16[128,1024]{1,0:T(8,128)(2,1)S(1)}, u32[]{:S(2)}, u32[]{:S(2)}) collective-permute-start(bf16[128,1024]{1,0:T(8,128)(2,1)S(1)} %copy-done.24), channel_id=1, source_target_pairs={{0,16},{8,24},{16,0},{24,8},{1,17},{9,25},{17,1},{25,9},{2,18},{10... | collective-permute-start | bytes 786440 | tf_op jit(solution)/shard_map/ppermute | solution.py:531
  95.1 1.9 %collective-permute-start.32 = (bf16[24,2048]{1,0:T(8,128)(2,1)S(1)}, bf16[24,2048]{1,0:T(8,128)(2,1)S(1)}, u32[]{:S(2)}, u32[]{:S(2)}) collective-permute-start(bf16[24,2048]{1,0:T(8,128)(2,1)S(1)} %get-tuple-element.61), channel_id=1, source_target_pairs={{0,24},{8,16},{16,8},{24,0},{1,25},{9,17},{17,9},{25,1},{2,26},{10... | collective-permute-start | bytes 294920 | tf_op jit(solution)/shard_map/ppermute | solution.py:515
  98.8 2.6 %collective-permute-done.32 = bf16[24,2048]{1,0:T(8,128)(2,1)S(1)} collective-permute-done((bf16[24,2048]{1,0:T(8,128)(2,1)S(1)}, bf16[24,2048]{1,0:T(8,128)(2,1)S(1)}, u32[]{:S(2)}, u32[]{:S(2)}) %collective-permute-start.32) | collective-permute-done | bytes 98336 | tf_op jit(solution)/shard_map/ppermute | solution.py:515
  101.3 1.9 %collective-permute-start.37 = (bf16[128,1024]{1,0:T(8,128)(2,1)S(1)}, bf16[128,1024]{1,0:T(8,128)(2,1)S(1)}, u32[]{:S(2)}, u32[]{:S(2)}) collective-permute-start(bf16[128,1024]{1,0:T(8,128)(2,1)S(1)} %copy-done.25), channel_id=1, source_target_pairs={{0,8},{8,0},{16,24},{24,16},{1,9},{9,1},{17,25},{25,17},{2,10},{10... | collective-permute-start | bytes 786440 | tf_op jit(solution)/shard_map/ppermute | solution.py:531
  103.2 2.8 %collective-permute-done.31 = bf16[24,2048]{1,0:T(8,128)(2,1)S(1)} collective-permute-done((bf16[24,2048]{1,0:T(8,128)(2,1)S(1)}, bf16[24,2048]{1,0:T(8,128)(2,1)S(1)}, u32[]{:S(2)}, u32[]{:S(2)}) %collective-permute-start.31) | collective-permute-done | bytes 98336 | tf_op jit(solution)/shard_map/ppermute | solution.py:515
  106.2 1.5 collective-permute-start.33
  109.9 2.0 %collective-permute-start.23 = (bf16[256,1024]{1,0:T(8,128)(2,1)S(1)}, bf16[256,1024]{1,0:T(8,128)(2,1)S(1)}, u32[]{:S(2)}, u32[]{:S(2)}) collective-permute-start(bf16[256,1024]{1,0:T(8,128)(2,1)S(1)} %add_convert_fusion.6), channel_id=1, source_target_pairs={{0,2},{2,4},{7,5},{5,3},{8,10},{10,12},{15,13},{13,11},{16,18},{18... | collective-permute-start | bytes 1572872 | tf_op jit(solution)/shard_map/ppermute | solution.py:465
  111.8 3.5 %collective-permute-done.33 = bf16[304,1024]{1,0:T(8,128)(2,1)S(1)} collective-permute-done((bf16[304,1024]{1,0:T(8,128)(2,1)S(1)}, bf16[304,1024]{1,0:T(8,128)(2,1)S(1)}, u32[]{:S(2)}, u32[]{:S(2)}) %collective-permute-start.33) | collective-permute-done | bytes 622624 | tf_op jit(solution)/shard_map/ppermute | solution.py:465
  115.7 4.7 %collective-permute-start.34 = (bf16[304,1024]{1,0:T(8,128)(2,1)S(1)}, bf16[304,1024]{1,0:T(8,128)(2,1)S(1)}, u32[]{:S(2)}, u32[]{:S(2)}) collective-permute-start(bf16[304,1024]{1,0:T(8,128)(2,1)S(1)} %pad_maximum_fusion.1), channel_id=1, source_target_pairs={{0,2},{2,4},{7,5},{5,3},{8,10},{10,12},{15,13},{13,11},{16,18},{18... | collective-permute-start | bytes 1867784 | tf_op jit(solution)/shard_map/ppermute | solution.py:465
  120.6 1.6 %collective-permute-start.36 = (bf16[128,2048]{1,0:T(8,128)(2,1)S(1)}, bf16[128,2048]{1,0:T(8,128)(2,1)S(1)}, u32[]{:S(2)}, u32[]{:S(2)}) collective-permute-start(bf16[128,2048]{1,0:T(8,128)(2,1)S(1)} %pad_maximum_fusion.3), channel_id=1, source_target_pairs={{0,8},{8,0},{16,24},{24,16},{1,9},{9,1},{17,25},{25,17},{2,10},{10... | collective-permute-start | bytes 1572872 | tf_op jit(solution)/shard_map/ppermute | solution.py:531
  122.5 3.2 %collective-permute-start.24 = (bf16[256,1024]{1,0:T(8,128)(2,1)S(1)}, bf16[256,1024]{1,0:T(8,128)(2,1)S(1)}, u32[]{:S(2)}, u32[]{:S(2)}) collective-permute-start(bf16[256,1024]{1,0:T(8,128)(2,1)S(1)} %add_convert_fusion.5), channel_id=1, source_target_pairs={{0,2},{2,4},{4,6},{7,5},{5,3},{3,1},{8,10},{10,12},{12,14},{15,13}... | collective-permute-start | bytes 1572872 | tf_op jit(solution)/shard_map/ppermute | solution.py:465
  125.7 2.5 %collective-permute-done.34 = bf16[304,1024]{1,0:T(8,128)(2,1)S(1)} collective-permute-done((bf16[304,1024]{1,0:T(8,128)(2,1)S(1)}, bf16[304,1024]{1,0:T(8,128)(2,1)S(1)}, u32[]{:S(2)}, u32[]{:S(2)}) %collective-permute-start.34) | collective-permute-done | bytes 622624 | tf_op jit(solution)/shard_map/ppermute | solution.py:465
  129.9 3.4 %collective-permute-start.39 = (bf16[304,1024]{1,0:T(8,128)(2,1)S(1)}, bf16[304,1024]{1,0:T(8,128)(2,1)S(1)}, u32[]{:S(2)}, u32[]{:S(2)}) collective-permute-start(bf16[304,1024]{1,0:T(8,128)(2,1)S(1)} %pad_maximum_fusion.2), channel_id=1, source_target_pairs={{0,2},{2,4},{4,6},{7,5},{5,3},{3,1},{8,10},{10,12},{12,14},{15,13}... | collective-permute-start | bytes 1867784 | tf_op jit(solution)/shard_map/ppermute | solution.py:465
  134.0 6.9 %collective-permute-done.39 = bf16[304,1024]{1,0:T(8,128)(2,1)S(1)} collective-permute-done((bf16[304,1024]{1,0:T(8,128)(2,1)S(1)}, bf16[304,1024]{1,0:T(8,128)(2,1)S(1)}, u32[]{:S(2)}, u32[]{:S(2)}) %collective-permute-start.39) | collective-permute-done | bytes 622624 | tf_op jit(solution)/shard_map/ppermute | solution.py:465
  141.4 1.6 %collective-permute-done.40 = bf16[176,1024]{1,0:T(8,128)(2,1)S(1)} collective-permute-done((bf16[176,1024]{1,0:T(8,128)(2,1)S(1)}, bf16[176,1024]{1,0:T(8,128)(2,1)S(1)}, u32[]{:S(2)}, u32[]{:S(2)}) %collective-permute-start.40) | collective-permute-done | bytes 360480 | tf_op jit(solution)/shard_map/ppermute | solution.py:456
  144.5 1.6 %collective-permute-start.42 = (f32[24,1]{0,1:T(1,128)S(1)}, f32[24,1]{0,1:T(1,128)S(1)}, u32[]{:S(2)}, u32[]{:S(2)}) collective-permute-start(f32[24,1]{0,1:T(1,128)S(1)} %bitcast.27), channel_id=1, source_target_pairs={{0,16},{8,24},{16,0},{24,8},{1,17},{9,25},{17,1},{25,9},{2,18},{10... | collective-permute-start | bytes 296 | tf_op jit(solution)/shard_map/ppermute | solution.py:515
  (170 shorter events, 30.0 us)
Async XLA Ops:
  7.2 12.5 %collective-permute-start.7 = (bf16[256,1152]{1,0:T(8,128)(2,1)}, bf16[256,1152]{1,0:T(8,128)(2,1)S(1)}, u32[]{:S(2)}, u32[]{:S(2)}) collective-permute-start(bf16[256,1152]{1,0:T(8,128)(2,1)} %get-tuple-element.33.refs_10_), channel_id=1, source_target_pairs={{0,2},{2,4},{4,6},{7,5},{5,3},{3,1},{8,10},{10,12},{12,14},{15,13}... | collective-permute-start | bytes 1769480 | tf_op jit(solution)/shard_map/ppermute | solution.py:465
  12.1 13.3 %collective-permute-start.10 = (bf16[256,1024]{1,0:T(8,128)(2,1)}, bf16[256,1024]{1,0:T(8,128)(2,1)}, u32[]{:S(2)}, u32[]{:S(2)}) collective-permute-start(bf16[256,1024]{1,0:T(8,128)(2,1)} %get-tuple-element.34.refs_17_), channel_id=1, source_target_pairs={{0,2},{2,4},{4,6},{7,5},{5,3},{3,1},{8,10},{10,12},{12,14},{15,13}... | collective-permute-start | bytes 1572872 | tf_op jit(solution)/shard_map/ppermute | solution.py:465
  19.8 7.1 %collective-permute-start.8 = (bf16[256,1152]{1,0:T(8,128)(2,1)S(1)}, bf16[256,1152]{1,0:T(8,128)(2,1)S(1)}, u32[]{:S(2)}, u32[]{:S(2)}) collective-permute-start(bf16[256,1152]{1,0:T(8,128)(2,1)S(1)} %collective-permute-done.7.refs_11_), channel_id=1, source_target_pairs={{2,4},{4,6},{5,3},{3,1},{10,12},{12,14},{13,11},{11,9},{18,20},{20... | collective-permute-start | bytes 1769480 | tf_op jit(solution)/shard_map/ppermute | solution.py:465
  20.5 14.3 %collective-permute-start.4 = (bf16[128,2048]{1,0:T(8,128)(2,1)}, bf16[128,2048]{1,0:T(8,128)(2,1)S(1)}, u32[]{:S(2)}, u32[]{:S(2)}) collective-permute-start(bf16[128,2048]{1,0:T(8,128)(2,1)} %get-tuple-element.32.refs_5_), channel_id=1, source_target_pairs={{0,16},{8,24},{16,0},{24,8},{1,17},{9,25},{17,1},{25,9},{2,18},{10... | collective-permute-start | bytes 1572872 | tf_op jit(solution)/shard_map/ppermute | solution.py:531
  22.1 14.5 %collective-permute-start.3 = (bf16[128,2048]{1,0:T(8,128)(2,1)}, bf16[128,2048]{1,0:T(8,128)(2,1)S(1)}, u32[]{:S(2)}, u32[]{:S(2)}) collective-permute-start(bf16[128,2048]{1,0:T(8,128)(2,1)} %get-tuple-element.32.refs_5_), channel_id=1, source_target_pairs={{0,8},{8,0},{16,24},{24,16},{1,9},{9,1},{17,25},{25,17},{2,10},{10... | collective-permute-start | bytes 1572872 | tf_op jit(solution)/shard_map/ppermute | solution.py:531
  25.4 13.5 %collective-permute-start.11 = (bf16[256,1024]{1,0:T(8,128)(2,1)}, bf16[256,1024]{1,0:T(8,128)(2,1)}, u32[]{:S(2)}, u32[]{:S(2)}) collective-permute-start(bf16[256,1024]{1,0:T(8,128)(2,1)} %collective-permute-done.10.refs_18_), channel_id=1, source_target_pairs={{2,4},{4,6},{5,3},{3,1},{10,12},{12,14},{13,11},{11,9},{18,20},{20... | collective-permute-start | bytes 1572872 | tf_op jit(solution)/shard_map/ppermute | solution.py:465
  26.8 18.3 %collective-permute-start.9 = (bf16[256,1152]{1,0:T(8,128)(2,1)S(1)}, bf16[256,1152]{1,0:T(8,128)(2,1)S(1)}, u32[]{:S(2)}, u32[]{:S(2)}) collective-permute-start(bf16[256,1152]{1,0:T(8,128)(2,1)S(1)} %collective-permute-done.8.refs_12_), channel_id=1, source_target_pairs={{4,6},{3,1},{12,14},{11,9},{20,22},{19,17},{28,30},{27,25}} | collective-permute-start | bytes 1769480 | tf_op jit(solution)/shard_map/ppermute | solution.py:465
  34.8 7.9 %collective-permute-start.5 = (bf16[128,1024]{1,0:T(8,128)(2,1)S(1)}, bf16[128,1024]{1,0:T(8,128)(2,1)}, u32[]{:S(2)}, u32[]{:S(2)}) collective-permute-start(bf16[128,1024]{1,0:T(8,128)(2,1)S(1)} %slice.139), channel_id=1, source_target_pairs={{0,8},{8,0},{16,24},{24,16},{1,9},{9,1},{17,25},{25,17},{2,10},{10... | collective-permute-start | bytes 786440 | tf_op jit(solution)/shard_map/ppermute | solution.py:531
  37.3 7.8 %collective-permute-start.6 = (bf16[128,1024]{1,0:T(8,128)(2,1)}, bf16[128,1024]{1,0:T(8,128)(2,1)}, u32[]{:S(2)}, u32[]{:S(2)}) collective-permute-start(bf16[128,1024]{1,0:T(8,128)(2,1)} %slice.140), channel_id=1, source_target_pairs={{0,16},{8,24},{16,0},{24,8},{1,17},{9,25},{17,1},{25,9},{2,18},{10... | collective-permute-start | bytes 786440 | tf_op jit(solution)/shard_map/ppermute | solution.py:531
  38.8 8.1 %collective-permute-start.15 = (bf16[256,1024]{1,0:T(8,128)(2,1)}, bf16[256,1024]{1,0:T(8,128)(2,1)}, u32[]{:S(2)}, u32[]{:S(2)}) collective-permute-start(bf16[256,1024]{1,0:T(8,128)(2,1)} %collective-permute-done.11.refs_19_), channel_id=1, source_target_pairs={{4,6},{3,1},{12,14},{11,9},{20,22},{19,17},{28,30},{27,25}} | collective-permute-start | bytes 1572872 | tf_op jit(solution)/shard_map/ppermute | solution.py:465
  40.3 8.7 %collective-permute-start.16 = (bf16[256,1024]{1,0:T(8,128)(2,1)}, bf16[256,1024]{1,0:T(8,128)(2,1)}, u32[]{:S(2)}, u32[]{:S(2)}) collective-permute-start(bf16[256,1024]{1,0:T(8,128)(2,1)} %collective-permute-done.10.refs_18_), channel_id=1, source_target_pairs={{0,1},{1,0},{2,3},{3,2},{4,5},{5,4},{6,7},{7,6},{8,9},{9,8},{10,11... | collective-permute-start | bytes 1572872 | tf_op jit(solution)/shard_map/ppermute | solution.py:456
  42.7 8.2 %collective-permute-start.12 = (bf16[256,1152]{1,0:T(8,128)(2,1)S(1)}, bf16[256,1152]{1,0:T(8,128)(2,1)S(1)}, u32[]{:S(2)}, u32[]{:S(2)}) collective-permute-start(bf16[256,1152]{1,0:T(8,128)(2,1)S(1)} %collective-permute-done.7.refs_11_), channel_id=1, source_target_pairs={{0,1},{1,0},{2,3},{3,2},{4,5},{5,4},{6,7},{7,6},{8,9},{9,8},{10,11... | collective-permute-start | bytes 1769480 | tf_op jit(solution)/shard_map/ppermute | solution.py:456
  45.1 5.8 %collective-permute-start.13 = (bf16[256,1152]{1,0:T(8,128)(2,1)S(1)}, bf16[256,1152]{1,0:T(8,128)(2,1)}, u32[]{:S(2)}, u32[]{:S(2)}) collective-permute-start(bf16[256,1152]{1,0:T(8,128)(2,1)S(1)} %collective-permute-done.8.refs_12_), channel_id=1, source_target_pairs={{0,1},{1,0},{2,3},{3,2},{4,5},{5,4},{6,7},{7,6},{8,9},{9,8},{10,11... | collective-permute-start | bytes 1769480 | tf_op jit(solution)/shard_map/ppermute | solution.py:456
  45.1 6.5 %collective-permute-start.14 = (bf16[256,1152]{1,0:T(8,128)(2,1)S(1)}, bf16[256,1152]{1,0:T(8,128)(2,1)}, u32[]{:S(2)}, u32[]{:S(2)}) collective-permute-start(bf16[256,1152]{1,0:T(8,128)(2,1)S(1)} %collective-permute-done.9.refs_13_), channel_id=1, source_target_pairs={{0,1},{1,0},{2,3},{3,2},{4,5},{5,4},{6,7},{7,6},{8,9},{9,8},{10,11... | collective-permute-start | bytes 1769480 | tf_op jit(solution)/shard_map/ppermute | solution.py:456
  89.1 5.9 %collective-permute-start.26 = (bf16[256,1024]{1,0:T(8,128)(2,1)}, bf16[256,1024]{1,0:T(8,128)(2,1)S(1)}, u32[]{:S(2)}, u32[]{:S(2)}) collective-permute-start(bf16[256,1024]{1,0:T(8,128)(2,1)} %get-tuple-element.45), channel_id=1, source_target_pairs={{0,1},{1,0},{2,3},{3,2},{4,5},{5,4},{6,7},{7,6},{8,9},{9,8},{10,11... | collective-permute-start | bytes 1572872 | tf_op jit(solution)/shard_map/ppermute | solution.py:456
  90.2 7.9 %collective-permute-start.27 = (bf16[256,1024]{1,0:T(8,128)(2,1)}, bf16[256,1024]{1,0:T(8,128)(2,1)S(1)}, u32[]{:S(2)}, u32[]{:S(2)}) collective-permute-start(bf16[256,1024]{1,0:T(8,128)(2,1)} %get-tuple-element.46), channel_id=1, source_target_pairs={{0,1},{1,0},{2,3},{3,2},{4,5},{5,4},{6,7},{7,6},{8,9},{9,8},{10,11... | collective-permute-start | bytes 1572872 | tf_op jit(solution)/shard_map/ppermute | solution.py:456
  91.0 18.6 %collective-permute-start.22 = (bf16[256,1024]{1,0:T(8,128)(2,1)S(1)}, bf16[256,1024]{1,0:T(8,128)(2,1)S(1)}, u32[]{:S(2)}, u32[]{:S(2)}) collective-permute-start(bf16[256,1024]{1,0:T(8,128)(2,1)S(1)} %add_convert_fusion.7), channel_id=1, source_target_pairs={{0,2},{7,5},{8,10},{15,13},{16,18},{23,21},{24,26},{31,29}} | collective-permute-start | bytes 1572872 | tf_op jit(solution)/shard_map/ppermute | solution.py:465
  93.1 27.4 %collective-permute-start.35 = (bf16[128,1024]{1,0:T(8,128)(2,1)S(1)}, bf16[128,1024]{1,0:T(8,128)(2,1)S(1)}, u32[]{:S(2)}, u32[]{:S(2)}) collective-permute-start(bf16[128,1024]{1,0:T(8,128)(2,1)S(1)} %copy-done.24), channel_id=1, source_target_pairs={{0,16},{8,24},{16,0},{24,8},{1,17},{9,25},{17,1},{25,9},{2,18},{10... | collective-permute-start | bytes 786440 | tf_op jit(solution)/shard_map/ppermute | solution.py:531
  95.1 6.3 %collective-permute-start.32 = (bf16[24,2048]{1,0:T(8,128)(2,1)S(1)}, bf16[24,2048]{1,0:T(8,128)(2,1)S(1)}, u32[]{:S(2)}, u32[]{:S(2)}) collective-permute-start(bf16[24,2048]{1,0:T(8,128)(2,1)S(1)} %get-tuple-element.61), channel_id=1, source_target_pairs={{0,24},{8,16},{16,8},{24,0},{1,25},{9,17},{17,9},{25,1},{2,26},{10... | collective-permute-start | bytes 294920 | tf_op jit(solution)/shard_map/ppermute | solution.py:515
  97.0 9.0 %collective-permute-start.31 = (bf16[24,2048]{1,0:T(8,128)(2,1)S(1)}, bf16[24,2048]{1,0:T(8,128)(2,1)S(1)}, u32[]{:S(2)}, u32[]{:S(2)}) collective-permute-start(bf16[24,2048]{1,0:T(8,128)(2,1)S(1)} %get-tuple-element.61), channel_id=1, source_target_pairs={{0,16},{8,24},{16,0},{24,8},{1,17},{9,25},{17,1},{25,9},{2,18},{10... | collective-permute-start | bytes 294920 | tf_op jit(solution)/shard_map/ppermute | solution.py:515
  98.1 7.9 %collective-permute-start.30 = (bf16[24,2048]{1,0:T(8,128)(2,1)S(1)}, bf16[24,2048]{1,0:T(8,128)(2,1)S(1)}, u32[]{:S(2)}, u32[]{:S(2)}) collective-permute-start(bf16[24,2048]{1,0:T(8,128)(2,1)S(1)} %get-tuple-element.61), channel_id=1, source_target_pairs={{0,8},{8,0},{16,24},{24,16},{1,9},{9,1},{17,25},{25,17},{2,10},{10... | collective-permute-start | bytes 294920 | tf_op jit(solution)/shard_map/ppermute | solution.py:515
  101.3 7.3 %collective-permute-start.37 = (bf16[128,1024]{1,0:T(8,128)(2,1)S(1)}, bf16[128,1024]{1,0:T(8,128)(2,1)S(1)}, u32[]{:S(2)}, u32[]{:S(2)}) collective-permute-start(bf16[128,1024]{1,0:T(8,128)(2,1)S(1)} %copy-done.25), channel_id=1, source_target_pairs={{0,8},{8,0},{16,24},{24,16},{1,9},{9,1},{17,25},{25,17},{2,10},{10... | collective-permute-start | bytes 786440 | tf_op jit(solution)/shard_map/ppermute | solution.py:531
  106.2 9.2 %collective-permute-start.33 = (bf16[304,1024]{1,0:T(8,128)(2,1)S(1)}, bf16[304,1024]{1,0:T(8,128)(2,1)S(1)}, u32[]{:S(2)}, u32[]{:S(2)}) collective-permute-start(bf16[304,1024]{1,0:T(8,128)(2,1)S(1)} %pad_maximum_fusion), channel_id=1, source_target_pairs={{0,2},{7,5},{8,10},{15,13},{16,18},{23,21},{24,26},{31,29}} | collective-permute-start | bytes 1867784 | tf_op jit(solution)/shard_map/ppermute | solution.py:465
  108.7 19.7 %collective-permute-start.38 = (bf16[128,2048]{1,0:T(8,128)(2,1)S(1)}, bf16[128,2048]{1,0:T(8,128)(2,1)S(1)}, u32[]{:S(2)}, u32[]{:S(2)}) collective-permute-start(bf16[128,2048]{1,0:T(8,128)(2,1)S(1)} %pad_maximum_fusion.4), channel_id=1, source_target_pairs={{0,16},{8,24},{16,0},{24,8},{1,17},{9,25},{17,1},{25,9},{2,18},{10... | collective-permute-start | bytes 1572872 | tf_op jit(solution)/shard_map/ppermute | solution.py:531
  109.9 12.3 %collective-permute-start.23 = (bf16[256,1024]{1,0:T(8,128)(2,1)S(1)}, bf16[256,1024]{1,0:T(8,128)(2,1)S(1)}, u32[]{:S(2)}, u32[]{:S(2)}) collective-permute-start(bf16[256,1024]{1,0:T(8,128)(2,1)S(1)} %add_convert_fusion.6), channel_id=1, source_target_pairs={{0,2},{2,4},{7,5},{5,3},{8,10},{10,12},{15,13},{13,11},{16,18},{18... | collective-permute-start | bytes 1572872 | tf_op jit(solution)/shard_map/ppermute | solution.py:465
  115.7 12.4 %collective-permute-start.34 = (bf16[304,1024]{1,0:T(8,128)(2,1)S(1)}, bf16[304,1024]{1,0:T(8,128)(2,1)S(1)}, u32[]{:S(2)}, u32[]{:S(2)}) collective-permute-start(bf16[304,1024]{1,0:T(8,128)(2,1)S(1)} %pad_maximum_fusion.1), channel_id=1, source_target_pairs={{0,2},{2,4},{7,5},{5,3},{8,10},{10,12},{15,13},{13,11},{16,18},{18... | collective-permute-start | bytes 1867784 | tf_op jit(solution)/shard_map/ppermute | solution.py:465
  120.6 9.2 %collective-permute-start.36 = (bf16[128,2048]{1,0:T(8,128)(2,1)S(1)}, bf16[128,2048]{1,0:T(8,128)(2,1)S(1)}, u32[]{:S(2)}, u32[]{:S(2)}) collective-permute-start(bf16[128,2048]{1,0:T(8,128)(2,1)S(1)} %pad_maximum_fusion.3), channel_id=1, source_target_pairs={{0,8},{8,0},{16,24},{24,16},{1,9},{9,1},{17,25},{25,17},{2,10},{10... | collective-permute-start | bytes 1572872 | tf_op jit(solution)/shard_map/ppermute | solution.py:531
  122.5 11.3 %collective-permute-start.24 = (bf16[256,1024]{1,0:T(8,128)(2,1)S(1)}, bf16[256,1024]{1,0:T(8,128)(2,1)S(1)}, u32[]{:S(2)}, u32[]{:S(2)}) collective-permute-start(bf16[256,1024]{1,0:T(8,128)(2,1)S(1)} %add_convert_fusion.5), channel_id=1, source_target_pairs={{0,2},{2,4},{4,6},{7,5},{5,3},{3,1},{8,10},{10,12},{12,14},{15,13}... | collective-permute-start | bytes 1572872 | tf_op jit(solution)/shard_map/ppermute | solution.py:465
  129.9 11.1 %collective-permute-start.39 = (bf16[304,1024]{1,0:T(8,128)(2,1)S(1)}, bf16[304,1024]{1,0:T(8,128)(2,1)S(1)}, u32[]{:S(2)}, u32[]{:S(2)}) collective-permute-start(bf16[304,1024]{1,0:T(8,128)(2,1)S(1)} %pad_maximum_fusion.2), channel_id=1, source_target_pairs={{0,2},{2,4},{4,6},{7,5},{5,3},{3,1},{8,10},{10,12},{12,14},{15,13}... | collective-permute-start | bytes 1867784 | tf_op jit(solution)/shard_map/ppermute | solution.py:465
  134.0 7.3 %collective-permute-start.25 = (bf16[128,1024]{1,0:T(8,128)(2,1)S(1)}, bf16[128,1024]{1,0:T(8,128)(2,1)S(1)}, u32[]{:S(2)}, u32[]{:S(2)}) collective-permute-start(bf16[128,1024]{1,0:T(8,128)(2,1)S(1)} %slice.148), channel_id=1, source_target_pairs={{0,1},{1,0},{2,3},{3,2},{4,5},{5,4},{6,7},{7,6},{8,9},{9,8},{10,11... | collective-permute-start | bytes 786440 | tf_op jit(solution)/shard_map/ppermute | solution.py:456
  144.5 5.2 %collective-permute-start.42 = (f32[24,1]{0,1:T(1,128)S(1)}, f32[24,1]{0,1:T(1,128)S(1)}, u32[]{:S(2)}, u32[]{:S(2)}) collective-permute-start(f32[24,1]{0,1:T(1,128)S(1)} %bitcast.27), channel_id=1, source_target_pairs={{0,16},{8,24},{16,0},{24,8},{1,17},{9,25},{17,1},{25,9},{2,18},{10... | collective-permute-start | bytes 296 | tf_op jit(solution)/shard_map/ppermute | solution.py:515
  146.1 4.4 %collective-permute-start.43 = (f32[24,1]{0,1:T(1,128)S(1)}, f32[24,1]{0,1:T(1,128)S(1)}, u32[]{:S(2)}, u32[]{:S(2)}) collective-permute-start(f32[24,1]{0,1:T(1,128)S(1)} %bitcast.28), channel_id=1, source_target_pairs={{0,24},{8,16},{16,8},{24,0},{1,25},{9,17},{17,9},{25,1},{2,26},{10... | collective-permute-start | bytes 296 | tf_op jit(solution)/shard_map/ppermute | solution.py:515
  (40 other events, 378.1 us)
